TPU v7x, 32 devices: a whole 2x2x4 slice. The times are simulated.
32 devices in a mesh: gx: 8 (over y, x, core), gy: 4 (over z).
Axes of the slice: x: 2, y: 2, z: 4, core: 2. Of those that a mesh axis runs over, the one named last changes fastest.
Arguments:
- residual_in: bfloat16 [1536, 8192], P('gy', 'gx'), may hold values from -6 to 6
- w_query: bfloat16 [2, 1536, 1536], P(None, 'gx', 'gy'), may hold values from -0.15625 to 0.15625
- w_key: bfloat16 [2, 1536, 256], P(None, 'gx', 'gy'), may hold values from -0.15625 to 0.15625
- w_value: bfloat16 [2, 1536, 256], P(None, 'gx', 'gy'), may hold values from -0.15625 to 0.15625
- b_query: bfloat16 [2, 1536], P(None, 'gy'), may hold values from -1.5 to 1.5
- b_key: bfloat16 [2, 256], P(None, 'gy'), may hold values from -1.5 to 1.5
- b_value: bfloat16 [2, 256], P(None, 'gy'), may hold values from -0.59765625 to 0.59765625
- w_output: bfloat16 [2, 1536, 1536], P(None, 'gx', 'gy'), may hold values from -0.3125 to 0.3125
- gain_attn: bfloat16 [2, 1536], P(None, 'gy'), may hold values from 0.5 to 1.5
- gain_ffn: bfloat16 [2, 1536], P(None, 'gy'), may hold values from 0.5 to 1.5
- w_gate: bfloat16 [2, 1536, 8960], P(None, 'gx', 'gy'), may hold values from -0.15625 to 0.15625
- w_up: bfloat16 [2, 1536, 8960], P(None, 'gx', 'gy'), may hold values from -0.15625 to 0.15625
- w_down: bfloat16 [2, 1536, 8960], P(None, 'gx', 'gy'), may hold values from -0.0625 to 0.0625
- cotangent: bfloat16 [1536, 8192], P('gy', 'gx'), may hold values from -6 to 6
Outputs:
- output: float32 [1536, 8192], P('gy', 'gx')
- grad_input: float32 [1536, 8192], P('gy', 'gx')
- grad_w_query: float32 [2, 1536, 1536], P(None, 'gx', 'gy')
- grad_w_key: float32 [2, 1536, 256], P(None, 'gx', 'gy')
- grad_w_value: float32 [2, 1536, 256], P(None, 'gx', 'gy')
- grad_b_query: float32 [2, 1536], P(None, 'gy')
- grad_b_key: float32 [2, 256], P(None, 'gy')
- grad_b_value: float32 [2, 256], P(None, 'gy')
- grad_w_output: float32 [2, 1536, 1536], P(None, 'gx', 'gy')
- grad_gain_attn: float32 [2, 1536], P(None, 'gy')
- grad_gain_ffn: float32 [2, 1536], P(None, 'gy')
- grad_w_gate: float32 [2, 1536, 8960], P(None, 'gx', 'gy')
- grad_w_up: float32 [2, 1536, 8960], P(None, 'gx', 'gy')
- grad_w_down: float32 [2, 1536, 8960], P(None, 'gx', 'gy')
All inputs are finite; a program needn't handle non-finite values.
Results may differ from a plain program's by a relative error of at most 0.018.
Values may be sent and summed in bfloat16 or wider, within the bound.
A program may use at most 384 MiB of HBM per device.

v0:
```python
import math

import jax
import jax.numpy as jnp
from jax import lax
from jax.sharding import PartitionSpec as P

D = 1536
HEADS = 12
KV_HEADS = 2
HEAD_DIM = 128
LEN = 1024
LAYERS = 2


epsilon = 1e-06
rope_base = 1000000.0
penalty = 0.25


def rope_tables(positions, head_size):
    freqs = rope_base ** (-jnp.arange(0, head_size, 2).astype(jnp.float32) / head_size)
    angles = positions.astype(jnp.float32)[:, None] * freqs[None, :]
    cosine = jnp.cos(angles)
    sine_table = jnp.sin(angles)
    return (
        jnp.concatenate([cosine, cosine], -1)[:, None, :],
        jnp.concatenate([sine_table, sine_table], -1)[:, None, :],
    )


def rotate(tensor, cosine, sine_table):
    half = tensor.shape[-1] // 2
    turned = jnp.concatenate([-tensor[..., half:], tensor[..., :half]], -1)
    return tensor * cosine + turned * sine_table


def rotate_back(tensor, cosine, sine_table):
    half = tensor.shape[-1] // 2
    moved = tensor * sine_table
    return tensor * cosine + jnp.concatenate([moved[..., half:], -moved[..., :half]], -1)


def widen(local_block):
    return lax.all_gather(local_block, "gy", axis=1, tiled=True)


def narrow(partial_sum):
    return lax.psum_scatter(partial_sum, "gy", scatter_dimension=1, tiled=True)


def row_total(column):
    return lax.psum(column, "gy")


def heads_back(blocked):
    return lax.all_to_all(blocked, "gy", split_axis=1, concat_axis=0, tiled=True)


def fetch_weights(stack, layer_index):
    w_query, w_key, w_value, w_gate, w_up, w_output, w_down = stack
    rows_full = (
        lax.all_gather(w_query[layer_index], "gx", axis=0, tiled=True),
        lax.all_gather(w_key[layer_index], "gx", axis=0, tiled=True),
        lax.all_gather(w_value[layer_index], "gx", axis=0, tiled=True),
        lax.all_gather(w_gate[layer_index], "gx", axis=0, tiled=True),
        lax.all_gather(w_up[layer_index], "gx", axis=0, tiled=True),
    )
    cols_full = (
        lax.all_gather(w_output[layer_index], "gx", axis=0, tiled=True),
        lax.all_gather(w_down[layer_index], "gx", axis=0, tiled=True),
    )
    return tuple(rows_full) + tuple(cols_full)


def norm_forward(resid, width):
    total = row_total(jnp.sum(resid * resid, axis=1))
    scale = lax.rsqrt(total / width + epsilon)
    return (resid * scale[:, None], scale)


def norm_backward(grad_normed, normed, scale, gain, width):
    grad_gain = jnp.sum(grad_normed * normed, axis=0)
    grad_scaled = grad_normed * gain
    project = row_total(jnp.sum(grad_scaled * normed, axis=1)) / width
    return (scale[:, None] * (grad_scaled - normed * project[:, None]), grad_gain)


def score_block(q_rot, k_rot, allowed, scale_factor):
    scores = (
        jnp.einsum("qkgd,skd->kgqs", q_rot, k_rot, preferred_element_type=jnp.float32)
        * scale_factor
    )
    return jnp.where(allowed, scores, -1e30)


def on_device(
    residual_in,
    w_query,
    w_key,
    w_value,
    b_query,
    b_key,
    b_value,
    w_output,
    gain_attn,
    gain_ffn,
    w_gate,
    w_up,
    w_down,
    cotangent,
):
    stack = (w_query, w_key, w_value, w_gate, w_up, w_output, w_down)
    rows_tok = residual_in.shape[1]
    q_count = rows_tok // lax.axis_size("gy")
    group = HEADS // KV_HEADS
    scale_factor = 1.0 / math.sqrt(HEAD_DIM)
    q_index = lax.axis_index("gy") * q_count + jnp.arange(q_count, dtype=jnp.int32)
    k_index = jnp.arange(rows_tok, dtype=jnp.int32)
    allowed = (q_index[:, None] // LEN == k_index[None, :] // LEN) & (
        k_index[None, :] <= q_index[:, None]
    )
    q_cos, q_sin = rope_tables(q_index % LEN, HEAD_DIM)
    k_cos, k_sin = rope_tables(k_index % LEN, HEAD_DIM)
    resid = residual_in.astype(jnp.float32).T
    kept = []
    for layer_index in range(LAYERS):
        weights_full = fetch_weights(stack, layer_index)
        wq_full, wk_full, wv_full, wg_full, wu_full, wo_full, wd_full = weights_full
        normed_one, scale_one = norm_forward(resid, D)
        acts_one = widen(
            (normed_one * gain_attn[layer_index].astype(jnp.float32)).astype(jnp.bfloat16)
        )
        queries = jnp.dot(acts_one, wq_full, preferred_element_type=jnp.float32) + b_query[
            layer_index
        ].astype(jnp.float32)
        keys = jnp.dot(acts_one, wk_full, preferred_element_type=jnp.float32) + b_key[
            layer_index
        ].astype(jnp.float32)
        values = (
            (
                jnp.dot(acts_one, wv_full, preferred_element_type=jnp.float32)
                + b_value[layer_index].astype(jnp.float32)
            )
            .astype(jnp.bfloat16)
            .astype(jnp.float32)
        )
        q_heads = lax.all_to_all(queries, "gy", split_axis=0, concat_axis=1, tiled=True)
        keys_all, values_all = (
            lax.all_gather(keys, "gy", axis=1, tiled=True),
            lax.all_gather(values, "gy", axis=1, tiled=True),
        )
        q_rot = (
            rotate(q_heads.reshape(q_count, HEADS, HEAD_DIM), q_cos, q_sin)
            .astype(jnp.bfloat16)
            .reshape(q_count, KV_HEADS, group, HEAD_DIM)
        )
        k_rot = rotate(keys_all.reshape(rows_tok, KV_HEADS, HEAD_DIM), k_cos, k_sin).astype(
            jnp.bfloat16
        )
        v_heads = values_all.astype(jnp.bfloat16).reshape(rows_tok, KV_HEADS, HEAD_DIM)
        scores = score_block(q_rot, k_rot, allowed, scale_factor)
        top = jnp.max(scores, axis=-1, keepdims=True)
        expo = jnp.exp(scores - top)
        total = jnp.sum(expo, axis=-1, keepdims=True)
        soft = (expo / total).astype(jnp.bfloat16)
        log_total = top + jnp.log(total)
        mixed = (
            jnp.einsum("kgqs,skd->qkgd", soft, v_heads, preferred_element_type=jnp.float32)
            .reshape(q_count, HEADS * HEAD_DIM)
            .astype(jnp.bfloat16)
        )
        mixed_local = heads_back(mixed)
        middle = resid + narrow(
            jnp.einsum("tq,dq->td", mixed_local, wo_full, preferred_element_type=jnp.float32)
        )
        normed_two, scale_two = norm_forward(middle, D)
        acts_two = widen(
            (normed_two * gain_ffn[layer_index].astype(jnp.float32)).astype(jnp.bfloat16)
        )
        gate_value = jnp.dot(acts_two, wg_full, preferred_element_type=jnp.float32)
        up_value = jnp.dot(acts_two, wu_full, preferred_element_type=jnp.float32)
        hidden = (gate_value * lax.logistic(gate_value) * up_value).astype(jnp.bfloat16)
        output = middle + narrow(
            jnp.einsum("tf,df->td", hidden, wd_full, preferred_element_type=jnp.float32)
        )
        kept_weights = None
        kept.append(
            (
                kept_weights,
                normed_one,
                scale_one,
                acts_one,
                q_rot,
                k_rot,
                v_heads,
                log_total,
                mixed_local,
                normed_two,
                scale_two,
                acts_two,
                gate_value,
                up_value,
                hidden,
            )
        )
        resid = output
    grad = cotangent.astype(jnp.float32).T + 2.0 * penalty * resid
    row_parts = [None] * LAYERS
    col_parts = [None] * LAYERS
    small_parts = [None] * LAYERS
    for layer_index in reversed(range(LAYERS)):
        (
            kept_weights,
            normed_one,
            scale_one,
            acts_one,
            q_rot,
            k_rot,
            v_heads,
            log_total,
            mixed_local,
            normed_two,
            scale_two,
            acts_two,
            gate_value,
            up_value,
            hidden,
        ) = kept[layer_index]
        weights_full = fetch_weights(stack, layer_index)
        wq_full, wk_full, wv_full, wg_full, wu_full, wo_full, wd_full = weights_full
        grad_out = widen(grad.astype(jnp.bfloat16))
        grad_down = jnp.einsum("td,tf->df", grad_out, hidden, preferred_element_type=jnp.float32)
        grad_hidden = jnp.einsum("td,df->tf", grad_out, wd_full, preferred_element_type=jnp.float32)
        sigma = lax.logistic(gate_value)
        grad_gate = (grad_hidden * up_value * sigma * (1.0 + gate_value * (1.0 - sigma))).astype(
            jnp.bfloat16
        )
        grad_up = (grad_hidden * gate_value * sigma).astype(jnp.bfloat16)
        grad_wgate = jnp.einsum(
            "td,tf->df", acts_two, grad_gate, preferred_element_type=jnp.float32
        )
        grad_wup = jnp.einsum("td,tf->df", acts_two, grad_up, preferred_element_type=jnp.float32)
        grad_acts_two = narrow(
            jnp.einsum("tf,df->td", grad_gate, wg_full, preferred_element_type=jnp.float32)
            + jnp.einsum("tf,df->td", grad_up, wu_full, preferred_element_type=jnp.float32)
        )
        grad_mid_norm, grad_gain_two = norm_backward(
            grad_acts_two, normed_two, scale_two, gain_ffn[layer_index].astype(jnp.float32), D
        )
        grad_mid = grad + grad_mid_norm
        grad_branch = widen(grad_mid.astype(jnp.bfloat16))
        grad_wout = jnp.einsum(
            "td,tq->dq", grad_branch, mixed_local, preferred_element_type=jnp.float32
        )
        grad_mixed = jnp.einsum(
            "td,dq->tq", grad_branch, wo_full, preferred_element_type=jnp.float32
        ).astype(jnp.bfloat16)
        grad_heads = lax.all_to_all(
            grad_mixed, "gy", split_axis=0, concat_axis=1, tiled=True
        ).reshape(q_count, KV_HEADS, group, HEAD_DIM)
        scores = score_block(q_rot, k_rot, allowed, scale_factor)
        soft_full = jnp.exp(scores - log_total)
        soft = soft_full.astype(jnp.bfloat16)
        grad_soft = jnp.einsum(
            "qkgd,skd->kgqs", grad_heads, v_heads, preferred_element_type=jnp.float32
        )
        inner = jnp.sum(soft_full * grad_soft, axis=-1, keepdims=True)
        grad_scores = (soft_full * (grad_soft - inner)).astype(jnp.bfloat16)
        grad_values = jnp.einsum(
            "kgqs,qkgd->skd", soft, grad_heads, preferred_element_type=jnp.float32
        ).reshape(rows_tok, KV_HEADS * HEAD_DIM)
        grad_qrot = (
            jnp.einsum("kgqs,skd->qkgd", grad_scores, k_rot, preferred_element_type=jnp.float32)
            * scale_factor
        )
        grad_krot = (
            jnp.einsum("kgqs,qkgd->skd", grad_scores, q_rot, preferred_element_type=jnp.float32)
            * scale_factor
        )
        grad_queries = (
            rotate_back(grad_qrot.reshape(q_count, HEADS, HEAD_DIM), q_cos, q_sin)
            .reshape(q_count, HEADS * HEAD_DIM)
            .astype(jnp.bfloat16)
        )
        grad_keys_full = rotate_back(grad_krot, k_cos, k_sin).reshape(rows_tok, KV_HEADS * HEAD_DIM)
        grad_q_local = heads_back(grad_queries)
        grad_k_local, grad_v_local = (
            lax.psum_scatter(grad_keys_full, "gy", scatter_dimension=1, tiled=True),
            lax.psum_scatter(grad_values, "gy", scatter_dimension=1, tiled=True),
        )
        grad_k_local = grad_k_local.astype(jnp.bfloat16)
        grad_v_local = grad_v_local.astype(jnp.bfloat16)
        grad_wq = jnp.einsum(
            "td,tq->dq", acts_one, grad_q_local, preferred_element_type=jnp.float32
        )
        grad_wk = jnp.einsum(
            "td,tq->dq", acts_one, grad_k_local, preferred_element_type=jnp.float32
        )
        grad_wv = jnp.einsum(
            "td,tq->dq", acts_one, grad_v_local, preferred_element_type=jnp.float32
        )
        grad_bq = jnp.sum(grad_q_local.astype(jnp.float32), axis=0)
        grad_bk = jnp.sum(grad_k_local.astype(jnp.float32), axis=0)
        grad_bv = jnp.sum(grad_v_local.astype(jnp.float32), axis=0)
        grad_acts_one = narrow(
            jnp.einsum("tq,dq->td", grad_q_local, wq_full, preferred_element_type=jnp.float32)
            + jnp.einsum("tq,dq->td", grad_k_local, wk_full, preferred_element_type=jnp.float32)
            + jnp.einsum("tq,dq->td", grad_v_local, wv_full, preferred_element_type=jnp.float32)
        )
        grad_in_norm, grad_gain_one = norm_backward(
            grad_acts_one, normed_one, scale_one, gain_attn[layer_index].astype(jnp.float32), D
        )
        grad = grad_mid + grad_in_norm
        row_parts[layer_index] = (
            lax.psum_scatter(grad_wq, "gx", scatter_dimension=0, tiled=True),
            lax.psum_scatter(grad_wk, "gx", scatter_dimension=0, tiled=True),
            lax.psum_scatter(grad_wv, "gx", scatter_dimension=0, tiled=True),
            lax.psum_scatter(grad_wgate, "gx", scatter_dimension=0, tiled=True),
            lax.psum_scatter(grad_wup, "gx", scatter_dimension=0, tiled=True),
        )
        col_parts[layer_index] = (
            lax.psum_scatter(grad_wout, "gx", scatter_dimension=0, tiled=True),
            lax.psum_scatter(grad_down, "gx", scatter_dimension=0, tiled=True),
        )
        small_parts[layer_index] = (grad_gain_one, grad_gain_two, grad_bq, grad_bk, grad_bv)
    gains_one, gains_two, biases_q, biases_k, biases_v = lax.psum(
        (
            jnp.stack([part[0] for part in small_parts]),
            jnp.stack([part[1] for part in small_parts]),
            jnp.stack([part[2] for part in small_parts]),
            jnp.stack([part[3] for part in small_parts]),
            jnp.stack([part[4] for part in small_parts]),
        ),
        "gx",
    )
    grad_w_query = jnp.stack([part[0] for part in row_parts])
    grad_w_key = jnp.stack([part[1] for part in row_parts])
    grad_w_value = jnp.stack([part[2] for part in row_parts])
    grad_w_gate = jnp.stack([part[3] for part in row_parts])
    grad_w_up = jnp.stack([part[4] for part in row_parts])
    grad_w_output = jnp.stack([part[0] for part in col_parts])
    grad_w_down = jnp.stack([part[1] for part in col_parts])
    return (
        resid.T,
        grad.T,
        grad_w_query,
        grad_w_key,
        grad_w_value,
        biases_q,
        biases_k,
        biases_v,
        grad_w_output,
        gains_one,
        gains_two,
        grad_w_gate,
        grad_w_up,
        grad_w_down,
    )


def solution(mesh):
    placed = (
        P("gy", "gx"),
        P(None, "gx", "gy"),
        P(None, "gx", "gy"),
        P(None, "gx", "gy"),
        P(None, "gy"),
        P(None, "gy"),
        P(None, "gy"),
        P(None, "gx", "gy"),
        P(None, "gy"),
        P(None, "gy"),
        P(None, "gx", "gy"),
        P(None, "gx", "gy"),
        P(None, "gx", "gy"),
        P("gy", "gx"),
    )
    return jax.shard_map(
        on_device,
        mesh=mesh,
        in_specs=placed,
        out_specs=(
            P("gy", "gx"),
            P("gy", "gx"),
            P(None, "gx", "gy"),
            P(None, "gx", "gy"),
            P(None, "gx", "gy"),
            P(None, "gy"),
            P(None, "gy"),
            P(None, "gy"),
            P(None, "gx", "gy"),
            P(None, "gy"),
            P(None, "gy"),
            P(None, "gx", "gy"),
            P(None, "gx", "gy"),
            P(None, "gx", "gy"),
        ),
        check_vma=False,
    )
```

profile of v0, /device:TPU:9, one launch (start us, length us, event | category | flops | bytes accessed | tf_op | source)
XLA Modules:
  0.0 3418.4 jit_solution(15071804819088963168)
XLA Ops:
  33.6 49.7 %all-gather.35.cloned.1.call-done = bf16[1024,1536]{1,0:T(8,128)(2,1)} async-done(((bf16[1024,384]{1,0:T(8,128)(2,1)}), bf16[1024,1536]{1,0:T(8,128)(2,1)}) %all-gather.35.cloned.1.call-update) | async-done | bytes 3145744 | tf_op jit(solution)/shard_map/all_gather | solution.py:45
  130.1 53.5 %all_gather.94 = bf16[1024,256]{0,1:T(8,128)(2,1)S(1)} all-gather(bf16[1024,64]{0,1:T(8,128)(2,1)S(1)} %fusion.85), channel_id=1, replica_groups=mesh['gx'=8,'gy'=4] {'gy'}, dimensions={1}, use_global_device_ids=true | all-gather | bytes 655360 | tf_op jit(solution)/shard_map/all_gather | solution.py:151
  230.3 111.7 %reduce-scatter.35.cloned.1.call-done = f32[1024,384]{1,0:T(8,128)} async-done(((f32[1024,1536]{1,0:T(8,128)}), f32[1024,384]{1,0:T(8,128)}) %reduce-scatter.35.cloned.1.call-update) | async-done | bytes 1572880 | tf_op jit(solution)/shard_map/reduce_scatter | solution.py:49
  394.1 62.6 %all-gather.39.cloned.1.call-done = bf16[1024,1536]{1,0:T(8,128)(2,1)} async-done(((bf16[1024,384]{1,0:T(8,128)(2,1)}), bf16[1024,1536]{1,0:T(8,128)(2,1)}) %all-gather.39.cloned.1.call-update) | async-done | bytes 3145744 | tf_op jit(solution)/shard_map/all_gather | solution.py:45
  470.0 39.0 %all-gather.61.cloned.1.call-done = bf16[1,1536,2240]{2,1,0:T(8,128)(2,1)} async-done(((bf16[1,192,2240]{2,1,0:T(8,128)(2,1)}), bf16[1,1536,2240]{2,1,0:T(8,128)(2,1)}) %all-gather.61.cloned.1.call-update) | async-done | bytes 6881296 | tf_op jit(solution)/shard_map/all_gather | solution.py:67
  573.5 110.5 %reduce-scatter.37.cloned.1.call-done = f32[1024,384]{1,0:T(8,128)} async-done(((f32[1024,1536]{1,0:T(8,128)}), f32[1024,384]{1,0:T(8,128)}) %reduce-scatter.37.cloned.1.call-update) | async-done | bytes 1572880 | tf_op jit(solution)/shard_map/reduce_scatter | solution.py:49
  710.8 47.6 %all-gather.41.cloned.1.call-done = bf16[1024,1536]{1,0:T(8,128)(2,1)} async-done(((bf16[1024,384]{1,0:T(8,128)(2,1)}), bf16[1024,1536]{1,0:T(8,128)(2,1)}) %all-gather.41.cloned.1.call-update) | async-done | bytes 3145744 | tf_op jit(solution)/shard_map/all_gather | solution.py:45
  815.9 39.9 %all_gather.105 = bf16[1024,256]{0,1:T(8,128)(2,1)S(1)} all-gather(bf16[1024,64]{0,1:T(8,128)(2,1)S(1)} %fusion.87), channel_id=1, replica_groups=mesh['gx'=8,'gy'=4] {'gy'}, dimensions={1}, use_global_device_ids=true | all-gather | bytes 655360 | tf_op jit(solution)/shard_map/all_gather | solution.py:151
  901.0 114.6 %reduce-scatter.39.cloned.1.call-done = f32[1024,384]{1,0:T(8,128)} async-done(((f32[1024,1536]{1,0:T(8,128)}), f32[1024,384]{1,0:T(8,128)}) %reduce-scatter.39.cloned.1.call-update) | async-done | bytes 1572880 | tf_op jit(solution)/shard_map/reduce_scatter | solution.py:49
  1027.6 40.1 %all-gather.69.cloned.1.call-done = bf16[1,1536,2240]{2,1,0:T(8,128)(2,1)} async-done(((bf16[1,192,2240]{2,1,0:T(8,128)(2,1)}), bf16[1,1536,2240]{2,1,0:T(8,128)(2,1)}) %all-gather.69.cloned.1.call-update) | async-done | bytes 6881296 | tf_op jit(solution)/shard_map/all_gather | solution.py:66
  1067.7 63.1 %all-gather.45.cloned.1.call-done = bf16[1024,1536]{1,0:T(8,128)(2,1)} async-done(((bf16[1024,384]{1,0:T(8,128)(2,1)}), bf16[1024,1536]{1,0:T(8,128)(2,1)}) %all-gather.45.cloned.1.call-update) | async-done | bytes 3145744 | tf_op jit(solution)/shard_map/all_gather | solution.py:45
  1144.0 38.3 %all-gather.71.cloned.1.call-done = bf16[1,1536,2240]{2,1,0:T(8,128)(2,1)} async-done(((bf16[1,192,2240]{2,1,0:T(8,128)(2,1)}), bf16[1,1536,2240]{2,1,0:T(8,128)(2,1)}) %all-gather.71.cloned.1.call-update) | async-done | bytes 6881296 | tf_op jit(solution)/shard_map/all_gather | solution.py:67
  1247.5 109.1 %reduce-scatter.41.cloned.1.call-done = f32[1024,384]{1,0:T(8,128)} async-done(((f32[1024,1536]{1,0:T(8,128)}), f32[1024,384]{1,0:T(8,128)}) %reduce-scatter.41.cloned.1.call-update) | async-done | bytes 1572880 | tf_op jit(solution)/shard_map/reduce_scatter | solution.py:49
  1359.1 62.0 %all-gather.47.cloned.1.call-done = bf16[1024,1536]{1,0:T(8,128)(2,1)} async-done(((bf16[1024,384]{1,0:T(8,128)(2,1)}), bf16[1024,1536]{1,0:T(8,128)(2,1)}) %all-gather.47.cloned.1.call-update) | async-done | bytes 3145744 | tf_op jit(solution)/shard_map/all_gather | solution.py:45
  1465.2 111.4 %reduce-scatter.43.cloned.1.call-done = f32[1024,384]{1,0:T(8,128)} async-done(((f32[1024,1536]{1,0:T(8,128)}), f32[1024,384]{1,0:T(8,128)}) %reduce-scatter.43.cloned.1.call-update) | async-done | bytes 1572880 | tf_op jit(solution)/shard_map/reduce_scatter | solution.py:49
  1590.9 63.5 %all-gather.49.cloned.1.call-done = bf16[1024,1536]{1,0:T(8,128)(2,1)} async-done(((bf16[1024,384]{1,0:T(8,128)(2,1)}), bf16[1024,1536]{1,0:T(8,128)(2,1)}) %all-gather.49.cloned.1.call-update) | async-done | bytes 3145744 | tf_op jit(solution)/shard_map/all_gather | solution.py:45
  1776.4 111.0 %reduce-scatter.49.cloned.1.call-done = f32[1024,384]{1,0:T(8,128)} async-done(((f32[1024,1536]{1,0:T(8,128)}), f32[1024,384]{1,0:T(8,128)}) %reduce-scatter.49.cloned.1.call-update) | async-done | bytes 1572880 | tf_op jit(solution)/shard_map/reduce_scatter | solution.py:49
  1900.9 63.2 %all-gather.51.cloned.1.call-done = bf16[1024,1536]{1,0:T(8,128)(2,1)} async-done(((bf16[1024,384]{1,0:T(8,128)(2,1)}), bf16[1024,1536]{1,0:T(8,128)(2,1)}) %all-gather.51.cloned.1.call-update) | async-done | bytes 3145744 | tf_op jit(solution)/shard_map/all_gather | solution.py:45
  2008.0 111.4 %reduce-scatter.51.cloned.1.call-done = f32[1024,384]{1,0:T(8,128)} async-done(((f32[1024,1536]{1,0:T(8,128)}), f32[1024,384]{1,0:T(8,128)}) %reduce-scatter.51.cloned.1.call-update) | async-done | bytes 1572880 | tf_op jit(solution)/shard_map/reduce_scatter | solution.py:49
  2132.6 63.5 %all-gather.53.cloned.1.call-done = bf16[1024,1536]{1,0:T(8,128)(2,1)} async-done(((bf16[1024,384]{1,0:T(8,128)(2,1)}), bf16[1024,1536]{1,0:T(8,128)(2,1)}) %all-gather.53.cloned.1.call-update) | async-done | bytes 3145744 | tf_op jit(solution)/shard_map/all_gather | solution.py:45
  2424.4 55.2 %reduce-scatter.77.cloned.1.call-done = f32[192,2240]{1,0:T(8,128)} async-done(((f32[1536,2240]{1,0:T(8,128)}), f32[192,2240]{1,0:T(8,128)}) %reduce-scatter.77.cloned.1.call-update) | async-done | bytes 1720336 | tf_op jit(solution)/shard_map/reduce_scatter | solution.py:324
  2479.6 104.4 %reduce-scatter.75.cloned.1.call-done = f32[192,2240]{1,0:T(8,128)} async-done(((f32[1536,2240]{1,0:T(8,128)}), f32[192,2240]{1,0:T(8,128)}) %reduce-scatter.75.cloned.1.call-update) | async-done | bytes 1720336 | tf_op jit(solution)/shard_map/reduce_scatter | solution.py:324
  2588.0 100.2 %reduce-scatter.73.cloned.1.call-done = f32[192,2240]{1,0:T(8,128)} async-done(((f32[1536,2240]{1,0:T(8,128)}), f32[192,2240]{1,0:T(8,128)}) %reduce-scatter.73.cloned.1.call-update) | async-done | bytes 1720336 | tf_op jit(solution)/shard_map/reduce_scatter | solution.py:320
  2688.2 104.2 %reduce-scatter.71.cloned.1.call-done = f32[192,2240]{1,0:T(8,128)} async-done(((f32[1536,2240]{1,0:T(8,128)}), f32[192,2240]{1,0:T(8,128)}) %reduce-scatter.71.cloned.1.call-update) | async-done | bytes 1720336 | tf_op jit(solution)/shard_map/reduce_scatter | solution.py:320
  2796.4 100.3 %reduce-scatter.69.cloned.1.call-done = f32[192,2240]{1,0:T(8,128)} async-done(((f32[1536,2240]{1,0:T(8,128)}), f32[192,2240]{1,0:T(8,128)}) %reduce-scatter.69.cloned.1.call-update) | async-done | bytes 1720336 | tf_op jit(solution)/shard_map/reduce_scatter | solution.py:319
  2896.7 104.2 %reduce-scatter.67.cloned.1.call-done = f32[192,2240]{1,0:T(8,128)} async-done(((f32[1536,2240]{1,0:T(8,128)}), f32[192,2240]{1,0:T(8,128)}) %reduce-scatter.67.cloned.1.call-update) | async-done | bytes 1720336 | tf_op jit(solution)/shard_map/reduce_scatter | solution.py:319
  3005.0 41.8 %reduce-scatter.65.cloned.1.call-done = f32[192,384]{1,0:T(8,128)} async-done(((f32[1536,384]{1,0:T(8,128)}), f32[192,384]{1,0:T(8,128)}) %reduce-scatter.65.cloned.1.call-update) | async-done | bytes 294928 | tf_op jit(solution)/shard_map/reduce_scatter | solution.py:323
  3046.8 46.2 %reduce-scatter.63.cloned.1.call-done = f32[192,384]{1,0:T(8,128)} async-done(((f32[1536,384]{1,0:T(8,128)}), f32[192,384]{1,0:T(8,128)}) %reduce-scatter.63.cloned.1.call-update) | async-done | bytes 294928 | tf_op jit(solution)/shard_map/reduce_scatter | solution.py:323
  3131.8 37.0 %reduce-scatter.79.cloned.1.call-done = f32[192,64]{1,0:T(8,128)} async-done(((f32[1536,64]{1,0:T(8,128)}), f32[192,64]{1,0:T(8,128)}) %reduce-scatter.79.cloned.1.call-update) | async-done | bytes 49168
  3171.2 43.9 %reduce-scatter.61.cloned.1.call-done = f32[192,384]{1,0:T(8,128)} async-done(((f32[1536,384]{1,0:T(8,128)}), f32[192,384]{1,0:T(8,128)}) %reduce-scatter.61.cloned.1.call-update) | async-done | bytes 294928 | tf_op jit(solution)/shard_map/reduce_scatter | solution.py:316
  3215.1 46.1 %reduce-scatter.59.cloned.1.call-done = f32[192,384]{1,0:T(8,128)} async-done(((f32[1536,384]{1,0:T(8,128)}), f32[192,384]{1,0:T(8,128)}) %reduce-scatter.59.cloned.1.call-update) | async-done | bytes 294928 | tf_op jit(solution)/shard_map/reduce_scatter | solution.py:316
  3263.0 111.1 %reduce-scatter.57.cloned.1.call-done = f32[1024,384]{1,0:T(8,128)} async-done(((f32[1024,1536]{1,0:T(8,128)}), f32[1024,384]{1,0:T(8,128)}) %reduce-scatter.57.cloned.1.call-update) | async-done | bytes 1572880 | tf_op jit(solution)/shard_map/reduce_scatter | solution.py:49
  (521 shorter events, 1041.9 us)
Async XLA Ops:
  19.7 163.9 %all-gather.37.cloned.1.call-start = ((), (), s32[]{:S(2)}) async-start(), calls=%async_computation.35 | async-start | bytes 1310720 | tf_op jit(solution)/shard_map/all_gather | solution.py:150
  227.3 166.8 %all-gather.59.cloned.1.call-start = ((), (), s32[]{:S(2)}) async-start(), calls=%async_computation.68 | async-start | bytes 7962624 | tf_op jit(solution)/shard_map/all_gather | solution.py:66
  230.2 226.5 %all-gather.39.cloned.1.call-start = ((), (), s32[]{:S(2)}) async-start(), calls=%async_computation.37 | async-start | bytes 3932160 | tf_op jit(solution)/shard_map/all_gather | solution.py:45
  355.3 205.0 %all-gather.63.cloned.1.call-start = ((), (), s32[]{:S(2)}) async-start(), calls=%async_computation.70 | async-start | bytes 7962624 | tf_op jit(solution)/shard_map/all_gather | solution.py:71
  358.1 325.9 %reduce-scatter.37.cloned.1.call-start = ((), (), s32[]{:S(2)}) async-start(), calls=%async_computation.38 | async-start | bytes 7864320 | tf_op jit(solution)/shard_map/reduce_scatter | solution.py:49
  573.5 184.9 %all-gather.41.cloned.1.call-start = ((), (), s32[]{:S(2)}) async-start(), calls=%async_computation.39 | async-start | bytes 3932160 | tf_op jit(solution)/shard_map/all_gather | solution.py:45
  900.4 167.3 %all-gather.69.cloned.1.call-start = ((), (), s32[]{:S(2)}) async-start(), calls=%async_computation.73 | async-start | bytes 7962624 | tf_op jit(solution)/shard_map/all_gather | solution.py:66
  900.9 229.8 %all-gather.45.cloned.1.call-start = ((), (), s32[]{:S(2)}) async-start(), calls=%async_computation.42 | async-start | bytes 3932160 | tf_op jit(solution)/shard_map/all_gather | solution.py:45
  1026.4 206.6 %all-gather.73.cloned.1.call-start = ((), (), s32[]{:S(2)}) async-start(), calls=%async_computation.75 | async-start | bytes 7962624 | tf_op jit(solution)/shard_map/all_gather | solution.py:71
  1027.1 329.4 %reduce-scatter.41.cloned.1.call-start = ((), (), s32[]{:S(2)}) async-start(), calls=%async_computation.43 | async-start | bytes 7864320 | tf_op jit(solution)/shard_map/reduce_scatter | solution.py:49
  1246.0 175.2 %all-gather.47.cloned.1.call-start = ((), (), s32[]{:S(2)}) async-start(), calls=%async_computation.44 | async-start | bytes 3932160 | tf_op jit(solution)/shard_map/all_gather | solution.py:45
  1359.1 217.5 %reduce-scatter.43.cloned.1.call-start = ((), (), s32[]{:S(2)}) async-start(), calls=%async_computation.45 | async-start | bytes 7864320 | tf_op jit(solution)/shard_map/reduce_scatter | solution.py:49
  1465.2 189.2 %all-gather.49.cloned.1.call-start = ((), (), s32[]{:S(2)}) async-start(), calls=%async_computation.46 | async-start | bytes 3932160 | tf_op jit(solution)/shard_map/all_gather | solution.py:45
  1720.3 167.1 %reduce-scatter.49.cloned.1.call-start = ((), (), s32[]{:S(2)}) async-start(), calls=%async_computation.49 | async-start | bytes 7864320 | tf_op jit(solution)/shard_map/reduce_scatter | solution.py:49
  1776.3 187.8 %all-gather.51.cloned.1.call-start = ((), (), s32[]{:S(2)}) async-start(), calls=%async_computation.50 | async-start | bytes 3932160 | tf_op jit(solution)/shard_map/all_gather | solution.py:45
  1900.7 218.7 %reduce-scatter.51.cloned.1.call-start = ((), (), s32[]{:S(2)}) async-start(), calls=%async_computation.51 | async-start | bytes 7864320 | tf_op jit(solution)/shard_map/reduce_scatter | solution.py:49
  2007.9 188.2 %all-gather.53.cloned.1.call-start = ((), (), s32[]{:S(2)}) async-start(), calls=%async_computation.52 | async-start | bytes 3932160 | tf_op jit(solution)/shard_map/all_gather | solution.py:45
  2255.8 164.1 %reduce-scatter.85.cloned.1.call-start = ((), (), s32[]{:S(2)}) async-start(), calls=%async_computation.79 | async-start | bytes 884736
  2259.9 161.0 %reduce-scatter.81.cloned.1.call-start = ((), (), s32[]{:S(2)}) async-start(), calls=%async_computation.77 | async-start | bytes 884736
  2262.2 217.4 %reduce-scatter.77.cloned.1.call-start = ((), (), s32[]{:S(2)}) async-start(), calls=%async_computation.65 | async-start | bytes 15925248 | tf_op jit(solution)/shard_map/reduce_scatter | solution.py:324
  2275.8 308.2 %reduce-scatter.75.cloned.1.call-start = ((), (), s32[]{:S(2)}) async-start(), calls=%async_computation.64 | async-start | bytes 15925248 | tf_op jit(solution)/shard_map/reduce_scatter | solution.py:324
  2290.1 398.0 %reduce-scatter.73.cloned.1.call-start = ((), (), s32[]{:S(2)}) async-start(), calls=%async_computation.63 | async-start | bytes 15925248 | tf_op jit(solution)/shard_map/reduce_scatter | solution.py:320
  2304.7 487.7 %reduce-scatter.71.cloned.1.call-start = ((), (), s32[]{:S(2)}) async-start(), calls=%async_computation.62 | async-start | bytes 15925248 | tf_op jit(solution)/shard_map/reduce_scatter | solution.py:320
  2319.1 577.6 %reduce-scatter.69.cloned.1.call-start = ((), (), s32[]{:S(2)}) async-start(), calls=%async_computation.61 | async-start | bytes 15925248 | tf_op jit(solution)/shard_map/reduce_scatter | solution.py:319
  2332.5 668.4 %reduce-scatter.67.cloned.1.call-start = ((), (), s32[]{:S(2)}) async-start(), calls=%async_computation.60 | async-start | bytes 15925248 | tf_op jit(solution)/shard_map/reduce_scatter | solution.py:319
  2345.4 701.4 %reduce-scatter.65.cloned.1.call-start = ((), (), s32[]{:S(2)}) async-start(), calls=%async_computation.59 | async-start | bytes 2654208 | tf_op jit(solution)/shard_map/reduce_scatter | solution.py:323
  2351.7 741.3 %reduce-scatter.63.cloned.1.call-start = ((), (), s32[]{:S(2)}) async-start(), calls=%async_computation.58 | async-start | bytes 2654208 | tf_op jit(solution)/shard_map/reduce_scatter | solution.py:323
  2357.5 773.4 %reduce-scatter.83.cloned.1.call-start = ((), (), s32[]{:S(2)}) async-start(), calls=%async_computation.78 | async-start | bytes 884736
  2360.8 808.1 %reduce-scatter.79.cloned.1.call-start = ((), (), s32[]{:S(2)}) async-start(), calls=%async_computation.76 | async-start | bytes 884736
  2364.0 851.0 %reduce-scatter.61.cloned.1.call-start = ((), (), s32[]{:S(2)}) async-start(), calls=%async_computation.57 | async-start | bytes 2654208 | tf_op jit(solution)/shard_map/reduce_scatter | solution.py:316
  2369.5 891.7 %reduce-scatter.59.cloned.1.call-start = ((), (), s32[]{:S(2)}) async-start(), calls=%async_computation.56 | async-start | bytes 2654208 | tf_op jit(solution)/shard_map/reduce_scatter | solution.py:316
  2406.5 967.6 %reduce-scatter.57.cloned.1.call-start = ((), (), s32[]{:S(2)}) async-start(), calls=%async_computation.55 | async-start | bytes 7864320 | tf_op jit(solution)/shard_map/reduce_scatter | solution.py:49
  (124 other events, 6575.2 us)
Sparse Core Ops, SparseCore 0:
  19.0 64.3 all-gather.34
  227.4 114.5 reduce-scatter.34
  344.3 49.7 all-gather.58
  395.7 61.0 all-gather.38
  459.2 49.7 all-gather.60
  511.5 48.8 all-gather.62
  573.6 110.3 reduce-scatter.36
  695.0 63.3 all-gather.40
  900.5 115.0 reduce-scatter.38
  1017.9 49.7 all-gather.68
  1069.7 61.0 all-gather.44
  1132.5 49.7 all-gather.70
  1184.1 48.8 all-gather.72
  1246.1 110.3 reduce-scatter.40
  1359.2 61.9 all-gather.46
  1465.3 111.2 reduce-scatter.42
  1591.0 63.2 all-gather.48
  1776.4 110.9 reduce-scatter.48
  1900.8 63.2 all-gather.50
  2008.0 111.2 reduce-scatter.50
  2132.7 63.3 all-gather.52
  2378.5 101.0 reduce-scatter.76
  2483.2 100.7 reduce-scatter.74
  2587.4 100.7 reduce-scatter.72
  2691.6 100.7 reduce-scatter.70
  2796.0 100.7 reduce-scatter.68
  2900.2 100.7 reduce-scatter.66
  3004.3 42.4 reduce-scatter.64
  3050.5 42.4 reduce-scatter.62
  3172.2 42.7 reduce-scatter.60
  3218.6 42.4 reduce-scatter.58
  3263.3 110.7 reduce-scatter.56
  (14 shorter events, 448.8 us)
where the time goes:
time: 3430 us; the launch traced here: 3420 us
  waiting for transfers between devices  2510 us (73%)
  matrix products  411 us (12%)
  blocking collectives  280 us (8%)
  other arithmetic  105 us (3%)
  local copies, waits for them, and re-layouts  67.3 us (2%)
    reduce_scatter x8, waiting for transfers between devices, narrow(): return lax.psum_scatter(partial_sum, 'gy', scatter_dimension=1, tiled=True)  891 us
    all_gather x8, waiting for transfers between devices, widen(): return lax.all_gather(local_block, 'gy', axis=1, tiled=True)  475 us
    reduce_scatter x2, waiting for transfers between devices, on_device(): lax.psum_scatter(grad_wgate, 'gx', scatter_dimension=0, tiled=True)  205 us
    reduce_scatter x2, waiting for transfers between devices, on_device(): lax.psum_scatter(grad_wup, 'gx', scatter_dimension=0, tiled=True)  204 us
    reduce_scatter x2, waiting for transfers between devices, on_device(): lax.psum_scatter(grad_down, 'gx', scatter_dimension=0, tiled=True)  160 us
    all_gather x2, blocking collectives, on_device(): lax.all_gather(values, 'gy', axis=1, tiled=True)  93.4 us
    reduce_scatter x2, waiting for transfers between devices, on_device(): lax.psum_scatter(grad_wq, 'gx', scatter_dimension=0, tiled=True)  89.9 us
    reduce_scatter x2, waiting for transfers between devices, on_device(): lax.psum_scatter(grad_wout, 'gx', scatter_dimension=0, tiled=True)  88 us
  transfers between devices with their start and end apart: 52, of which 41 were waited for; matrix products, arithmetic and copies ran while one was open for 10% of the time, Pallas kernels for 0%

commit v1 on v0

v1 whole, which is shorter than its diff:
```python
import math

import jax
import jax.numpy as jnp
from jax import lax
from jax.sharding import PartitionSpec as P

D = 1536
HEADS = 12
KV_HEADS = 2
HEAD_DIM = 128
LEN = 1024
LAYERS = 2
GROUP = HEADS // KV_HEADS

epsilon = 1e-06
rope_base = 1000000.0
penalty = 0.25
bf16 = jnp.bfloat16
f32 = jnp.float32


def rope_tables(positions, head_size):
    freqs = rope_base ** (-jnp.arange(0, head_size, 2).astype(f32) / head_size)
    angles = positions.astype(f32)[:, None] * freqs[None, :]
    cosine = jnp.cos(angles)
    sine_table = jnp.sin(angles)
    return (
        jnp.concatenate([cosine, cosine], -1)[:, None, :],
        jnp.concatenate([sine_table, sine_table], -1)[:, None, :],
    )


def rotate(tensor, cosine, sine_table):
    half = tensor.shape[-1] // 2
    turned = jnp.concatenate([-tensor[..., half:], tensor[..., :half]], -1)
    return tensor * cosine + turned * sine_table


def rotate_back(tensor, cosine, sine_table):
    half = tensor.shape[-1] // 2
    moved = tensor * sine_table
    return tensor * cosine + jnp.concatenate([moved[..., half:], -moved[..., :half]], -1)


def dot(pattern, left, right):
    return jnp.einsum(pattern, left, right, preferred_element_type=f32)


def rms_parts(resid):
    scale = lax.rsqrt(jnp.mean(resid * resid, axis=1, keepdims=True) + epsilon)
    return resid * scale, scale


def norm_backward(grad_normed, normed, scale, gain):
    grad_gain = jnp.sum(grad_normed * normed, axis=0)
    scaled = grad_normed * gain
    project = jnp.mean(scaled * normed, axis=1, keepdims=True)
    return scale * (scaled - normed * project), grad_gain


def gather_attention(w_query, w_key, w_value, w_output):
    sizes = (w_query.shape[1], w_key.shape[1], w_value.shape[1], w_output.shape[1])
    pack = jnp.concatenate([w_query, w_key, w_value, w_output], axis=1)
    pack = lax.all_gather(pack, "gy", axis=0)
    pack = lax.all_gather(pack, "gx", axis=0)
    full, start = [], 0
    for size in sizes:
        part = pack[..., start : start + size].transpose(0, 2, 1, 3)
        full.append(part.reshape(D, -1))
        start += size
    return full


def scatter_attention(grads, devices_x, devices_y):
    parts = [
        grad.reshape(devices_x, D // devices_x, devices_y, -1).transpose(0, 2, 1, 3)
        for grad in grads
    ]
    sizes = [part.shape[-1] for part in parts]
    pack = jnp.concatenate(parts, axis=-1)
    pack = lax.psum_scatter(pack, "gx", scatter_dimension=0)
    pack = lax.psum_scatter(pack, "gy", scatter_dimension=0).astype(f32)
    out, start = [], 0
    for size in sizes:
        out.append(pack[:, start : start + size])
        start += size
    return out


def score_block(q_rot, k_rot, allowed):
    scores = dot("qkgd,skd->kgqs", q_rot, k_rot) * (1.0 / math.sqrt(HEAD_DIM))
    return jnp.where(allowed, scores, -1e30)


def on_device(
    residual_in,
    w_query,
    w_key,
    w_value,
    b_query,
    b_key,
    b_value,
    w_output,
    gain_attn,
    gain_ffn,
    w_gate,
    w_up,
    w_down,
    cotangent,
):
    devices_x = lax.axis_size("gx")
    devices_y = lax.axis_size("gy")
    rows_tok = residual_in.shape[1]
    count = rows_tok // devices_y
    q_index = lax.axis_index("gy") * count + jnp.arange(count, dtype=jnp.int32)
    k_index = jnp.arange(rows_tok, dtype=jnp.int32)
    allowed = (q_index[:, None] // LEN == k_index[None, :] // LEN) & (
        k_index[None, :] <= q_index[:, None]
    )
    cosine, sine = rope_tables(q_index % LEN, HEAD_DIM)

    small = jnp.concatenate([gain_attn, gain_ffn, b_query, b_key, b_value], axis=1)
    small_sizes = [v.shape[1] for v in (gain_attn, gain_ffn, b_query, b_key, b_value)]
    small = lax.all_gather(small, "gy", axis=1).astype(f32)
    vectors, start = [], 0
    for size in small_sizes:
        vectors.append(small[:, :, start : start + size].reshape(LAYERS, -1))
        start += size
    gains_one, gains_two, bias_q, bias_k, bias_v = vectors

    resid = lax.all_to_all(residual_in, "gy", split_axis=1, concat_axis=0, tiled=True)
    resid = resid.astype(f32).T
    attn_full, ffn_full = [], []
    for l in range(LAYERS):
        attn_full.append(gather_attention(w_query[l], w_key[l], w_value[l], w_output[l]))
        ffn_full.append(
            tuple(lax.all_gather(w[l], "gx", axis=0, tiled=True) for w in (w_gate, w_up, w_down))
        )
    cot = lax.all_to_all(cotangent, "gy", split_axis=1, concat_axis=0, tiled=True)

    kept = []
    for l in range(LAYERS):
        wq, wk, wv, wo = attn_full[l]
        wg, wu, wd = ffn_full[l]
        normed_one, scale_one = rms_parts(resid)
        acts_one = (normed_one * gains_one[l]).astype(bf16)
        queries = dot("td,dq->tq", acts_one, wq) + bias_q[l]
        keys = dot("td,dq->tq", acts_one, wk) + bias_k[l]
        values = (dot("td,dq->tq", acts_one, wv) + bias_v[l]).astype(bf16)
        q_rot = rotate(queries.reshape(count, HEADS, HEAD_DIM), cosine, sine).astype(bf16)
        q_rot = q_rot.reshape(count, KV_HEADS, GROUP, HEAD_DIM)
        k_rot = rotate(keys.reshape(count, KV_HEADS, HEAD_DIM), cosine, sine).astype(bf16)
        both = jnp.concatenate([k_rot.reshape(count, -1), values], axis=1)
        both = lax.all_gather(both, "gy", axis=0, tiled=True)
        half = both.shape[1] // 2
        k_rot = both[:, :half].reshape(rows_tok, KV_HEADS, HEAD_DIM)
        v_heads = both[:, half:].reshape(rows_tok, KV_HEADS, HEAD_DIM)
        scores = score_block(q_rot, k_rot, allowed)
        top = jnp.max(scores, axis=-1, keepdims=True)
        expo = jnp.exp(scores - top)
        total = jnp.sum(expo, axis=-1, keepdims=True)
        soft = (expo / total).astype(bf16)
        log_total = top + jnp.log(total)
        mixed = dot("kgqs,skd->qkgd", soft, v_heads).reshape(count, -1).astype(bf16)
        middle = resid + dot("tq,dq->td", mixed, wo)
        normed_two, scale_two = rms_parts(middle)
        acts_two = (normed_two * gains_two[l]).astype(bf16)
        acts_two = lax.all_gather(acts_two, "gy", axis=0, tiled=True)
        gate = dot("td,df->tf", acts_two, wg)
        up = dot("td,df->tf", acts_two, wu)
        hidden = (gate * lax.logistic(gate) * up).astype(bf16)
        part = dot("tf,df->td", hidden, wd).astype(bf16)
        part = lax.psum_scatter(part, "gy", scatter_dimension=0, tiled=True)
        kept.append(
            (
                normed_one,
                scale_one,
                acts_one,
                q_rot,
                k_rot,
                v_heads,
                log_total,
                mixed,
                normed_two,
                scale_two,
                acts_two,
                gate.astype(bf16),
                up.astype(bf16),
                hidden,
            )
        )
        resid = middle + part.astype(f32)

    def to_blocks(tokens_major):
        flipped = tokens_major.astype(bf16).T
        out = lax.all_to_all(flipped, "gy", split_axis=0, concat_axis=1, tiled=True)
        return out.astype(f32)

    output = to_blocks(resid)
    grad = cot.astype(f32).T + 2.0 * penalty * resid
    attn_grads = [None] * LAYERS
    ffn_grads = [None] * LAYERS
    small_grads = [None] * LAYERS

    def scatter_x(weight_grad):
        return lax.psum_scatter(
            weight_grad.astype(bf16), "gx", scatter_dimension=0, tiled=True
        ).astype(f32)

    for l in reversed(range(LAYERS)):
        (
            normed_one,
            scale_one,
            acts_one,
            q_rot,
            k_rot,
            v_heads,
            log_total,
            mixed,
            normed_two,
            scale_two,
            acts_two,
            gate,
            up,
            hidden,
        ) = kept[l]
        wq, wk, wv, wo = attn_full[l]
        wg, wu, wd = ffn_full[l]
        grad_out = lax.all_gather(grad.astype(bf16), "gy", axis=0, tiled=True)
        grad_hidden = dot("td,df->tf", grad_out, wd)
        gate = gate.astype(f32)
        up = up.astype(f32)
        sigma = lax.logistic(gate)
        grad_gate = (grad_hidden * up * sigma * (1.0 + gate * (1.0 - sigma))).astype(bf16)
        grad_up = (grad_hidden * gate * sigma).astype(bf16)
        part = dot("tf,df->td", grad_gate, wg) + dot("tf,df->td", grad_up, wu)
        grad_acts_two = lax.psum_scatter(
            part.astype(bf16), "gy", scatter_dimension=0, tiled=True
        ).astype(f32)
        ffn_grads[l] = (
            scatter_x(dot("td,tf->df", acts_two, grad_gate)),
            scatter_x(dot("td,tf->df", acts_two, grad_up)),
            scatter_x(dot("td,tf->df", grad_out, hidden)),
        )
        grad_norm, grad_gain_two = norm_backward(
            grad_acts_two, normed_two, scale_two, gains_two[l]
        )
        grad_mid = grad + grad_norm
        grad_branch = grad_mid.astype(bf16)
        grad_wo = dot("td,tq->dq", grad_branch, mixed)
        grad_mixed = dot("td,dq->tq", grad_branch, wo).astype(bf16)
        grad_heads = grad_mixed.reshape(count, KV_HEADS, GROUP, HEAD_DIM)
        scores = score_block(q_rot, k_rot, allowed)
        soft_full = jnp.exp(scores - log_total)
        soft = soft_full.astype(bf16)
        grad_soft = dot("qkgd,skd->kgqs", grad_heads, v_heads)
        inner = jnp.sum(soft_full * grad_soft, axis=-1, keepdims=True)
        grad_scores = (soft_full * (grad_soft - inner)).astype(bf16)
        grad_values = dot("kgqs,qkgd->skd", soft, grad_heads)
        factor = 1.0 / math.sqrt(HEAD_DIM)
        grad_qrot = dot("kgqs,skd->qkgd", grad_scores, k_rot) * factor
        grad_krot = dot("kgqs,qkgd->skd", grad_scores, q_rot) * factor
        grad_q = rotate_back(grad_qrot.reshape(count, HEADS, HEAD_DIM), cosine, sine)
        grad_q = grad_q.reshape(count, -1).astype(bf16)
        both = jnp.concatenate(
            [grad_krot.reshape(rows_tok, -1), grad_values.reshape(rows_tok, -1)], axis=1
        ).astype(bf16)
        both = lax.psum_scatter(both, "gy", scatter_dimension=0, tiled=True).astype(f32)
        half = both.shape[1] // 2
        grad_k = rotate_back(both[:, :half].reshape(count, KV_HEADS, HEAD_DIM), cosine, sine)
        grad_k = grad_k.reshape(count, -1).astype(bf16)
        grad_v = both[:, half:].astype(bf16)
        grad_acts_one = (
            dot("tq,dq->td", grad_q, wq)
            + dot("tq,dq->td", grad_k, wk)
            + dot("tq,dq->td", grad_v, wv)
        )
        attn_grads[l] = scatter_attention(
            [
                g.astype(bf16)
                for g in (
                    dot("td,tq->dq", acts_one, grad_q),
                    dot("td,tq->dq", acts_one, grad_k),
                    dot("td,tq->dq", acts_one, grad_v),
                    grad_wo,
                )
            ],
            devices_x,
            devices_y,
        )
        grad_norm, grad_gain_one = norm_backward(
            grad_acts_one, normed_one, scale_one, gains_one[l]
        )
        grad = grad_mid + grad_norm
        small_grads[l] = [
            v.reshape(devices_y, -1)
            for v in (
                grad_gain_one,
                grad_gain_two,
                jnp.sum(grad_q.astype(f32), axis=0),
                jnp.sum(grad_k.astype(f32), axis=0),
                jnp.sum(grad_v.astype(f32), axis=0),
            )
        ]
    small = jnp.stack([jnp.concatenate(v, axis=1) for v in small_grads], axis=1)
    small = lax.psum(small, ("gx", "gy"))
    small = lax.dynamic_index_in_dim(small, lax.axis_index("gy"), 0, keepdims=False)
    small_out, start = [], 0
    for size in small_sizes:
        small_out.append(small[:, start : start + size])
        start += size

    def stack(parts, k):
        return jnp.stack([part[k] for part in parts])

    return (
        output,
        to_blocks(grad),
        stack(attn_grads, 0),
        stack(attn_grads, 1),
        stack(attn_grads, 2),
        small_out[2],
        small_out[3],
        small_out[4],
        stack(attn_grads, 3),
        small_out[0],
        small_out[1],
        stack(ffn_grads, 0),
        stack(ffn_grads, 1),
        stack(ffn_grads, 2),
    )


def solution(mesh):
    tokens = P("gy", "gx")
    weight = P(None, "gx", "gy")
    vector = P(None, "gy")
    return jax.shard_map(
        on_device,
        mesh=mesh,
        in_specs=(
            tokens,
            weight,
            weight,
            weight,
            vector,
            vector,
            vector,
            weight,
            vector,
            vector,
            weight,
            weight,
            weight,
            tokens,
        ),
        out_specs=(
            tokens,
            tokens,
            weight,
            weight,
            weight,
            vector,
            vector,
            vector,
            weight,
            vector,
            vector,
            weight,
            weight,
            weight,
        ),
        check_vma=False,
    )
```

time: 3430 us -> 2040 us (0.59)
  waiting for transfers between devices: 2510 us -> 1220 us
  blocking collectives: 280 us -> 104 us
  local copies, waits for them, and re-layouts: 67.3 us -> 207 us
  matrix products: 411 us -> 358 us
    reduce_scatter x22 -> x16, waiting for transfers between devices: 1640 us -> 605 us  [the longest x6 352 us: scatter_x(): lax.psum_scatter(weight_grad.astype(bf16), 'gx', scatter_dimension=0, til...]
    all_gather x20 -> x16, waiting for transfers between devices: 725 us -> 602 us  [the longest x6 230 us: on_device(): lax.all_gather(w[l], 'gx', axis=0, tiled=True)]
    all_gather x6 -> x1, blocking collectives: 144 us -> 22.7 us  [on_device(): small = lax.all_gather(small, 'gy', axis=1).astype(f32)]
    reshape x0 -> x26, local copies, waits for them, and re-layouts: none -> 75 us  [the longest x12 65.3 us: scatter_attention(): grad.reshape(devices_x, D // devices_x, devices_y, -1).transpose(0, 2, 1, 3)]
    unnamed x50 -> x32, waiting for transfers between devices: 76.5 us -> 2.47 us
    transpose x0 -> x18, local copies, waits for them, and re-layouts: none -> 59.1 us  [the longest x12 49.1 us: gather_attention(): part = pack[..., start:start + size].transpose(0, 2, 1, 3)]
    all_to_all x6 -> x3, waiting for transfers between devices: 64 us -> 15.8 us  [the longest x2 15.8 us: to_blocks(): out = lax.all_to_all(flipped, 'gy', split_axis=0, concat_axis=1, tiled=True)]
    dot_general x50 -> x54, matrix products: 399 us -> 358 us  [dot(): return jnp.einsum(pattern, left, right, preferred_element_type=f32)]
  transfers between devices with their start and end apart: 52 -> 35, of which waited for: 41 -> 28; matrix products, arithmetic and copies ran while one was open for 10% -> 21% of each run, Pallas kernels for 0% -> 0%
where the time goes in v1:
time: 2040 us; the launch traced here: 2030 us
  waiting for transfers between devices  1220 us (60%)
  matrix products  358 us (18%)
  local copies, waits for them, and re-layouts  207 us (10%)
  blocking collectives  104 us (5%)
  other arithmetic  101 us (5%)
    dot_general x54, matrix products, dot(): return jnp.einsum(pattern, left, right, preferred_element_type=f32)  358 us
    reduce_scatter x6, waiting for transfers between devices, scatter_x(): lax.psum_scatter(weight_grad.astype(bf16), 'gx', scatter_dimension=0, til...  352 us
    all_gather x6, waiting for transfers between devices, on_device(): lax.all_gather(w[l], 'gx', axis=0, tiled=True)  230 us
    all_gather x2, waiting for transfers between devices, on_device(): acts_two = lax.all_gather(acts_two, 'gy', axis=0, tiled=True)  125 us
    all_gather x2, waiting for transfers between devices, on_device(): grad_out = lax.all_gather(grad.astype(bf16), 'gy', axis=0, tiled=True)  121 us
    reduce_scatter x2, waiting for transfers between devices, on_device(): lax.psum_scatter(part.astype(bf16), 'gy', scatter_dimension=0, tiled=True)  90.6 us
    all_gather x2, waiting for transfers between devices, gather_attention(): pack = lax.all_gather(pack, 'gx', axis=0)  88.8 us
    reduce_scatter x2, waiting for transfers between devices, on_device(): part = lax.psum_scatter(part, 'gy', scatter_dimension=0, tiled=True)  86.9 us
  transfers between devices with their start and end apart: 35, of which 28 were waited for; matrix products, arithmetic and copies ran while one was open for 21% of the time, Pallas kernels for 0%

profile of v1, /device:TPU:9, one launch (start us, length us, event | category | flops | bytes accessed | tf_op | source)
XLA Modules:
  0.0 2028.6 jit_solution(15205184176939957496)
XLA Ops:
  13.2 34.1 %all-gather.40.cloned.1.call-done = bf16[768,896]{1,0:T(8,128)(2,1)} async-done(((bf16[192,896]{1,0:T(8,128)(2,1)}), bf16[768,896]{1,0:T(8,128)(2,1)}) %all-gather.40.cloned.1.call-update) | async-done | bytes 1376272 | tf_op jit(solution)/shard_map/all_gather | solution.py:65
  52.6 22.7 %all-gather = bf16[2,5120]{1,0:T(2,128)(2,1)S(1)} all-gather(bf16[2,1280]{1,0:T(2,128)(2,1)S(1)} %concatenate.97), channel_id=2, replica_groups=mesh['gx'=8,'gy'=4] {'gy'}, dimensions={1}, use_global_device_ids=true | all-gather | bytes 25600 | tf_op jit(solution)/shard_map/all_gather | solution.py:125
  79.6 35.4 %all-gather.42.cloned.1.call-done = bf16[32,192,896]{2,1,0:T(8,128)(2,1)} async-done(((bf16[4,192,896]{2,1,0:T(8,128)(2,1)}), bf16[32,192,896]{2,1,0:T(8,128)(2,1)}) %all-gather.42.cloned.1.call-update) | async-done | bytes 11010064 | tf_op jit(solution)/shard_map/all_gather | solution.py:66
  199.0 51.3 %all-gather.44.cloned.1.call-done = bf16[1,1536,2240]{2,1,0:T(8,128)(2,1)} async-done(((bf16[1,192,2240]{2,1,0:T(8,128)(2,1)}), bf16[1,1536,2240]{2,1,0:T(8,128)(2,1)}) %all-gather.44.cloned.1.call-update) | async-done | bytes 6881296 | tf_op jit(solution)/shard_map/all_gather | solution.py:138
  250.4 62.1 %all-gather.30.cloned.1.call-done = bf16[1024,1536]{1,0:T(8,128)(2,1)} async-done(((bf16[256,1536]{1,0:T(8,128)(2,1)}), bf16[1024,1536]{1,0:T(8,128)(2,1)}) %all-gather.30.cloned.1.call-update) | async-done | bytes 3145744 | tf_op jit(solution)/shard_map/all_gather | solution.py:169
  325.8 39.6 %all-gather.46.cloned.1.call-done = bf16[1,1536,2240]{2,1,0:T(8,128)(2,1)} async-done(((bf16[1,192,2240]{2,1,0:T(8,128)(2,1)}), bf16[1,1536,2240]{2,1,0:T(8,128)(2,1)}) %all-gather.46.cloned.1.call-update) | async-done | bytes 6881296 | tf_op jit(solution)/shard_map/all_gather | solution.py:138
  365.4 15.8 multiply_convert_fusion.1
  381.1 35.6 %all-gather.48.cloned.1.call-done = bf16[1,1536,2240]{2,1,0:T(8,128)(2,1)} async-done(((bf16[1,192,2240]{2,1,0:T(8,128)(2,1)}), bf16[1,1536,2240]{2,1,0:T(8,128)(2,1)}) %all-gather.48.cloned.1.call-update) | async-done | bytes 6881296 | tf_op jit(solution)/shard_map/all_gather | solution.py:138
  430.7 53.4 %all-gather.52.cloned.1.call-done = bf16[32,192,896]{2,1,0:T(8,128)(2,1)} async-done(((bf16[4,192,896]{2,1,0:T(8,128)(2,1)}), bf16[32,192,896]{2,1,0:T(8,128)(2,1)}) %all-gather.52.cloned.1.call-update) | async-done | bytes 11010064 | tf_op jit(solution)/shard_map/all_gather | solution.py:66
  494.2 52.0 %reduce-scatter.17.cloned.1.call-done = bf16[256,1536]{1,0:T(8,128)(2,1)} async-done(((bf16[1024,1536]{1,0:T(8,128)(2,1)}), bf16[256,1536]{1,0:T(8,128)(2,1)}) %reduce-scatter.17.cloned.1.call-update) | async-done | bytes 786448 | tf_op jit(solution)/shard_map/reduce_scatter | solution.py:174
  603.0 30.0 %all-gather.54.cloned.1.call-done = bf16[1,1536,2240]{2,1,0:T(8,128)(2,1)} async-done(((bf16[1,192,2240]{2,1,0:T(8,128)(2,1)}), bf16[1,1536,2240]{2,1,0:T(8,128)(2,1)}) %all-gather.54.cloned.1.call-update) | async-done | bytes 6881296 | tf_op jit(solution)/shard_map/all_gather | solution.py:138
  633.0 62.8 %all-gather.34.cloned.1.call-done = bf16[1024,1536]{1,0:T(8,128)(2,1)} async-done(((bf16[256,1536]{1,0:T(8,128)(2,1)}), bf16[1024,1536]{1,0:T(8,128)(2,1)}) %all-gather.34.cloned.1.call-update) | async-done | bytes 3145744 | tf_op jit(solution)/shard_map/all_gather | solution.py:169
  709.1 38.8 %all-gather.56.cloned.1.call-done = bf16[1,1536,2240]{2,1,0:T(8,128)(2,1)} async-done(((bf16[1,192,2240]{2,1,0:T(8,128)(2,1)}), bf16[1,1536,2240]{2,1,0:T(8,128)(2,1)}) %all-gather.56.cloned.1.call-update) | async-done | bytes 6881296 | tf_op jit(solution)/shard_map/all_gather | solution.py:138
  747.9 15.8 multiply_convert_fusion
  763.7 34.8 %all-gather.58.cloned.1.call-done = bf16[1,1536,2240]{2,1,0:T(8,128)(2,1)} async-done(((bf16[1,192,2240]{2,1,0:T(8,128)(2,1)}), bf16[1,1536,2240]{2,1,0:T(8,128)(2,1)}) %all-gather.58.cloned.1.call-update) | async-done | bytes 6881296 | tf_op jit(solution)/shard_map/all_gather | solution.py:138
  811.4 40.5 %all_to_all.52 = bf16[384,4,256]{0,2,1:T(8,128)(2,1)S(1)} all-to-all(bf16[384,4,256]{0,2,1:T(8,128)(2,1)S(1)} %bitcast.594), channel_id=1, replica_groups=mesh['gx'=8,'gy'=4] {'gy'}, dimensions={1} | all-to-all | bytes 1572864 | tf_op jit(solution)/shard_map/all_to_all | solution.py:140
  852.2 34.9 %reduce-scatter.19.cloned.1.call-done = bf16[256,1536]{1,0:T(8,128)(2,1)} async-done(((bf16[1024,1536]{1,0:T(8,128)(2,1)}), bf16[256,1536]{1,0:T(8,128)(2,1)}) %reduce-scatter.19.cloned.1.call-update) | async-done | bytes 786448 | tf_op jit(solution)/shard_map/reduce_scatter | solution.py:174
  889.6 59.1 %all-gather.36.cloned.1.call-done = bf16[1024,1536]{1,0:T(8,128)(2,1)} async-done(((bf16[256,1536]{1,0:T(8,128)(2,1)}), bf16[1024,1536]{1,0:T(8,128)(2,1)}) %all-gather.36.cloned.1.call-update) | async-done | bytes 3145744 | tf_op jit(solution)/shard_map/all_gather | solution.py:230
  948.7 20.0 fusion.15
  991.5 61.0 %reduce-scatter.21.cloned.1.call-done = bf16[256,1536]{1,0:T(8,128)(2,1)} async-done(((bf16[1024,1536]{1,0:T(8,128)(2,1)}), bf16[256,1536]{1,0:T(8,128)(2,1)}) %reduce-scatter.21.cloned.1.call-update) | async-done | bytes 786448 | tf_op jit(solution)/shard_map/reduce_scatter | solution.py:238
  1130.5 61.8 %all-gather.38.cloned.1.call-done = bf16[1024,1536]{1,0:T(8,128)(2,1)} async-done(((bf16[256,1536]{1,0:T(8,128)(2,1)}), bf16[1024,1536]{1,0:T(8,128)(2,1)}) %all-gather.38.cloned.1.call-update) | async-done | bytes 3145744 | tf_op jit(solution)/shard_map/all_gather | solution.py:230
  1192.3 20.0 fusion.23
  1266.4 29.6 %reduce-scatter.25.cloned.1.call-done = bf16[256,1536]{1,0:T(8,128)(2,1)} async-done(((bf16[1024,1536]{1,0:T(8,128)(2,1)}), bf16[256,1536]{1,0:T(8,128)(2,1)}) %reduce-scatter.25.cloned.1.call-update) | async-done | bytes 786448 | tf_op jit(solution)/shard_map/reduce_scatter | solution.py:238
  1511.3 15.8 all-to-all-done.1
  1548.5 41.1 %psum.7 = f32[4,2,1280]{2,0,1:T(4,128)S(1)} all-reduce(f32[4,2,1280]{2,0,1:T(4,128)S(1)} %pad_maximum_fusion.18), channel_id=1, replica_groups=mesh['gx'=8,'gy'=4] {'gx','gy'}, use_global_device_ids=true, to_apply=%region_34.35 | all-reduce | flops 10240 | bytes 81920 | tf_op jit(solution)/shard_map/psum | solution.py:307
  1605.1 69.3 %reduce-scatter.45.cloned.1.call-done = bf16[192,2240]{1,0:T(8,128)(2,1)} async-done(((bf16[1536,2240]{1,0:T(8,128)(2,1)}), bf16[192,2240]{1,0:T(8,128)(2,1)}) %reduce-scatter.45.cloned.1.call-update) | async-done | bytes 860176 | tf_op jit(solution)/shard_map/reduce_scatter | solution.py:207
  1677.8 65.4 %reduce-scatter.43.cloned.1.call-done = bf16[192,2240]{1,0:T(8,128)(2,1)} async-done(((bf16[1536,2240]{1,0:T(8,128)(2,1)}), bf16[192,2240]{1,0:T(8,128)(2,1)}) %reduce-scatter.43.cloned.1.call-update) | async-done | bytes 860176 | tf_op jit(solution)/shard_map/reduce_scatter | solution.py:207
  1743.3 69.5 %reduce-scatter.41.cloned.1.call-done = bf16[192,2240]{1,0:T(8,128)(2,1)} async-done(((bf16[1536,2240]{1,0:T(8,128)(2,1)}), bf16[192,2240]{1,0:T(8,128)(2,1)}) %reduce-scatter.41.cloned.1.call-update) | async-done | bytes 860176 | tf_op jit(solution)/shard_map/reduce_scatter | solution.py:207
  1816.2 65.6 %reduce-scatter.39.cloned.1.call-done = bf16[192,2240]{1,0:T(8,128)(2,1)} async-done(((bf16[1536,2240]{1,0:T(8,128)(2,1)}), bf16[192,2240]{1,0:T(8,128)(2,1)}) %reduce-scatter.39.cloned.1.call-update) | async-done | bytes 860176 | tf_op jit(solution)/shard_map/reduce_scatter | solution.py:207
  1881.8 69.3 %reduce-scatter.37.cloned.1.call-done = bf16[192,2240]{1,0:T(8,128)(2,1)} async-done(((bf16[1536,2240]{1,0:T(8,128)(2,1)}), bf16[192,2240]{1,0:T(8,128)(2,1)}) %reduce-scatter.37.cloned.1.call-update) | async-done | bytes 860176 | tf_op jit(solution)/shard_map/reduce_scatter | solution.py:207
  1954.5 29.1 %reduce-scatter.35.cloned.1.call-done = bf16[1,192,896]{2,1,0:T(8,128)(2,1)} async-done(((bf16[4,192,896]{2,1,0:T(8,128)(2,1)}), bf16[1,192,896]{2,1,0:T(8,128)(2,1)}) %reduce-scatter.35.cloned.1.call-update) | async-done | bytes 344080 | tf_op jit(solution)/shard_map/reduce_scatter | solution.py:83
  1984.8 32.4 %reduce-scatter.31.cloned.1.call-done = bf16[1,192,896]{2,1,0:T(8,128)(2,1)} async-done(((bf16[4,192,896]{2,1,0:T(8,128)(2,1)}), bf16[1,192,896]{2,1,0:T(8,128)(2,1)}) %reduce-scatter.31.cloned.1.call-update) | async-done | bytes 344080 | tf_op jit(solution)/shard_map/reduce_scatter | solution.py:83
  (563 shorter events, 643.6 us)
Async XLA Ops:
  13.1 101.9 %all-gather.42.cloned.1.call-start = ((), (), s32[]{:S(2)}) async-start(), calls=%async_computation.43 | async-start | bytes 12386304 | tf_op jit(solution)/shard_map/all_gather | solution.py:66
  52.4 119.4 %all-gather.28.cloned.1.call-start = ((), (), s32[]{:S(2)}) async-start(), calls=%async_computation.20 | async-start | bytes 1310720 | tf_op jit(solution)/shard_map/all_gather | solution.py:155
  135.8 63.0 %all-gather.50.cloned.1.call-start = ((), (), s32[]{:S(2)}) async-start(), calls=%async_computation.47 | async-start | bytes 1720320 | tf_op jit(solution)/shard_map/all_gather | solution.py:65
  139.4 111.0 %all-gather.44.cloned.1.call-start = ((), (), s32[]{:S(2)}) async-start(), calls=%async_computation.44 | async-start | bytes 7962624 | tf_op jit(solution)/shard_map/all_gather | solution.py:138
  142.2 170.3 %all-gather.30.cloned.1.call-start = ((), (), s32[]{:S(2)}) async-start(), calls=%async_computation.21 | async-start | bytes 3932160 | tf_op jit(solution)/shard_map/all_gather | solution.py:169
  191.6 173.7 %all-gather.46.cloned.1.call-start = ((), (), s32[]{:S(2)}) async-start(), calls=%async_computation.45 | async-start | bytes 7962624 | tf_op jit(solution)/shard_map/all_gather | solution.py:138
  194.5 222.2 %all-gather.48.cloned.1.call-start = ((), (), s32[]{:S(2)}) async-start(), calls=%async_computation.46 | async-start | bytes 7962624 | tf_op jit(solution)/shard_map/all_gather | solution.py:138
  195.9 288.2 %all-gather.52.cloned.1.call-start = ((), (), s32[]{:S(2)}) async-start(), calls=%async_computation.48 | async-start | bytes 12386304 | tf_op jit(solution)/shard_map/all_gather | solution.py:66
  198.8 347.4 %reduce-scatter.17.cloned.1.call-start = ((), (), s32[]{:S(2)}) async-start(), calls=%async_computation.22 | async-start | bytes 3932160 | tf_op jit(solution)/shard_map/reduce_scatter | solution.py:174
  429.3 153.8 %all-gather.32.cloned.1.call-start = ((), (), s32[]{:S(2)}) async-start(), calls=%async_computation.23 | async-start | bytes 1310720 | tf_op jit(solution)/shard_map/all_gather | solution.py:155
  552.2 80.7 %all-gather.54.cloned.1.call-start = ((), (), s32[]{:S(2)}) async-start(), calls=%async_computation.49 | async-start | bytes 7962624 | tf_op jit(solution)/shard_map/all_gather | solution.py:138
  552.8 143.0 %all-gather.34.cloned.1.call-start = ((), (), s32[]{:S(2)}) async-start(), calls=%async_computation.24 | async-start | bytes 3932160 | tf_op jit(solution)/shard_map/all_gather | solution.py:169
  601.6 146.3 %all-gather.56.cloned.1.call-start = ((), (), s32[]{:S(2)}) async-start(), calls=%async_computation.50 | async-start | bytes 7962624 | tf_op jit(solution)/shard_map/all_gather | solution.py:138
  602.1 196.4 %all-gather.58.cloned.1.call-start = ((), (), s32[]{:S(2)}) async-start(), calls=%async_computation.51 | async-start | bytes 7962624 | tf_op jit(solution)/shard_map/all_gather | solution.py:138
  602.7 284.4 %reduce-scatter.19.cloned.1.call-start = ((), (), s32[]{:S(2)}) async-start(), calls=%async_computation.25 | async-start | bytes 3932160 | tf_op jit(solution)/shard_map/reduce_scatter | solution.py:174
  811.0 137.7 %all-gather.36.cloned.1.call-start = ((), (), s32[]{:S(2)}) async-start(), calls=%async_computation.26 | async-start | bytes 3932160 | tf_op jit(solution)/shard_map/all_gather | solution.py:230
  889.6 163.0 %reduce-scatter.21.cloned.1.call-start = ((), (), s32[]{:S(2)}) async-start(), calls=%async_computation.27 | async-start | bytes 3932160 | tf_op jit(solution)/shard_map/reduce_scatter | solution.py:238
  991.5 129.5 %reduce-scatter.23.cloned.1.call-start = ((), (), s32[]{:S(2)}) async-start(), calls=%async_computation.28 | async-start | bytes 1310720 | tf_op jit(solution)/shard_map/reduce_scatter | solution.py:269
  1095.2 97.1 %all-gather.38.cloned.1.call-start = ((), (), s32[]{:S(2)}) async-start(), calls=%async_computation.29 | async-start | bytes 3932160 | tf_op jit(solution)/shard_map/all_gather | solution.py:230
  1130.5 165.5 %reduce-scatter.25.cloned.1.call-start = ((), (), s32[]{:S(2)}) async-start(), calls=%async_computation.30 | async-start | bytes 3932160 | tf_op jit(solution)/shard_map/reduce_scatter | solution.py:238
  1234.9 167.8 %reduce-scatter.27.cloned.1.call-start = ((), (), s32[]{:S(2)}) async-start(), calls=%async_computation.31 | async-start | bytes 1310720 | tf_op jit(solution)/shard_map/reduce_scatter | solution.py:269
  1334.3 176.5 %reduce-scatter.33.cloned.1.call-start = ((), (), s32[]{:S(2)}) async-start(), calls=%async_computation.34 | async-start | bytes 12386304 | tf_op jit(solution)/shard_map/reduce_scatter | solution.py:82
  1362.7 226.9 %reduce-scatter.29.cloned.1.call-start = ((), (), s32[]{:S(2)}) async-start(), calls=%async_computation.32 | async-start | bytes 12386304 | tf_op jit(solution)/shard_map/reduce_scatter | solution.py:82
  1426.5 178.5 %reduce-scatter.47.cloned.1.call-start = ((), (), s32[]{:S(2)}) async-start(), calls=%async_computation.41 | async-start | bytes 7962624 | tf_op jit(solution)/shard_map/reduce_scatter | solution.py:207
  1439.2 235.2 %reduce-scatter.45.cloned.1.call-start = ((), (), s32[]{:S(2)}) async-start(), calls=%async_computation.40 | async-start | bytes 7962624 | tf_op jit(solution)/shard_map/reduce_scatter | solution.py:207
  1451.8 291.5 %reduce-scatter.43.cloned.1.call-start = ((), (), s32[]{:S(2)}) async-start(), calls=%async_computation.39 | async-start | bytes 7962624 | tf_op jit(solution)/shard_map/reduce_scatter | solution.py:207
  1464.4 348.3 %reduce-scatter.41.cloned.1.call-start = ((), (), s32[]{:S(2)}) async-start(), calls=%async_computation.38 | async-start | bytes 7962624 | tf_op jit(solution)/shard_map/reduce_scatter | solution.py:207
  1478.4 403.4 %reduce-scatter.39.cloned.1.call-start = ((), (), s32[]{:S(2)}) async-start(), calls=%async_computation.37 | async-start | bytes 7962624 | tf_op jit(solution)/shard_map/reduce_scatter | solution.py:207
  1491.7 459.4 %reduce-scatter.37.cloned.1.call-start = ((), (), s32[]{:S(2)}) async-start(), calls=%async_computation.36 | async-start | bytes 7962624 | tf_op jit(solution)/shard_map/reduce_scatter | solution.py:207
  1510.5 473.1 %reduce-scatter.35.cloned.1.call-start = ((), (), s32[]{:S(2)}) async-start(), calls=%async_computation.35 | async-start | bytes 1720320 | tf_op jit(solution)/shard_map/reduce_scatter | solution.py:83
  1538.1 52.8 %all-to-all-start.3 = ((bf16[4,384,256]{1,2,0:T(8,128)(2,1)}), bf16[4,384,256]{1,2,0:T(8,128)(2,1)S(1)}, u32[]{:S(2)}, u32[]{:S(2)}) async-start(bf16[4,384,256]{1,2,0:T(8,128)(2,1)} %bitcast.528), calls=%async_computation.9 | async-start | bytes 1572864 | tf_op jit(solution)/shard_map/all_to_all | solution.py:197
  1544.9 472.3 %reduce-scatter.31.cloned.1.call-start = ((), (), s32[]{:S(2)}) async-start(), calls=%async_computation.33 | async-start | bytes 1720320 | tf_op jit(solution)/shard_map/reduce_scatter | solution.py:83
  (127 other events, 2607.2 us)
Sparse Core Ops, SparseCore 0:
  13.2 33.9 all-gather.39
  49.1 65.8 all-gather.41
  135.9 26.2 all-gather.27
  164.2 34.5 all-gather.49
  201.1 49.2 all-gather.43
  251.8 60.6 all-gather.29
  314.9 50.3 all-gather.45
  367.8 48.8 all-gather.47
  418.6 65.4 all-gather.51
  486.8 59.4 reduce-scatter.16
  552.3 27.1 all-gather.31
  581.8 51.0 all-gather.53
  635.1 60.6 all-gather.33
  697.5 50.3 all-gather.55
  749.7 48.8 all-gather.57
  811.1 75.9 reduce-scatter.18
  889.7 59.0 all-gather.35
  991.6 60.9 reduce-scatter.20
  1095.3 25.5 reduce-scatter.22
  1130.6 61.6 all-gather.37
  1235.0 60.9 reduce-scatter.24
  1334.4 25.5 reduce-scatter.26
  1363.7 84.6 reduce-scatter.32
  1451.8 83.9 reduce-scatter.28
  1539.4 65.6 reduce-scatter.46
  1608.8 65.4 reduce-scatter.44
  1677.7 65.4 reduce-scatter.42
  1747.2 65.5 reduce-scatter.40
  1816.3 65.4 reduce-scatter.38
  1885.5 65.4 reduce-scatter.36
  1953.4 30.2 reduce-scatter.34
  1986.1 31.0 reduce-scatter.30

commit v2 on v1

--- a/solution.py
+++ b/solution.py
@@ -3,6 +3,8 @@
 import jax
 import jax.numpy as jnp
 from jax import lax
+from jax.experimental import pallas as pl
+from jax.experimental.pallas import tpu as pltpu
 from jax.sharding import PartitionSpec as P
 
 D = 1536
@@ -18,6 +20,8 @@
 penalty = 0.25
 bf16 = jnp.bfloat16
 f32 = jnp.float32
+MESH = pl.DeviceIdType.MESH
+VMEM_LIMIT = 60 << 20
 
 
 def rope_tables(positions, head_size):
@@ -91,6 +95,352 @@
 def score_block(q_rot, k_rot, allowed):
     scores = dot("qkgd,skd->kgqs", q_rot, k_rot) * (1.0 / math.sqrt(HEAD_DIM))
     return jnp.where(allowed, scores, -1e30)
+
+
+FF_CHUNK = 512
+PIECES = 4
+
+
+def spans(total):
+    return [(start, min(FF_CHUNK, total - start)) for start in range(0, total, FF_CHUNK)]
+
+
+def nn(left, right):
+    return lax.dot_general(left, right, (((1,), (0,)), ((), ())), preferred_element_type=f32)
+
+
+def nt(left, right):
+    return lax.dot_general(left, right, (((1,), (1,)), ((), ())), preferred_element_type=f32)
+
+
+def line_pass(own_ref, sum_ref, gathered, part, own, outb, inb, sems, load, finish):
+    own_sem, ag_send, ag_recv, rs_send, rs_recv = sems
+    gx, me, size = lax.axis_index("gx"), lax.axis_index("gy"), lax.axis_size("gy")
+    rows = own.shape[0]
+    piece = rows // PIECES
+    last = size - 1
+    inner = jnp.logical_and(me > 0, me < last)
+
+    first = pltpu.make_async_copy(own_ref, gathered.at[me], own_sem)
+    first.start()
+    barrier = pltpu.get_barrier_semaphore()
+
+    @pl.when(me > 0)
+    def _():
+        pl.semaphore_signal(barrier, inc=1, device_id=(gx, me - 1), device_id_type=MESH)
+
+    @pl.when(me < last)
+    def _():
+        pl.semaphore_signal(barrier, inc=1, device_id=(gx, me + 1), device_id_type=MESH)
+
+    pl.semaphore_wait(barrier, jnp.where(inner, 2, 1))
+    first.wait()
+
+    def gather_copy(b, s, way):
+        here = gathered.at[b, pl.ds(s * piece, piece)]
+        return pltpu.make_async_remote_copy(
+            src_ref=here,
+            dst_ref=here,
+            send_sem=ag_send.at[b, way, s],
+            recv_sem=ag_recv.at[b, s],
+            device_id=(gx, me - 1 + 2 * way),
+            device_id_type=MESH,
+        )
+
+    def sum_copy(b, s):
+        towards = jnp.where(b > me, me + 1, me - 1)
+        slot = jnp.where(jnp.logical_and(towards == b, me > b), size, b)
+        return pltpu.make_async_remote_copy(
+            src_ref=outb.at[b, pl.ds(s * piece, piece)],
+            dst_ref=inb.at[slot, pl.ds(s * piece, piece)],
+            send_sem=rs_send.at[b, s],
+            recv_sem=rs_recv.at[slot, s],
+            device_id=(gx, towards),
+            device_id_type=MESH,
+        )
+
+    def sum_arrived(slot, s):
+        here = inb.at[slot, pl.ds(s * piece, piece)]
+        pltpu.make_async_copy(here, here, rs_recv.at[slot, s]).wait()
+
+    def step(t, carry):
+        short = jnp.minimum(me, last - me)
+        even = lax.rem(t, 2) == 0
+        near = jnp.where(even, me - t // 2, me + (t + 1) // 2)
+        far = jnp.where(me < last - me, me + (t - short), me - (t - short))
+        b = jnp.where(t <= 2 * short, near, far)
+        for s in range(PIECES):
+
+            @pl.when(t > 0)
+            def _():
+                gather_copy(b, s, 0).wait_recv()
+
+            @pl.when(jnp.logical_and(b <= me, me < last))
+            def _():
+                gather_copy(b, s, 1).start()
+
+            @pl.when(jnp.logical_and(b >= me, me > 0))
+            def _():
+                gather_copy(b, s, 0).start()
+
+        @pl.when(t == 0)
+        def _():
+            load()
+
+        finish(b)
+
+        @pl.when(b == me)
+        def _():
+            own[...] = part[...]
+
+        @pl.when(b != me)
+        def _():
+            outb[b] = part[...].astype(bf16)
+
+            @pl.when(jnp.logical_not(inner))
+            def _():
+                for s in range(PIECES):
+                    sum_copy(b, s).start()
+
+        return carry
+
+    lax.fori_loop(0, size, step, 0)
+
+    def relay(t, carry):
+        above, below = last - me, me
+        low = jnp.where(t < above, me + 1 + t, me - 1 - (t - above))
+        high = jnp.where(t < below, me - 1 - t, me + 1 + (t - below))
+        b = jnp.where(2 * me < size, low, high)
+
+        @pl.when(inner)
+        def _():
+            for s in range(PIECES):
+                at = pl.ds(s * piece, piece)
+                sum_arrived(b, s)
+                outb[b, at] = (outb[b, at].astype(f32) + inb[b, at].astype(f32)).astype(bf16)
+                sum_copy(b, s).start()
+
+        return carry
+
+    lax.fori_loop(0, last, relay, 0)
+
+    @pl.when(me > 0)
+    def _():
+        for s in range(PIECES):
+            sum_arrived(me, s)
+        own[...] += inb[me].astype(f32)
+
+    @pl.when(me < last)
+    def _():
+        for s in range(PIECES):
+            sum_arrived(size, s)
+        own[...] += inb[size].astype(f32)
+
+    sum_ref[...] = own[...]
+
+    def drain(b, carry):
+        for s in range(PIECES):
+
+            @pl.when(jnp.logical_and(b <= me, me < last))
+            def _():
+                gather_copy(b, s, 1).wait_send()
+
+            @pl.when(jnp.logical_and(b >= me, me > 0))
+            def _():
+                gather_copy(b, s, 0).wait_send()
+
+            @pl.when(b != me)
+            def _():
+                sum_copy(b, s).wait_send()
+
+        return carry
+
+    lax.fori_loop(0, size, drain, 0)
+
+
+def line_scratch(size, rows, width):
+    return [
+        pltpu.VMEM((size, rows, width), bf16),
+        pltpu.VMEM((rows, width), f32),
+        pltpu.VMEM((rows, width), f32),
+        pltpu.VMEM((size, rows, width), bf16),
+        pltpu.VMEM((size + 1, rows, width), bf16),
+        pltpu.SemaphoreType.DMA,
+        pltpu.SemaphoreType.DMA((size, 2, PIECES)),
+        pltpu.SemaphoreType.DMA((size, PIECES)),
+        pltpu.SemaphoreType.DMA((size, PIECES)),
+        pltpu.SemaphoreType.DMA((size + 1, PIECES)),
+    ]
+
+
+LINE = 10
+
+
+def forward_kernel(
+    acts_ref, wg_ref, wu_ref, wd_ref, sum_ref, full_ref, gate_ref, up_ref, hidden_ref, *scratch
+):
+    gathered, part, own, outb, inb = scratch[:5]
+    sems = scratch[5:LINE]
+    wg, wu, wd, gate, up, hidden, w_sem, out_sem = scratch[LINE:]
+    loads = [
+        pltpu.make_async_copy(src, dst, w_sem.at[k])
+        for k, (src, dst) in enumerate(((wg_ref, wg), (wu_ref, wu), (wd_ref, wd)))
+    ]
+    for copy in loads:
+        copy.start()
+
+    def load():
+        for copy in loads:
+            copy.wait()
+
+    def results(b):
+        pairs = ((gathered, full_ref), (gate, gate_ref), (up, up_ref), (hidden, hidden_ref))
+        return [
+            pltpu.make_async_copy(src.at[b], dst.at[b], out_sem.at[b, k])
+            for k, (src, dst) in enumerate(pairs)
+        ]
+
+    def finish(b):
+        block = gathered[b]
+        for start, width in spans(wg.shape[1]):
+            at = slice(start, start + width)
+            g = nn(block, wg[:, at])
+            u = nn(block, wu[:, at])
+            h = (g * lax.logistic(g) * u).astype(bf16)
+            gate[b, :, at] = g.astype(bf16)
+            up[b, :, at] = u.astype(bf16)
+            hidden[b, :, at] = h
+            p = nt(h, wd[:, at])
+            if start == 0:
+                part[...] = p
+            else:
+                part[...] += p
+        for copy in results(b):
+            copy.start()
+
+    line_pass(acts_ref, sum_ref, gathered, part, own, outb, inb, sems, load, finish)
+
+    def settle(b, carry):
+        for copy in results(b):
+            copy.wait()
+        return carry
+
+    lax.fori_loop(0, gathered.shape[0], settle, 0)
+
+
+ANY = pl.BlockSpec(memory_space=pl.ANY)
+
+
+def forward_ffn(acts, wg, wu, wd):
+    rows, width = acts.shape
+    size, hidden = lax.axis_size("gy"), wg.shape[1]
+    wide = jax.ShapeDtypeStruct((size, rows, hidden), bf16)
+    return pl.pallas_call(
+        forward_kernel,
+        out_shape=[
+            jax.ShapeDtypeStruct((rows, width), f32),
+            jax.ShapeDtypeStruct((size, rows, width), bf16),
+            wide,
+            wide,
+            wide,
+        ],
+        in_specs=[ANY] * 4,
+        out_specs=[pl.BlockSpec(memory_space=pltpu.VMEM)] + [ANY] * 4,
+        scratch_shapes=line_scratch(size, rows, width)
+        + [pltpu.VMEM((width, hidden), bf16)] * 3
+        + [pltpu.VMEM((size, rows, hidden), bf16)] * 3
+        + [pltpu.SemaphoreType.DMA((3,)), pltpu.SemaphoreType.DMA((size, 4))],
+        compiler_params=pltpu.CompilerParams(
+            collective_id=0, has_side_effects=True, vmem_limit_bytes=VMEM_LIMIT
+        ),
+        cost_estimate=pl.CostEstimate(
+            flops=6 * size * rows * width * hidden, bytes_accessed=40 << 20, transcendentals=0
+        ),
+        name="ffn_forward",
+    )(acts, wg, wu, wd)
+
+
+def backward_kernel(
+    grad_ref, gate_ref, up_ref, wg_ref, wu_ref, wd_ref, sum_ref, full_ref, dg_ref, du_ref, *scratch
+):
+    gathered, part, own, outb, inb = scratch[:5]
+    sems = scratch[5:LINE]
+    wg, wu, wd, gate, up, w_sem, out_sem = scratch[LINE:]
+    operands = ((wd_ref, wd), (gate_ref, gate), (up_ref, up), (wg_ref, wg), (wu_ref, wu))
+    loads = [
+        pltpu.make_async_copy(src, dst, w_sem.at[k]) for k, (src, dst) in enumerate(operands)
+    ]
+    for copy in loads:
+        copy.start()
+
+    def load():
+        for copy in loads:
+            copy.wait()
+
+    def results(b):
+        pairs = ((gathered, full_ref), (gate, dg_ref), (up, du_ref))
+        return [
+            pltpu.make_async_copy(src.at[b], dst.at[b], out_sem.at[b, k])
+            for k, (src, dst) in enumerate(pairs)
+        ]
+
+    def finish(b):
+        block = gathered[b]
+        for start, width in spans(wg.shape[1]):
+            at = slice(start, start + width)
+            d = nn(block, wd[:, at])
+            g = gate[b, :, at].astype(f32)
+            u = up[b, :, at].astype(f32)
+            sigma = lax.logistic(g)
+            ds = d * sigma
+            dg = (ds * u * (1.0 + g * (1.0 - sigma))).astype(bf16)
+            du = (ds * g).astype(bf16)
+            gate[b, :, at] = dg
+            up[b, :, at] = du
+            p = nt(dg, wg[:, at]) + nt(du, wu[:, at])
+            if start == 0:
+                part[...] = p
+            else:
+                part[...] += p
+        for copy in results(b):
+            copy.start()
+
+    line_pass(grad_ref, sum_ref, gathered, part, own, outb, inb, sems, load, finish)
+
+    def settle(b, carry):
+        for copy in results(b):
+            copy.wait()
+        return carry
+
+    lax.fori_loop(0, gathered.shape[0], settle, 0)
+
+
+def backward_ffn(grad, gate, up, wg, wu, wd):
+    rows, width = grad.shape
+    size, hidden = lax.axis_size("gy"), wg.shape[1]
+    wide = jax.ShapeDtypeStruct((size, rows, hidden), bf16)
+    return pl.pallas_call(
+        backward_kernel,
+        out_shape=[
+            jax.ShapeDtypeStruct((rows, width), f32),
+            jax.ShapeDtypeStruct((size, rows, width), bf16),
+            wide,
+            wide,
+        ],
+        in_specs=[ANY] * 6,
+        out_specs=[pl.BlockSpec(memory_space=pltpu.VMEM)] + [ANY] * 3,
+        scratch_shapes=line_scratch(size, rows, width)
+        + [pltpu.VMEM((width, hidden), bf16)] * 3
+        + [pltpu.VMEM((size, rows, hidden), bf16)] * 2
+        + [pltpu.SemaphoreType.DMA((5,)), pltpu.SemaphoreType.DMA((size, 3))],
+        compiler_params=pltpu.CompilerParams(
+            collective_id=1, has_side_effects=True, vmem_limit_bytes=VMEM_LIMIT
+        ),
+        cost_estimate=pl.CostEstimate(
+            flops=6 * size * rows * width * hidden, bytes_accessed=40 << 20, transcendentals=0
+        ),
+        name="ffn_backward",
+    )(grad, gate, up, wg, wu, wd)
 
 
 def on_device(
@@ -166,12 +516,7 @@
         middle = resid + dot("tq,dq->td", mixed, wo)
         normed_two, scale_two = rms_parts(middle)
         acts_two = (normed_two * gains_two[l]).astype(bf16)
-        acts_two = lax.all_gather(acts_two, "gy", axis=0, tiled=True)
-        gate = dot("td,df->tf", acts_two, wg)
-        up = dot("td,df->tf", acts_two, wu)
-        hidden = (gate * lax.logistic(gate) * up).astype(bf16)
-        part = dot("tf,df->td", hidden, wd).astype(bf16)
-        part = lax.psum_scatter(part, "gy", scatter_dimension=0, tiled=True)
+        part, acts_two, gate, up, hidden = forward_ffn(acts_two, wg, wu, wd)
         kept.append(
             (
                 normed_one,
@@ -185,12 +530,12 @@
                 normed_two,
                 scale_two,
                 acts_two,
-                gate.astype(bf16),
-                up.astype(bf16),
+                gate,
+                up,
                 hidden,
             )
         )
-        resid = middle + part.astype(f32)
+        resid = middle + part
 
     def to_blocks(tokens_major):
         flipped = tokens_major.astype(bf16).T
@@ -227,21 +572,13 @@
         ) = kept[l]
         wq, wk, wv, wo = attn_full[l]
         wg, wu, wd = ffn_full[l]
-        grad_out = lax.all_gather(grad.astype(bf16), "gy", axis=0, tiled=True)
-        grad_hidden = dot("td,df->tf", grad_out, wd)
-        gate = gate.astype(f32)
-        up = up.astype(f32)
-        sigma = lax.logistic(gate)
-        grad_gate = (grad_hidden * up * sigma * (1.0 + gate * (1.0 - sigma))).astype(bf16)
-        grad_up = (grad_hidden * gate * sigma).astype(bf16)
-        part = dot("tf,df->td", grad_gate, wg) + dot("tf,df->td", grad_up, wu)
-        grad_acts_two = lax.psum_scatter(
-            part.astype(bf16), "gy", scatter_dimension=0, tiled=True
-        ).astype(f32)
+        grad_acts_two, grad_out, grad_gate, grad_up = backward_ffn(
+            grad.astype(bf16), gate, up, wg, wu, wd
+        )
         ffn_grads[l] = (
-            scatter_x(dot("td,tf->df", acts_two, grad_gate)),
-            scatter_x(dot("td,tf->df", acts_two, grad_up)),
-            scatter_x(dot("td,tf->df", grad_out, hidden)),
+            scatter_x(dot("ztd,ztf->df", acts_two, grad_gate)),
+            scatter_x(dot("ztd,ztf->df", acts_two, grad_up)),
+            scatter_x(dot("ztd,ztf->df", grad_out, hidden)),
         )
         grad_norm, grad_gain_two = norm_backward(
             grad_acts_two, normed_two, scale_two, gains_two[l]

time: 2040 us -> 1870 us (0.917)
  Pallas kernels: 0 us -> 415 us
  waiting for transfers between devices: 1220 us -> 836 us
  matrix products: 358 us -> 182 us
  blocking collectives: 104 us -> 68.1 us
    pallas_call x0 -> x4, Pallas kernels: none -> 415 us  [the longest x2 208 us: forward_ffn(): pl.pallas_call(forward_kernel, out_shape=[jax.ShapeDtypeStruct((rows, wid...]
    all_gather x4 -> x0, waiting for transfers between devices: 246 us -> none  [the longest x2 125 us: on_device(): acts_two = lax.all_gather(acts_two, 'gy', axis=0, tiled=True)]
    reduce_scatter x4 -> x0, waiting for transfers between devices: 178 us -> none  [the longest x2 90.6 us: on_device(): lax.psum_scatter(part.astype(bf16), 'gy', scatter_dimension=0, tiled=True)]
    dot_general x54 -> x42, matrix products: 358 us -> 182 us  [dot(): return jnp.einsum(pattern, left, right, preferred_element_type=f32)]
    all_to_all x1 -> x0, blocking collectives: 40.5 us -> none  [on_device(): lax.all_to_all(cotangent, 'gy', split_axis=1, concat_axis=0, tiled=True)]
    all_gather x2, waiting for transfers between devices: 36.9 us -> 67.7 us  [gather_attention(): pack = lax.all_gather(pack, 'gy', axis=0)]
    all_to_all x0 -> x1, waiting for transfers between devices: none -> 28.3 us  [on_device(): lax.all_to_all(cotangent, 'gy', split_axis=1, concat_axis=0, tiled=True)]
    all_gather x2, waiting for transfers between devices: 88.8 us -> 64.6 us  [gather_attention(): pack = lax.all_gather(pack, 'gx', axis=0)]
  transfers between devices with their start and end apart: 35 -> 28, of which waited for: 28 -> 21; matrix products, arithmetic and copies ran while one was open for 21% -> 20% of each run, Pallas kernels for 0% -> 0%
where the time goes in v2:
time: 1870 us; the launch traced here: 1850 us
  waiting for transfers between devices  836 us (45%)
  Pallas kernels  415 us (22%)
  local copies, waits for them, and re-layouts  209 us (11%)
  matrix products  182 us (10%)
  other arithmetic  98.3 us (5%)
  blocking collectives  68.1 us (4%)
  starting transfers between devices  29.5 us (2%)
    reduce_scatter x6, waiting for transfers between devices, scatter_x(): lax.psum_scatter(weight_grad.astype(bf16), 'gx', scatter_dimension=0, til...  350 us
    all_gather x6, waiting for transfers between devices, on_device(): lax.all_gather(w[l], 'gx', axis=0, tiled=True)  242 us
    pallas_call x2, Pallas kernels, forward_ffn(): pl.pallas_call(forward_kernel, out_shape=[jax.ShapeDtypeStruct((rows, wid...  208 us
    pallas_call x2, Pallas kernels, backward_ffn(): pl.pallas_call(backward_kernel, out_shape=[jax.ShapeDtypeStruct((rows, wi...  207 us
    dot_general x42, matrix products, dot(): return jnp.einsum(pattern, left, right, preferred_element_type=f32)  182 us
    all_gather x2, waiting for transfers between devices, gather_attention(): pack = lax.all_gather(pack, 'gy', axis=0)  67.7 us
    reshape x12, local copies, waits for them, and re-layouts, scatter_attention(): grad.reshape(devices_x, D // devices_x, devices_y, -1).transpose(0, 2, 1, 3)  64.9 us
    all_gather x2, waiting for transfers between devices, gather_attention(): pack = lax.all_gather(pack, 'gx', axis=0)  64.6 us
  transfers between devices with their start and end apart: 28, of which 21 were waited for; matrix products, arithmetic and copies ran while one was open for 20% of the time, Pallas kernels for 0%

profile of v2, /device:TPU:9, one launch (start us, length us, event | category | flops | bytes accessed | tf_op | source)
XLA Modules:
  0.0 1854.6 jit_solution(3418528406307396374)
XLA Ops:
  12.4 32.9 %all-gather.28.cloned.1.call-done = bf16[768,896]{1,0:T(8,128)(2,1)} async-done(((bf16[192,896]{1,0:T(8,128)(2,1)}), bf16[768,896]{1,0:T(8,128)(2,1)}) %all-gather.28.cloned.1.call-update) | async-done | bytes 1376272 | tf_op jit(solution)/shard_map/all_gather | solution.py:69
  45.3 34.9 %all-gather.38.cloned.1.call-done = bf16[768,896]{1,0:T(8,128)(2,1)} async-done(((bf16[192,896]{1,0:T(8,128)(2,1)}), bf16[768,896]{1,0:T(8,128)(2,1)}) %all-gather.38.cloned.1.call-update) | async-done | bytes 1376272 | tf_op jit(solution)/shard_map/all_gather | solution.py:69
  85.6 22.7 %all-gather = bf16[2,5120]{1,0:T(2,128)(2,1)S(1)} all-gather(bf16[2,1280]{1,0:T(2,128)(2,1)S(1)} %concatenate.97), channel_id=2, replica_groups=mesh['gx'=8,'gy'=4] {'gy'}, dimensions={1}, use_global_device_ids=true | all-gather | bytes 25600 | tf_op jit(solution)/shard_map/all_gather | solution.py:475
  110.3 37.7 %all-gather.30.cloned.1.call-done = bf16[32,192,896]{2,1,0:T(8,128)(2,1)} async-done(((bf16[4,192,896]{2,1,0:T(8,128)(2,1)}), bf16[32,192,896]{2,1,0:T(8,128)(2,1)}) %all-gather.30.cloned.1.call-update) | async-done | bytes 11010064 | tf_op jit(solution)/shard_map/all_gather | solution.py:70
  188.3 26.9 %all-gather.40.cloned.1.call-done = bf16[32,192,896]{2,1,0:T(8,128)(2,1)} async-done(((bf16[4,192,896]{2,1,0:T(8,128)(2,1)}), bf16[32,192,896]{2,1,0:T(8,128)(2,1)}) %all-gather.40.cloned.1.call-update) | async-done | bytes 11010064 | tf_op jit(solution)/shard_map/all_gather | solution.py:70
  266.6 30.3 %all-gather.32.cloned.1.call-done = bf16[1,1536,2240]{2,1,0:T(8,128)(2,1)} async-done(((bf16[1,192,2240]{2,1,0:T(8,128)(2,1)}), bf16[1,1536,2240]{2,1,0:T(8,128)(2,1)}) %all-gather.32.cloned.1.call-update) | async-done | bytes 6881296 | tf_op jit(solution)/shard_map/all_gather | solution.py:488
  297.0 50.8 %all-gather.34.cloned.1.call-done = bf16[1,1536,2240]{2,1,0:T(8,128)(2,1)} async-done(((bf16[1,192,2240]{2,1,0:T(8,128)(2,1)}), bf16[1,1536,2240]{2,1,0:T(8,128)(2,1)}) %all-gather.34.cloned.1.call-update) | async-done | bytes 6881296 | tf_op jit(solution)/shard_map/all_gather | solution.py:488
  347.7 50.8 %all-gather.36.cloned.1.call-done = bf16[1,1536,2240]{2,1,0:T(8,128)(2,1)} async-done(((bf16[1,192,2240]{2,1,0:T(8,128)(2,1)}), bf16[1,1536,2240]{2,1,0:T(8,128)(2,1)}) %all-gather.36.cloned.1.call-update) | async-done | bytes 6881296 | tf_op jit(solution)/shard_map/all_gather | solution.py:488
  398.5 104.2 %ffn_forward.2 = (f32[256,1536]{1,0:T(8,128)}, bf16[4,256,1536]{2,1,0:T(8,128)(2,1)}, bf16[4,256,2240]{2,1,0:T(8,128)(2,1)}, bf16[4,256,2240]{2,1,0:T(8,128)(2,1)}, bf16[4,256,2240]{2,1,0:T(8,128)(2,1)}) custom-call(bf16[256,1536]{1,0:T(8,128)(2,1)} %multiply_convert_fusion.2.acts_ref, bf16[1536,2240]{1,0:T(8,128)(2,1)} %bitcast.595, ...), custom_call_target="tpu_custom_call" | custom-call | flops 21139292160 | bytes 41943040 | tf_op jit(solution)/shard_map/ffn_forward/pallas_call | solution.py:338
  520.5 28.3 %all-to-all-done.2 = bf16[384,4,256]{0,2,1:T(8,128)(2,1)S(1)} async-done(((bf16[384,4,256]{0,2,1:T(8,128)(2,1)}), bf16[384,4,256]{0,2,1:T(8,128)(2,1)S(1)}, u32[]{:S(2)}, u32[]{:S(2)}) %all-to-all-start.2) | async-done | bytes 786464 | tf_op jit(solution)/shard_map/all_to_all | solution.py:490
  607.6 50.8 %all-gather.44.cloned.1.call-done = bf16[1,1536,2240]{2,1,0:T(8,128)(2,1)} async-done(((bf16[1,192,2240]{2,1,0:T(8,128)(2,1)}), bf16[1,1536,2240]{2,1,0:T(8,128)(2,1)}) %all-gather.44.cloned.1.call-update) | async-done | bytes 6881296 | tf_op jit(solution)/shard_map/all_gather | solution.py:488
  658.4 50.6 %all-gather.46.cloned.1.call-done = bf16[1,1536,2240]{2,1,0:T(8,128)(2,1)} async-done(((bf16[1,192,2240]{2,1,0:T(8,128)(2,1)}), bf16[1,1536,2240]{2,1,0:T(8,128)(2,1)}) %all-gather.46.cloned.1.call-update) | async-done | bytes 6881296 | tf_op jit(solution)/shard_map/all_gather | solution.py:488
  709.0 104.2 %ffn_forward.3 = (f32[256,1536]{1,0:T(8,128)}, bf16[4,256,1536]{2,1,0:T(8,128)(2,1)}, bf16[4,256,2240]{2,1,0:T(8,128)(2,1)}, bf16[4,256,2240]{2,1,0:T(8,128)(2,1)}, bf16[4,256,2240]{2,1,0:T(8,128)(2,1)}) custom-call(bf16[256,1536]{1,0:T(8,128)(2,1)} %multiply_convert_fusion.acts_ref, bf16[1536,2240]{1,0:T(8,128)(2,1)} %bitcast.601, ...), custom_call_target="tpu_custom_call" | custom-call | flops 21139292160 | bytes 41943040 | tf_op jit(solution)/shard_map/ffn_forward/pallas_call | solution.py:338
  816.5 104.7 %ffn_backward.2 = (f32[256,1536]{1,0:T(8,128)}, bf16[4,256,1536]{2,1,0:T(8,128)(2,1)}, bf16[4,256,2240]{2,1,0:T(8,128)(2,1)}, bf16[4,256,2240]{2,1,0:T(8,128)(2,1)}) custom-call(bf16[256,1536]{1,0:T(8,128)(2,1)} %fusion.56.grad_ref, bf16[4,256,2240]{2,1,0:T(8,128)(2,1)} %get-tuple-element.34.gate_ref, bf16[4,256,2240]{2,1,0:T(8,128)(2,1)} %get-tuple-element.35.up_ref, ...), custom_call_target="tpu_custom_call" | custom-call | flops 21139292160 | bytes 41943040 | tf_op jit(solution)/shard_map/ffn_backward/pallas_call | solution.py:422
  999.2 102.1 %ffn_backward.3 = (f32[256,1536]{1,0:T(8,128)}, bf16[4,256,1536]{2,1,0:T(8,128)(2,1)}, bf16[4,256,2240]{2,1,0:T(8,128)(2,1)}, bf16[4,256,2240]{2,1,0:T(8,128)(2,1)}) custom-call(bf16[256,1536]{1,0:T(8,128)(2,1)} %get-tuple-element.120.grad_ref, bf16[4,256,2240]{2,1,0:T(8,128)(2,1)} %get-tuple-element.37.gate_ref, ...), custom_call_target="tpu_custom_call" | custom-call | flops 21139292160 | bytes 41943040 | tf_op jit(solution)/shard_map/ffn_backward/pallas_call | solution.py:422
  1236.2 11.7 pad_maximum_fusion
  1248.1 12.6 bitcast_convert_fusion.4
  1260.8 12.5 bitcast_convert_fusion.5
  1273.4 12.4 bitcast_convert_fusion.2
  1286.1 13.8 bitcast_convert_fusion.3
  1300.0 12.4 bitcast_convert_fusion
  1312.5 12.4 bitcast_convert_fusion.1
  1334.4 14.7 all-to-all-done.1
  1370.2 45.5 %psum.7 = f32[4,2,1280]{2,0,1:T(4,128)S(1)} all-reduce(f32[4,2,1280]{2,0,1:T(4,128)S(1)} %pad_maximum_fusion.18), channel_id=1, replica_groups=mesh['gx'=8,'gy'=4] {'gx','gy'}, use_global_device_ids=true, to_apply=%region_30.31 | all-reduce | flops 10240 | bytes 81920 | tf_op jit(solution)/shard_map/psum | solution.py:644
  1419.9 10.9 reduce-scatter.27.cloned.1.call-done
  1430.8 69.3 %reduce-scatter.25.cloned.1.call-done = bf16[192,2240]{1,0:T(8,128)(2,1)} async-done(((bf16[1536,2240]{1,0:T(8,128)(2,1)}), bf16[192,2240]{1,0:T(8,128)(2,1)}) %reduce-scatter.25.cloned.1.call-update) | async-done | bytes 860176 | tf_op jit(solution)/shard_map/reduce_scatter | solution.py:552
  1503.5 65.6 %reduce-scatter.31.cloned.1.call-done = bf16[192,2240]{1,0:T(8,128)(2,1)} async-done(((bf16[1536,2240]{1,0:T(8,128)(2,1)}), bf16[192,2240]{1,0:T(8,128)(2,1)}) %reduce-scatter.31.cloned.1.call-update) | async-done | bytes 860176 | tf_op jit(solution)/shard_map/reduce_scatter | solution.py:552
  1569.1 69.3 %reduce-scatter.29.cloned.1.call-done = bf16[192,2240]{1,0:T(8,128)(2,1)} async-done(((bf16[1536,2240]{1,0:T(8,128)(2,1)}), bf16[192,2240]{1,0:T(8,128)(2,1)}) %reduce-scatter.29.cloned.1.call-update) | async-done | bytes 860176 | tf_op jit(solution)/shard_map/reduce_scatter | solution.py:552
  1641.9 65.6 %reduce-scatter.35.cloned.1.call-done = bf16[192,2240]{1,0:T(8,128)(2,1)} async-done(((bf16[1536,2240]{1,0:T(8,128)(2,1)}), bf16[192,2240]{1,0:T(8,128)(2,1)}) %reduce-scatter.35.cloned.1.call-update) | async-done | bytes 860176 | tf_op jit(solution)/shard_map/reduce_scatter | solution.py:552
  1707.5 69.4 %reduce-scatter.33.cloned.1.call-done = bf16[192,2240]{1,0:T(8,128)(2,1)} async-done(((bf16[1536,2240]{1,0:T(8,128)(2,1)}), bf16[192,2240]{1,0:T(8,128)(2,1)}) %reduce-scatter.33.cloned.1.call-update) | async-done | bytes 860176 | tf_op jit(solution)/shard_map/reduce_scatter | solution.py:552
  1780.4 29.1 %reduce-scatter.23.cloned.1.call-done = bf16[1,192,896]{2,1,0:T(8,128)(2,1)} async-done(((bf16[4,192,896]{2,1,0:T(8,128)(2,1)}), bf16[1,192,896]{2,1,0:T(8,128)(2,1)}) %reduce-scatter.23.cloned.1.call-update) | async-done | bytes 344080 | tf_op jit(solution)/shard_map/reduce_scatter | solution.py:87
  1810.6 32.2 %reduce-scatter.19.cloned.1.call-done = bf16[1,192,896]{2,1,0:T(8,128)(2,1)} async-done(((bf16[4,192,896]{2,1,0:T(8,128)(2,1)}), bf16[1,192,896]{2,1,0:T(8,128)(2,1)}) %reduce-scatter.19.cloned.1.call-update) | async-done | bytes 344080 | tf_op jit(solution)/shard_map/reduce_scatter | solution.py:87
  (496 shorter events, 446.7 us)
Async XLA Ops:
  7.2 38.1 %all-gather.28.cloned.1.call-start = ((), (), s32[]{:S(2)}) async-start(), calls=%async_computation.30 | async-start | bytes 1720320 | tf_op jit(solution)/shard_map/all_gather | solution.py:69
  11.2 69.0 %all-gather.38.cloned.1.call-start = ((), (), s32[]{:S(2)}) async-start(), calls=%async_computation.35 | async-start | bytes 1720320 | tf_op jit(solution)/shard_map/all_gather | solution.py:69
  12.3 135.7 %all-gather.30.cloned.1.call-start = ((), (), s32[]{:S(2)}) async-start(), calls=%async_computation.31 | async-start | bytes 12386304 | tf_op jit(solution)/shard_map/all_gather | solution.py:70
  45.3 170.0 %all-gather.40.cloned.1.call-start = ((), (), s32[]{:S(2)}) async-start(), calls=%async_computation.36 | async-start | bytes 12386304 | tf_op jit(solution)/shard_map/all_gather | solution.py:70
  81.4 28.2 %all-to-all-start = ((bf16[384,4,256]{0,2,1:T(8,128)(2,1)}), bf16[384,4,256]{0,2,1:T(8,128)(2,1)S(1)}, u32[]{:S(2)}, u32[]{:S(2)}) async-start(bf16[384,4,256]{0,2,1:T(8,128)(2,1)} %bitcast), calls=%async_computation | async-start | bytes 1572864 | tf_op jit(solution)/shard_map/all_to_all | solution.py:482
  85.4 162.5 %all-gather.24.cloned.1.call-start = ((), (), s32[]{:S(2)}) async-start(), calls=%async_computation.16 | async-start | bytes 1310720 | tf_op jit(solution)/shard_map/all_gather | solution.py:505
  109.9 150.4 %copy-start.3 = (f32[4,32,8,384]{3,2,0,1:T(8,128)}, f32[4,32,8,384]{3,2,0,1:T(8,128)S(1)}, u32[]{:S(2)}) copy-start(f32[4,32,8,384]{3,2,0,1:T(8,128)S(1)} %copy.325) | copy-start | bytes 4718596
  110.3 127.6 %copy-start.5 = (bf16[256,1536]{1,0:T(8,128)(2,1)}, bf16[256,1536]{1,0:T(8,128)(2,1)S(1)}, u32[]{:S(2)}) copy-start(bf16[256,1536]{1,0:T(8,128)(2,1)S(1)} %multiply_convert_fusion.3) | copy-start | bytes 2359300
  165.3 131.7 %all-gather.32.cloned.1.call-start = ((), (), s32[]{:S(2)}) async-start(), calls=%async_computation.32 | async-start | bytes 7962624 | tf_op jit(solution)/shard_map/all_gather | solution.py:488
  168.1 179.6 %all-gather.34.cloned.1.call-start = ((), (), s32[]{:S(2)}) async-start(), calls=%async_computation.33 | async-start | bytes 7962624 | tf_op jit(solution)/shard_map/all_gather | solution.py:488
  171.0 227.6 %all-gather.36.cloned.1.call-start = ((), (), s32[]{:S(2)}) async-start(), calls=%async_computation.34 | async-start | bytes 7962624 | tf_op jit(solution)/shard_map/all_gather | solution.py:488
  173.8 406.0 %all-gather.26.cloned.1.call-start = ((), (), s32[]{:S(2)}) async-start(), calls=%async_computation.17 | async-start | bytes 1310720 | tf_op jit(solution)/shard_map/all_gather | solution.py:505
  174.2 330.3 %copy-start.73 = (f32[1536]{0:T(1024)}, f32[1536]{0:T(1024)S(1)}, u32[]{:S(2)}) copy-start(f32[1536]{0:T(1024)S(1)} %mul.459) | copy-start | bytes 18436
  264.4 238.3 %copy-start.80 = (f32[256]{0:T(256)}, f32[256]{0:T(256)S(1)}, u32[]{:S(2)}) copy-start(f32[256]{0:T(256)S(1)} %add_rsqrt_fusion.2) | copy-start | bytes 3076
  507.3 100.3 %all-gather.42.cloned.1.call-start = ((), (), s32[]{:S(2)}) async-start(), calls=%async_computation.37 | async-start | bytes 7962624 | tf_op jit(solution)/shard_map/all_gather | solution.py:488
  507.9 150.5 %all-gather.44.cloned.1.call-start = ((), (), s32[]{:S(2)}) async-start(), calls=%async_computation.38 | async-start | bytes 7962624 | tf_op jit(solution)/shard_map/all_gather | solution.py:488
  508.7 200.4 %all-gather.46.cloned.1.call-start = ((), (), s32[]{:S(2)}) async-start(), calls=%async_computation.39 | async-start | bytes 7962624 | tf_op jit(solution)/shard_map/all_gather | solution.py:488
  510.4 38.4 %all-to-all-start.2 = ((bf16[384,4,256]{0,2,1:T(8,128)(2,1)}), bf16[384,4,256]{0,2,1:T(8,128)(2,1)S(1)}, u32[]{:S(2)}, u32[]{:S(2)}) async-start(bf16[384,4,256]{0,2,1:T(8,128)(2,1)} %bitcast.61), calls=%async_computation.2 | async-start | bytes 1572864 | tf_op jit(solution)/shard_map/all_to_all | solution.py:490
  520.2 470.9 %reduce-scatter.13.cloned.1.call-start = ((), (), s32[]{:S(2)}) async-start(), calls=%async_computation.18 | async-start | bytes 1310720 | tf_op jit(solution)/shard_map/reduce_scatter | solution.py:606
  957.4 266.8 %reduce-scatter.15.cloned.1.call-start = ((), (), s32[]{:S(2)}) async-start(), calls=%async_computation.19 | async-start | bytes 1310720 | tf_op jit(solution)/shard_map/reduce_scatter | solution.py:606
  1139.4 194.6 %reduce-scatter.21.cloned.1.call-start = ((), (), s32[]{:S(2)}) async-start(), calls=%async_computation.22 | async-start | bytes 12386304 | tf_op jit(solution)/shard_map/reduce_scatter | solution.py:86
  1184.4 231.3 %reduce-scatter.17.cloned.1.call-start = ((), (), s32[]{:S(2)}) async-start(), calls=%async_computation.20 | async-start | bytes 12386304 | tf_op jit(solution)/shard_map/reduce_scatter | solution.py:86
  1247.9 182.9 %reduce-scatter.27.cloned.1.call-start = ((), (), s32[]{:S(2)}) async-start(), calls=%async_computation.25 | async-start | bytes 7962624 | tf_op jit(solution)/shard_map/reduce_scatter | solution.py:552
  1260.7 239.3 %reduce-scatter.25.cloned.1.call-start = ((), (), s32[]{:S(2)}) async-start(), calls=%async_computation.24 | async-start | bytes 7962624 | tf_op jit(solution)/shard_map/reduce_scatter | solution.py:552
  1273.3 295.8 %reduce-scatter.31.cloned.1.call-start = ((), (), s32[]{:S(2)}) async-start(), calls=%async_computation.27 | async-start | bytes 7962624 | tf_op jit(solution)/shard_map/reduce_scatter | solution.py:552
  1285.8 352.6 %reduce-scatter.29.cloned.1.call-start = ((), (), s32[]{:S(2)}) async-start(), calls=%async_computation.26 | async-start | bytes 7962624 | tf_op jit(solution)/shard_map/reduce_scatter | solution.py:552
  1300.0 407.5 %reduce-scatter.35.cloned.1.call-start = ((), (), s32[]{:S(2)}) async-start(), calls=%async_computation.29 | async-start | bytes 7962624 | tf_op jit(solution)/shard_map/reduce_scatter | solution.py:552
  1312.4 464.5 %reduce-scatter.33.cloned.1.call-start = ((), (), s32[]{:S(2)}) async-start(), calls=%async_computation.28 | async-start | bytes 7962624 | tf_op jit(solution)/shard_map/reduce_scatter | solution.py:552
  1326.9 22.2 %all-to-all-start.1 = ((bf16[4,384,256]{1,2,0:T(8,128)(2,1)}), bf16[4,384,256]{1,2,0:T(8,128)(2,1)S(1)}, u32[]{:S(2)}, u32[]{:S(2)}) async-start(bf16[4,384,256]{1,2,0:T(8,128)(2,1)} %bitcast.489), calls=%async_computation.1 | async-start | bytes 1572864 | tf_op jit(solution)/shard_map/all_to_all | solution.py:542
  1333.7 475.8 %reduce-scatter.23.cloned.1.call-start = ((), (), s32[]{:S(2)}) async-start(), calls=%async_computation.23 | async-start | bytes 1720320 | tf_op jit(solution)/shard_map/reduce_scatter | solution.py:87
  1361.4 55.6 %all-to-all-start.3 = ((bf16[4,384,256]{1,2,0:T(8,128)(2,1)}), bf16[4,384,256]{1,2,0:T(8,128)(2,1)}, u32[]{:S(2)}, u32[]{:S(2)}) async-start(bf16[4,384,256]{1,2,0:T(8,128)(2,1)} %bitcast.553), calls=%async_computation.5 | async-start | bytes 1572864 | tf_op jit(solution)/shard_map/all_to_all | solution.py:542
  1367.4 475.5 %reduce-scatter.19.cloned.1.call-start = ((), (), s32[]{:S(2)}) async-start(), calls=%async_computation.21 | async-start | bytes 1720320 | tf_op jit(solution)/shard_map/reduce_scatter | solution.py:87
  (101 other events, 1473.1 us)
Sparse Core Ops, SparseCore 0:
  11.3 33.9 all-gather.27
  47.4 32.7 all-gather.37
  82.1 65.8 all-gather.29
  149.7 65.4 all-gather.39
  217.2 26.2 all-gather.23
  245.9 51.0 all-gather.31
  298.9 48.8 all-gather.33
  349.6 48.8 all-gather.35
  507.5 50.1 all-gather.25
  560.0 47.5 all-gather.41
  609.5 48.8 all-gather.43
  660.1 48.8 all-gather.45
  957.6 33.5 reduce-scatter.12
  1139.5 30.8 reduce-scatter.14
  1184.5 89.7 reduce-scatter.20
  1277.7 83.9 reduce-scatter.16
  1365.1 65.6 reduce-scatter.26
  1434.6 65.4 reduce-scatter.24
  1503.6 65.4 reduce-scatter.30
  1572.9 65.4 reduce-scatter.28
  1641.9 65.4 reduce-scatter.34
  1711.4 65.4 reduce-scatter.32
  1779.2 30.2 reduce-scatter.22
  1811.7 31.0 reduce-scatter.18

commit v3 on v2

--- a/solution.py
+++ b/solution.py
@@ -1,3 +1,4 @@
+import functools
 import math
 
 import jax
@@ -21,7 +22,8 @@
 bf16 = jnp.bfloat16
 f32 = jnp.float32
 MESH = pl.DeviceIdType.MESH
-VMEM_LIMIT = 60 << 20
+VMEM_LIMIT = 62 << 20
+ANY = pl.BlockSpec(memory_space=pl.ANY)
 
 
 def rope_tables(positions, head_size):
@@ -63,11 +65,7 @@
     return scale * (scaled - normed * project), grad_gain
 
 
-def gather_attention(w_query, w_key, w_value, w_output):
-    sizes = (w_query.shape[1], w_key.shape[1], w_value.shape[1], w_output.shape[1])
-    pack = jnp.concatenate([w_query, w_key, w_value, w_output], axis=1)
-    pack = lax.all_gather(pack, "gy", axis=0)
-    pack = lax.all_gather(pack, "gx", axis=0)
+def unpack_attention(pack, sizes):
     full, start = [], 0
     for size in sizes:
         part = pack[..., start : start + size].transpose(0, 2, 1, 3)
@@ -113,7 +111,300 @@
     return lax.dot_general(left, right, (((1,), (1,)), ((), ())), preferred_element_type=f32)
 
 
-def line_pass(own_ref, sum_ref, gathered, part, own, outb, inb, sems, load, finish):
+def wait_for(ref, sem):
+    pltpu.make_async_copy(ref, ref, sem).wait()
+
+
+def places():
+    gx, devices = lax.axis_index("gx"), lax.axis_size("gx")
+    chips = devices // 2
+    chip, core = gx // 2, lax.rem(gx, 2)
+    partner = gx + 1 - 2 * core
+    others = [lax.rem(chip + k, chips) * 2 + core for k in range(1, chips)]
+    return partner, others
+
+
+def square():
+    gx = lax.axis_index("gx")
+    chip, core = gx // 2, lax.rem(gx, 2)
+    side = gx + 2 - 4 * lax.rem(chip, 2)
+    along = gx + 4 - 8 * (chip // 2)
+    return side, along, (3 - chip) * 2 + core
+
+
+def spread_slots():
+    chips = lax.axis_size("gx") // 2
+    return 14 if chips == 4 else 2 * chips + 2 * (chips - 1)
+
+
+def spread_scratch(count):
+    devices = lax.axis_size("gx")
+    return [
+        pltpu.SemaphoreType.DMA((count,)),
+        pltpu.SemaphoreType.DMA((count, spread_slots())),
+        pltpu.SemaphoreType.DMA((count, devices, 2)),
+    ]
+
+
+def greet(gx_peers, gy_peers):
+    gx, gy = lax.axis_index("gx"), lax.axis_index("gy")
+    barrier = pltpu.get_barrier_semaphore()
+    for peer in gx_peers:
+        pl.semaphore_signal(barrier, inc=1, device_id=(peer, gy), device_id_type=MESH)
+    for peer in gy_peers:
+        pl.semaphore_signal(barrier, inc=1, device_id=(gx, peer), device_id_type=MESH)
+    pl.semaphore_wait(barrier, len(gx_peers) + len(gy_peers))
+
+
+class Spread:
+    def __init__(self, items, sems):
+        self.items, (self.local, self.send_sem, self.recv_sem) = items, sems
+        self.partner, self.others = places()
+        self.four = lax.axis_size("gx") // 2 == 4
+        self.near = list(square()[:2]) if self.four else self.others
+
+    def part(self, i, k, h):
+        full = self.items[i][1]
+        half = full.shape[1] // 2
+        return full.at[k, pl.ds(h * half, half)]
+
+    def send(self, i, k, h, target, slot, first=False):
+        here = self.part(i, k, h)
+        half = here.shape[0]
+        source = self.items[i][0].at[pl.ds(h * half, half)] if first else here
+        pltpu.make_async_remote_copy(
+            src_ref=source,
+            dst_ref=here,
+            send_sem=self.send_sem.at[i, slot],
+            recv_sem=self.recv_sem.at[i, k, h],
+            device_id=(target, lax.axis_index("gy")),
+            device_id_type=MESH,
+        ).start()
+
+    def arrived(self, i, k, h):
+        wait_for(self.part(i, k, h), self.recv_sem.at[i, k, h])
+
+    def place(self, i):
+        own, full = self.items[i]
+        return pltpu.make_async_copy(own, full.at[lax.axis_index("gx")], self.local.at[i])
+
+    def begin(self, i):
+        gx = lax.axis_index("gx")
+        self.place(i).start()
+        slot = 0
+        for target in self.near + [self.partner]:
+            for h in range(2):
+                self.send(i, gx, h, target, slot, True)
+                slot += 1
+
+    def relay(self, i):
+        slot = 2 * len(self.near) + 2
+        if self.four:
+            side, along, _ = square()
+            steps = [(side, 0, along), (along, 1, side), (side, 1, None), (along, 0, None)]
+        else:
+            steps = [(k, h, None) for k in self.others for h in range(2)]
+        for k, h, target in steps:
+            self.arrived(i, k, h)
+            for to in [self.partner] if target is None else [target, self.partner]:
+                self.send(i, k, h, to, slot)
+                slot += 1
+
+    def finish(self, i):
+        if self.four:
+            for h in range(2):
+                self.arrived(i, square()[2], h)
+                self.send(i, square()[2], h, self.partner, 12 + h)
+
+    def close(self, i):
+        core = lax.rem(lax.axis_index("gx"), 2)
+        for k in [self.partner] + [k + 1 - 2 * core for k in self.others]:
+            for h in range(2):
+                self.arrived(i, k, h)
+        for slot in range(spread_slots()):
+            wait_for(self.part(i, 0, 0), self.send_sem.at[i, slot])
+        self.place(i).wait()
+
+
+def line_order(t, me, last):
+    short = jnp.minimum(me, last - me)
+    near = jnp.where(lax.rem(t, 2) == 0, me - t // 2, me + (t + 1) // 2)
+    far = jnp.where(me < last - me, me + (t - short), me - (t - short))
+    return jnp.where(t <= 2 * short, near, far)
+
+
+class Chain:
+    def __init__(self, own, full, sems):
+        self.own, self.full, (self.local, self.send_sem, self.recv_sem) = own, full, sems
+
+    def copy(self, b, way, first=False):
+        me = lax.axis_index("gy")
+        return pltpu.make_async_remote_copy(
+            src_ref=self.own if first else self.full.at[b],
+            dst_ref=self.full.at[b],
+            send_sem=self.send_sem.at[b, way],
+            recv_sem=self.recv_sem.at[b],
+            device_id=(lax.axis_index("gx"), me - 1 + 2 * way),
+            device_id_type=MESH,
+        )
+
+    def each(self, b, act, first=False):
+        me, last = lax.axis_index("gy"), lax.axis_size("gy") - 1
+
+        @pl.when(jnp.logical_and(b <= me, me < last))
+        def _():
+            act(self.copy(b, 1, first))
+
+        @pl.when(jnp.logical_and(b >= me, me > 0))
+        def _():
+            act(self.copy(b, 0, first))
+
+    def begin(self):
+        me = lax.axis_index("gy")
+        self.place = pltpu.make_async_copy(self.own, self.full.at[me], self.local)
+        self.place.start()
+        self.each(me, lambda copy: copy.start(), True)
+
+    def relay(self, t):
+        b = line_order(t, lax.axis_index("gy"), lax.axis_size("gy") - 1)
+        wait_for(self.full.at[b], self.recv_sem.at[b])
+        self.each(b, lambda copy: copy.start())
+
+    def close(self):
+        self.place.wait()
+        for b in range(lax.axis_size("gy")):
+            self.each(b, lambda copy: copy.wait_send())
+
+
+class Exchange:
+    def __init__(self, own, full, sems):
+        self.own, self.full, (self.local, self.send_sem, self.recv_sem) = own, full, sems
+
+    def begin(self):
+        gx, me, size = lax.axis_index("gx"), lax.axis_index("gy"), lax.axis_size("gy")
+        width = self.full.shape[2]
+
+        def columns(k):
+            return self.own.at[:, pl.ds(pl.multiple_of(k * width, width), width)]
+
+        self.place = pltpu.make_async_copy(columns(me), self.full.at[me], self.local)
+        self.place.start()
+        self.sent = []
+        for d in range(1, size):
+            target = lax.rem(me + d, size)
+            copy = pltpu.make_async_remote_copy(
+                src_ref=columns(target),
+                dst_ref=self.full.at[me],
+                send_sem=self.send_sem.at[d],
+                recv_sem=self.recv_sem.at[me],
+                device_id=(gx, target),
+                device_id_type=MESH,
+            )
+            copy.start()
+            self.sent.append(copy)
+
+    def close(self):
+        me, size = lax.axis_index("gy"), lax.axis_size("gy")
+        self.place.wait()
+        for copy in self.sent:
+            copy.wait_send()
+        for d in range(1, size):
+            k = lax.rem(me + d, size)
+            wait_for(self.full.at[k], self.recv_sem.at[k])
+
+
+def chain_scratch():
+    size = lax.axis_size("gy")
+    return [
+        pltpu.SemaphoreType.DMA,
+        pltpu.SemaphoreType.DMA((size, 2)),
+        pltpu.SemaphoreType.DMA((size,)),
+    ]
+
+
+def exchange_scratch():
+    size = lax.axis_size("gy")
+    return [
+        pltpu.SemaphoreType.DMA,
+        pltpu.SemaphoreType.DMA((size,)),
+        pltpu.SemaphoreType.DMA((size,)),
+    ]
+
+
+def opening_kernel(*refs):
+    ins, outs, sems = refs[:8], refs[8:17], refs[17:]
+    resid, cot, small, pack_a, pack_b, wg, wu, wd = ins
+    resid_out, cot_out, small_out, line_a, line_b, attn, gate, up, down = outs
+    me, size = lax.axis_index("gy"), lax.axis_size("gy")
+    partner, others = places()
+    near = list(square()[:2]) if lax.axis_size("gx") == 8 else others
+    chains = [
+        Chain(own, full, sems[3 * k : 3 * k + 3])
+        for k, (own, full) in enumerate(((pack_a, line_a), (pack_b, line_b), (small, small_out)))
+    ]
+    swaps = [
+        Exchange(own, full, sems[9 + 3 * k : 12 + 3 * k])
+        for k, (own, full) in enumerate(((resid, resid_out), (cot, cot_out)))
+    ]
+    spread = Spread(
+        [(line_a, attn), (wg.at[0], gate), (wu.at[0], up), (wd.at[0], down)], sems[15:18]
+    )
+    greet([partner] + near, [lax.rem(me + d, size) for d in range(1, size)])
+    chains[0].begin()
+    chains[2].begin()
+    spread.begin(1)
+    for t in range(1, size):
+        chains[0].relay(t)
+    chains[0].close()
+    spread.begin(0)
+    swaps[0].begin()
+    for t in range(1, size):
+        chains[2].relay(t)
+    spread.begin(2)
+    chains[1].begin()
+    spread.relay(1)
+    for t in range(1, size):
+        chains[1].relay(t)
+    spread.begin(3)
+    swaps[1].begin()
+    spread.relay(0)
+    spread.finish(1)
+    spread.relay(2)
+    spread.finish(0)
+    spread.relay(3)
+    spread.finish(2)
+    spread.finish(3)
+    for i in (1, 2, 3, 0):
+        spread.close(i)
+    for part in chains[1:] + swaps:
+        part.close()
+
+
+def opening(resid, cot, small, pack_a, pack_b, wg, wu, wd):
+    devices, size = lax.axis_size("gx"), lax.axis_size("gy")
+    count = resid.shape[1] // size
+
+    def shape(*dims, kind=bf16):
+        return jax.ShapeDtypeStruct(dims, kind)
+
+    blocks = shape(size, resid.shape[0], count)
+    line = shape(size, *pack_a.shape)
+    weight = shape(devices, *wg.shape[1:])
+    packed = shape(devices, size, *pack_a.shape)
+    out = [blocks, blocks, shape(size, *small.shape, kind=f32), line, line, packed] + [weight] * 3
+
+    return pl.pallas_call(
+        opening_kernel,
+        out_shape=out,
+        in_specs=[ANY] * 8,
+        out_specs=[ANY] * 9,
+        scratch_shapes=chain_scratch() * 3 + exchange_scratch() * 2 + spread_scratch(4),
+        compiler_params=pltpu.CompilerParams(collective_id=2, has_side_effects=True),
+        name="opening",
+    )(resid, cot, small, pack_a, pack_b, wg, wu, wd)
+
+
+def line_pass(own_ref, own, gathered, part, outb, inb, sems, load, finish, peers=(), plan={}):
     own_sem, ag_send, ag_recv, rs_send, rs_recv = sems
     gx, me, size = lax.axis_index("gx"), lax.axis_index("gy"), lax.axis_size("gy")
     rows = own.shape[0]
@@ -133,8 +424,16 @@
     def _():
         pl.semaphore_signal(barrier, inc=1, device_id=(gx, me + 1), device_id_type=MESH)
 
-    pl.semaphore_wait(barrier, jnp.where(inner, 2, 1))
+    for peer in peers:
+        pl.semaphore_signal(barrier, inc=1, device_id=(peer, me), device_id_type=MESH)
+    pl.semaphore_wait(barrier, jnp.where(inner, 2, 1) + len(peers))
     first.wait()
+
+    def planned(name, t):
+        for (key, when), act in plan.items():
+            if key == name:
+                pl.when(t == when)(act)
+
 
     def gather_copy(b, s, way):
         here = gathered.at[b, pl.ds(s * piece, piece)]
@@ -164,11 +463,7 @@
         pltpu.make_async_copy(here, here, rs_recv.at[slot, s]).wait()
 
     def step(t, carry):
-        short = jnp.minimum(me, last - me)
-        even = lax.rem(t, 2) == 0
-        near = jnp.where(even, me - t // 2, me + (t + 1) // 2)
-        far = jnp.where(me < last - me, me + (t - short), me - (t - short))
-        b = jnp.where(t <= 2 * short, near, far)
+        b = line_order(t, me, last)
         for s in range(PIECES):
 
             @pl.when(t > 0)
@@ -187,6 +482,7 @@
         def _():
             load()
 
+        planned("step", t)
         finish(b)
 
         @pl.when(b == me)
@@ -211,6 +507,7 @@
         low = jnp.where(t < above, me + 1 + t, me - 1 - (t - above))
         high = jnp.where(t < below, me - 1 - t, me + 1 + (t - below))
         b = jnp.where(2 * me < size, low, high)
+        planned("hop", t)
 
         @pl.when(inner)
         def _():
@@ -236,8 +533,6 @@
             sum_arrived(size, s)
         own[...] += inb[size].astype(f32)
 
-    sum_ref[...] = own[...]
-
     def drain(b, carry):
         for s in range(PIECES):
 
@@ -261,7 +556,6 @@
 def line_scratch(size, rows, width):
     return [
         pltpu.VMEM((size, rows, width), bf16),
-        pltpu.VMEM((rows, width), f32),
         pltpu.VMEM((rows, width), f32),
         pltpu.VMEM((size, rows, width), bf16),
         pltpu.VMEM((size + 1, rows, width), bf16),
@@ -273,15 +567,47 @@
     ]
 
 
-LINE = 10
-
-
-def forward_kernel(
-    acts_ref, wg_ref, wu_ref, wd_ref, sum_ref, full_ref, gate_ref, up_ref, hidden_ref, *scratch
-):
-    gathered, part, own, outb, inb = scratch[:5]
-    sems = scratch[5:LINE]
-    wg, wu, wd, gate, up, hidden, w_sem, out_sem = scratch[LINE:]
+LINE = 9
+
+
+ORDER = {
+    ("step", 0): "b0",
+    ("step", 2): "b1",
+    ("hop", 0): "r0 r1 b2",
+    ("hop", 1): "f0 f1 b3",
+}
+REST = "r2 r3 f2 f3 c0 c1 c2 c3"
+VERBS = {"b": "begin", "r": "relay", "f": "finish", "c": "close"}
+
+
+def schedule(spread, size):
+    def run(text):
+        def act():
+            for word in text.split():
+                getattr(spread, VERBS[word[0]])(int(word[1]))
+
+        return act
+
+    plan = {key: run(text) for key, text in ORDER.items()}
+    return plan, [(VERBS[word[0]], int(word[1])) for word in REST.split()]
+
+
+def forward_kernel(extra, *refs):
+    acts_ref, wg_ref, wu_ref, wd_ref = refs[:4]
+    shards, refs = refs[4 : 4 + extra], refs[4 + extra :]
+    sum_ref, turned_ref, gate_ref, up_ref, hidden_ref = refs[:5]
+    wholes, scratch = refs[5 : 5 + extra], refs[5 + extra :]
+    gathered, part, outb, inb = scratch[:4]
+    sems = scratch[4:LINE]
+    wg, wu, wd, gate, up, hidden, turned, w_sem, out_sem = scratch[LINE : LINE + 9]
+    peers, spread = [], None
+    if extra:
+        items = [(r if r.shape == w.shape[1:] else r.at[1], w) for r, w in zip(shards, wholes)]
+        spread = Spread(items, scratch[LINE + 9 :])
+        partner, others = places()
+        peers = [partner] + (list(square()[:2]) if spread.four else others)
+
+    plan, rest = schedule(spread, lax.axis_size("gy")) if extra else ({}, ())
     loads = [
         pltpu.make_async_copy(src, dst, w_sem.at[k])
         for k, (src, dst) in enumerate(((wg_ref, wg), (wu_ref, wu), (wd_ref, wd)))
@@ -294,7 +620,7 @@
             copy.wait()
 
     def results(b):
-        pairs = ((gathered, full_ref), (gate, gate_ref), (up, up_ref), (hidden, hidden_ref))
+        pairs = ((gate, gate_ref), (up, up_ref), (hidden, hidden_ref))
         return [
             pltpu.make_async_copy(src.at[b], dst.at[b], out_sem.at[b, k])
             for k, (src, dst) in enumerate(pairs)
@@ -302,6 +628,7 @@
 
     def finish(b):
         block = gathered[b]
+        store_turned(block, turned, b)
         for start, width in spans(wg.shape[1]):
             at = slice(start, start + width)
             g = nn(block, wg[:, at])
@@ -318,7 +645,13 @@
         for copy in results(b):
             copy.start()
 
-    line_pass(acts_ref, sum_ref, gathered, part, own, outb, inb, sems, load, finish)
+    line_pass(
+        acts_ref, sum_ref, gathered, part, outb, inb, sems, load, finish, peers, plan
+    )
+    keep = pltpu.make_async_copy(turned, turned_ref, w_sem.at[0])
+    keep.start()
+    for act, i in rest:
+        getattr(spread, act)(i)
 
     def settle(b, carry):
         for copy in results(b):
@@ -326,47 +659,244 @@
         return carry
 
     lax.fori_loop(0, gathered.shape[0], settle, 0)
-
-
-ANY = pl.BlockSpec(memory_space=pl.ANY)
-
-
-def forward_ffn(acts, wg, wu, wd):
+    keep.wait()
+
+
+def forward_ffn(acts, wg, wu, wd, shards=()):
     rows, width = acts.shape
-    size, hidden = lax.axis_size("gy"), wg.shape[1]
+    devices, size, hidden = lax.axis_size("gx"), lax.axis_size("gy"), wg.shape[1]
     wide = jax.ShapeDtypeStruct((size, rows, hidden), bf16)
+    extra = len(shards)
+    wholes = [
+        jax.ShapeDtypeStruct((devices,) + (s.shape if k == 0 else s.shape[1:]), bf16)
+        for k, s in enumerate(shards)
+    ]
     return pl.pallas_call(
-        forward_kernel,
+        functools.partial(forward_kernel, extra),
         out_shape=[
             jax.ShapeDtypeStruct((rows, width), f32),
-            jax.ShapeDtypeStruct((size, rows, width), bf16),
+            jax.ShapeDtypeStruct((2, width // 2, size * rows), bf16),
             wide,
             wide,
             wide,
-        ],
-        in_specs=[ANY] * 4,
-        out_specs=[pl.BlockSpec(memory_space=pltpu.VMEM)] + [ANY] * 4,
+        ]
+        + wholes,
+        in_specs=[ANY] * (4 + extra),
+        out_specs=[pl.BlockSpec(memory_space=pltpu.VMEM)] + [ANY] * (4 + extra),
         scratch_shapes=line_scratch(size, rows, width)
         + [pltpu.VMEM((width, hidden), bf16)] * 3
         + [pltpu.VMEM((size, rows, hidden), bf16)] * 3
-        + [pltpu.SemaphoreType.DMA((3,)), pltpu.SemaphoreType.DMA((size, 4))],
+        + [pltpu.VMEM((2, width // 2, size * rows), bf16)]
+        + [pltpu.SemaphoreType.DMA((3,)), pltpu.SemaphoreType.DMA((size, 3))]
+        + (spread_scratch(extra) if extra else []),
         compiler_params=pltpu.CompilerParams(
-            collective_id=0, has_side_effects=True, vmem_limit_bytes=VMEM_LIMIT
+            collective_id=3 if extra else 0, has_side_effects=True, vmem_limit_bytes=VMEM_LIMIT
         ),
         cost_estimate=pl.CostEstimate(
             flops=6 * size * rows * width * hidden, bytes_accessed=40 << 20, transcendentals=0
         ),
         name="ffn_forward",
-    )(acts, wg, wu, wd)
+    )(acts, wg, wu, wd, *shards)
+
+
+class Reduce:
+    def __init__(self, lhs, rhs, bufs, abuf, fbuf, ftail, a_all, r_all, c_all, outs, sems):
+        self.lhs, self.rhs, self.bufs, self.outs = lhs, rhs, bufs, outs
+        self.abuf, self.fbuf, self.ftail = abuf, fbuf, ftail
+        self.a_all, self.r_all, self.c_all = a_all, r_all, c_all
+        (
+            self.a_send,
+            self.a_recv,
+            self.r_send,
+            self.r_recv,
+            self.c_send,
+            self.c_recv,
+            self.local,
+        ) = sems
+        gx, self.gy = lax.axis_index("gx"), lax.axis_index("gy")
+        self.chip, self.core = gx // 2, lax.rem(gx, 2)
+        self.chips = lax.axis_size("gx") // 2
+        self.half, self.wide = bufs[0].shape[0] // 2, bufs[0].shape[1]
+        self.r = self.half // self.chips
+        self.four = self.chips == 4
+        self.partner, self.others = places()
+        self.near = list(square()[:2]) if self.four else self.others
+
+    def product(self, m, which, at):
+        z, n, _ = self.rhs[m].shape
+        right = self.rhs[m][:, :, at].reshape(z * n, at.stop - at.start)
+        return nn(self.lhs[which], right)
+
+    def remote(self, src, dst, send, recv, target):
+        return pltpu.make_async_remote_copy(
+            src_ref=src,
+            dst_ref=dst,
+            send_sem=send,
+            recv_sem=recv,
+            device_id=(target, self.gy),
+            device_id_type=MESH,
+        )
+
+    def columns(self):
+        return [(j, slice(s, s + w)) for j, (s, w) in enumerate(spans(self.wide))]
+
+    def swap(self, m, j, at):
+        here = (slice(0, self.half), at)
+        return self.remote(
+            self.bufs[m].at[here],
+            self.a_all.at[m, :, at],
+            self.a_send.at[m, j],
+            self.a_recv.at[m, j],
+            self.partner,
+        )
+
+    def block(self, m, device, start=0, size=None):
+        size = self.r if size is None else size
+        first = self.half + (device // 2) * self.r + start
+        return self.bufs[m].at[pl.ds(pl.multiple_of(first, 16), size)]
+
+    def first(self, m):
+        for j, at in self.columns():
+            self.bufs[m][: self.half, at] = self.product(m, 1 - self.core, at).astype(bf16)
+            self.swap(m, j, at).start()
+
+    def corner(self, m, h):
+        side, along, across = square()
+        half = self.r // 2
+        return self.remote(
+            self.block(m, across, h * half, half),
+            self.r_all.at[m, h],
+            self.r_send.at[m, h],
+            self.r_recv.at[m, h],
+            along if h else side,
+        )
+
+    def second(self, m):
+        for j, at in self.columns():
+            self.swap(m, j, at).wait_recv()
+            landed = self.abuf.at[:, at]
+            fetch = pltpu.make_async_copy(self.a_all.at[m, :, at], landed, self.local.at[0])
+            fetch.start()
+            mine = self.product(m, self.core, at)
+            fetch.wait()
+            self.bufs[m][self.half :, at] = (mine + landed[...].astype(f32)).astype(bf16)
+        if self.four:
+            for h in range(2):
+                self.corner(m, h).start()
+
+    def hand(self, m, k):
+        target = self.near[k]
+        return self.remote(
+            self.block(m, target),
+            self.c_all.at[m, k],
+            self.c_send.at[m, k],
+            self.c_recv.at[m, k],
+            target,
+        )
+
+    def third(self, m):
+        if self.four:
+            side, along, _ = square()
+            half = self.r // 2
+            for h, device in ((0, along), (1, side)):
+                self.corner(m, h).wait_recv()
+                here = self.block(m, device, h * half, half)
+                landed = self.abuf.at[h * half : (h + 1) * half]
+                fetch = pltpu.make_async_copy(self.r_all.at[m, h], landed, self.local.at[0])
+                fetch.start()
+                fetch.wait()
+                here[...] = (here[...].astype(f32) + landed[...].astype(f32)).astype(bf16)
+        for k in range(len(self.near)):
+            self.hand(m, k).start()
+
+    def fourth(self, m):
+        for j, at in self.columns():
+            self.swap(m, j, at).wait_send()
+        fetches = []
+        for k in range(len(self.near)):
+            self.hand(m, k).wait_recv()
+            here = self.bufs[m].at[pl.ds(k * self.r, self.r)]
+            fetch = pltpu.make_async_copy(self.c_all.at[m, k], here, self.local.at[k])
+            fetch.start()
+            fetches.append(fetch)
+        for fetch in fetches:
+            fetch.wait()
+        first = pl.multiple_of(self.half + self.chip * self.r, 16)
+        for _, at in self.columns():
+            total = self.bufs[m][pl.ds(first, self.r), at].astype(f32)
+            for k in range(len(self.near)):
+                total = total + self.bufs[m][k * self.r : (k + 1) * self.r, at].astype(f32)
+            stage = self.fbuf if total.shape[1] == FF_CHUNK else self.ftail
+            stage[...] = total
+            store = pltpu.make_async_copy(stage, self.outs[m].at[:, at], self.local.at[0])
+            store.start()
+            store.wait()
+
+    def drain(self, m):
+        if self.four:
+            for h in range(2):
+                self.corner(m, h).wait_send()
+        for k in range(len(self.near)):
+            self.hand(m, k).wait_send()
+
+
+def reduce_scratch(width, hidden, count=3):
+    devices = lax.axis_size("gx")
+    rows, parts = width // devices, len(spans(hidden))
+    near = 2 if devices == 8 else devices // 2 - 1
+    dma = pltpu.SemaphoreType.DMA
+    return [
+        pltpu.VMEM((width // 2, hidden), bf16),
+        pltpu.VMEM((rows, FF_CHUNK), f32),
+        pltpu.VMEM((rows, hidden % FF_CHUNK), f32),
+        dma((count, parts)),
+        dma((count, parts)),
+        dma((count, 2)),
+        dma((count, 2)),
+        dma((count, near)),
+        dma((count, near)),
+        dma((near,)),
+    ]
+
+
+def store_turned(block, turned, b):
+    count, width = block.shape
+    _, chips_rows, _ = turned.shape
+    devices = lax.axis_size("gx")
+    r = width // devices
+    flipped = block.T
+    at = pl.ds(pl.multiple_of(b * count, count), count)
+    for k in range(devices):
+        q = k // 2
+        turned[k % 2, q * r : (q + 1) * r, at] = flipped[k * r : (k + 1) * r]
+
+
+AFTER = (
+    ("hop", 0, "first", 0),
+    ("hop", 1, "second", 0),
+    ("hop", 1, "first", 1),
+    ("hop", 2, "third", 0),
+    ("hop", 2, "second", 1),
+)
 
 
 def backward_kernel(
-    grad_ref, gate_ref, up_ref, wg_ref, wu_ref, wd_ref, sum_ref, full_ref, dg_ref, du_ref, *scratch
+    grad_ref, gate_ref, up_ref, hidden_ref, turned_ref, wg_ref, wu_ref, wd_ref, *refs
 ):
-    gathered, part, own, outb, inb = scratch[:5]
-    sems = scratch[5:LINE]
-    wg, wu, wd, gate, up, w_sem, out_sem = scratch[LINE:]
-    operands = ((wd_ref, wd), (gate_ref, gate), (up_ref, up), (wg_ref, wg), (wu_ref, wu))
+    sum_ref, og, ou, od, a_all, r_all, c_all = refs[:7]
+    scratch = refs[7:]
+    gathered, part, outb, inb = scratch[:4]
+    sems = scratch[4:LINE]
+    wg, wu, wd, gate, up, hidden, turned, w_sem = scratch[LINE : LINE + 8]
+    abuf, fbuf, ftail = scratch[LINE + 8 : LINE + 11]
+    operands = (
+        (wd_ref, wd),
+        (gate_ref, gate),
+        (up_ref, up),
+        (wg_ref, wg),
+        (wu_ref, wu),
+        (hidden_ref, hidden),
+    )
     loads = [
         pltpu.make_async_copy(src, dst, w_sem.at[k]) for k, (src, dst) in enumerate(operands)
     ]
@@ -377,15 +907,23 @@
         for copy in loads:
             copy.wait()
 
-    def results(b):
-        pairs = ((gathered, full_ref), (gate, dg_ref), (up, du_ref))
-        return [
-            pltpu.make_async_copy(src.at[b], dst.at[b], out_sem.at[b, k])
-            for k, (src, dst) in enumerate(pairs)
-        ]
+    reduce = Reduce(
+        turned,
+        (hidden, gate, up),
+        (wd, wg, wu),
+        abuf,
+        fbuf,
+        ftail,
+        a_all,
+        r_all,
+        c_all,
+        (od, og, ou),
+        scratch[LINE + 11 :],
+    )
 
     def finish(b):
         block = gathered[b]
+        store_turned(block, turned, b)
         for start, width in spans(wg.shape[1]):
             at = slice(start, start + width)
             d = nn(block, wd[:, at])
@@ -402,45 +940,67 @@
                 part[...] = p
             else:
                 part[...] += p
-        for copy in results(b):
-            copy.start()
-
-    line_pass(grad_ref, sum_ref, gathered, part, own, outb, inb, sems, load, finish)
-
-    def settle(b, carry):
-        for copy in results(b):
-            copy.wait()
-        return carry
-
-    lax.fori_loop(0, gathered.shape[0], settle, 0)
-
-
-def backward_ffn(grad, gate, up, wg, wu, wd):
+
+    def swap_operand():
+        copy = pltpu.make_async_copy(turned_ref, turned, w_sem.at[0])
+        copy.start()
+        copy.wait()
+
+    def work(when):
+        def act():
+            for name, t, verb, m in AFTER:
+                if t == when:
+                    getattr(reduce, verb)(m)
+                    if verb == "second" and m == 0:
+                        swap_operand()
+
+        return act
+
+    peers = [reduce.partner] + reduce.near
+    plan = {("hop", t): work(t) for t in range(3)}
+    line_pass(grad_ref, sum_ref, gathered, part, outb, inb, sems, load, finish, peers, plan)
+    reduce.first(2)
+    reduce.third(1)
+    reduce.second(2)
+    reduce.fourth(0)
+    reduce.third(2)
+    reduce.fourth(1)
+    reduce.fourth(2)
+    for m in range(3):
+        reduce.drain(m)
+
+
+def backward_ffn(grad, gate, up, hidden, turned, wg, wu, wd):
     rows, width = grad.shape
-    size, hidden = lax.axis_size("gy"), wg.shape[1]
-    wide = jax.ShapeDtypeStruct((size, rows, hidden), bf16)
+    devices, size, wide = lax.axis_size("gx"), lax.axis_size("gy"), wg.shape[1]
+    near = 2 if devices == 8 else devices // 2 - 1
+    mine = jax.ShapeDtypeStruct((width // devices, wide), f32)
     return pl.pallas_call(
         backward_kernel,
         out_shape=[
             jax.ShapeDtypeStruct((rows, width), f32),
-            jax.ShapeDtypeStruct((size, rows, width), bf16),
-            wide,
-            wide,
+            mine,
+            mine,
+            mine,
+            jax.ShapeDtypeStruct((3, width // 2, wide), bf16),
+            jax.ShapeDtypeStruct((3, 2, width // devices // 2, wide), bf16),
+            jax.ShapeDtypeStruct((3, near, width // devices, wide), bf16),
         ],
-        in_specs=[ANY] * 6,
-        out_specs=[pl.BlockSpec(memory_space=pltpu.VMEM)] + [ANY] * 3,
+        in_specs=[ANY] * 8,
+        out_specs=[pl.BlockSpec(memory_space=pltpu.VMEM)] + [ANY] * 6,
         scratch_shapes=line_scratch(size, rows, width)
-        + [pltpu.VMEM((width, hidden), bf16)] * 3
-        + [pltpu.VMEM((size, rows, hidden), bf16)] * 2
-        + [pltpu.SemaphoreType.DMA((5,)), pltpu.SemaphoreType.DMA((size, 3))],
+        + [pltpu.VMEM((width, wide), bf16)] * 3
+        + [pltpu.VMEM((size, rows, wide), bf16)] * 3
+        + [pltpu.VMEM((2, width // 2, size * rows), bf16), pltpu.SemaphoreType.DMA((6,))]
+        + reduce_scratch(width, wide),
         compiler_params=pltpu.CompilerParams(
             collective_id=1, has_side_effects=True, vmem_limit_bytes=VMEM_LIMIT
         ),
         cost_estimate=pl.CostEstimate(
-            flops=6 * size * rows * width * hidden, bytes_accessed=40 << 20, transcendentals=0
+            flops=12 * size * rows * width * wide, bytes_accessed=40 << 20, transcendentals=0
         ),
         name="ffn_backward",
-    )(grad, gate, up, wg, wu, wd)
+    )(grad, gate, up, hidden, turned, wg, wu, wd)
 
 
 def on_device(
@@ -472,22 +1032,25 @@
 
     small = jnp.concatenate([gain_attn, gain_ffn, b_query, b_key, b_value], axis=1)
     small_sizes = [v.shape[1] for v in (gain_attn, gain_ffn, b_query, b_key, b_value)]
-    small = lax.all_gather(small, "gy", axis=1).astype(f32)
+    small = jnp.pad(small.astype(f32), ((0, 8 - LAYERS), (0, 0)))
+    packs = [
+        jnp.concatenate([w[l] for w in (w_query, w_key, w_value, w_output)], axis=1)
+        for l in range(LAYERS)
+    ]
+    pack_sizes = [w.shape[2] for w in (w_query, w_key, w_value, w_output)]
+    opened = opening(residual_in, cotangent, small, *packs, w_gate, w_up, w_down)
+    resid, cot, small, _, line_next, attn_pack = opened[:6]
+    ffn_full = [[w.reshape(D, -1) for w in opened[6:]], None]
+    small = small[:, :LAYERS].transpose(1, 0, 2)
     vectors, start = [], 0
     for size in small_sizes:
         vectors.append(small[:, :, start : start + size].reshape(LAYERS, -1))
         start += size
     gains_one, gains_two, bias_q, bias_k, bias_v = vectors
 
-    resid = lax.all_to_all(residual_in, "gy", split_axis=1, concat_axis=0, tiled=True)
-    resid = resid.astype(f32).T
-    attn_full, ffn_full = [], []
-    for l in range(LAYERS):
-        attn_full.append(gather_attention(w_query[l], w_key[l], w_value[l], w_output[l]))
-        ffn_full.append(
-            tuple(lax.all_gather(w[l], "gx", axis=0, tiled=True) for w in (w_gate, w_up, w_down))
-        )
-    cot = lax.all_to_all(cotangent, "gy", split_axis=1, concat_axis=0, tiled=True)
+    resid = resid.reshape(D, count).astype(f32).T
+    cot = cot.reshape(D, count)
+    attn_full = [unpack_attention(attn_pack, pack_sizes), None]
 
     kept = []
     for l in range(LAYERS):
@@ -516,7 +1079,14 @@
         middle = resid + dot("tq,dq->td", mixed, wo)
         normed_two, scale_two = rms_parts(middle)
         acts_two = (normed_two * gains_two[l]).astype(bf16)
-        part, acts_two, gate, up, hidden = forward_ffn(acts_two, wg, wu, wd)
+        if l == 0:
+            shards = (line_next, w_gate, w_up, w_down)
+            done = forward_ffn(acts_two, wg, wu, wd, shards)
+            attn_full[1] = unpack_attention(done[5], pack_sizes)
+            ffn_full[1] = [w.reshape(D, -1) for w in done[6:]]
+        else:
+            done = forward_ffn(acts_two, wg, wu, wd)
+        part, acts_two, gate, up, hidden = done[:5]
         kept.append(
             (
                 normed_one,
@@ -548,11 +1118,6 @@
     ffn_grads = [None] * LAYERS
     small_grads = [None] * LAYERS
 
-    def scatter_x(weight_grad):
-        return lax.psum_scatter(
-            weight_grad.astype(bf16), "gx", scatter_dimension=0, tiled=True
-        ).astype(f32)
-
     for l in reversed(range(LAYERS)):
         (
             normed_one,
@@ -572,14 +1137,8 @@
         ) = kept[l]
         wq, wk, wv, wo = attn_full[l]
         wg, wu, wd = ffn_full[l]
-        grad_acts_two, grad_out, grad_gate, grad_up = backward_ffn(
-            grad.astype(bf16), gate, up, wg, wu, wd
-        )
-        ffn_grads[l] = (
-            scatter_x(dot("ztd,ztf->df", acts_two, grad_gate)),
-            scatter_x(dot("ztd,ztf->df", acts_two, grad_up)),
-            scatter_x(dot("ztd,ztf->df", grad_out, hidden)),
-        )
+        done = backward_ffn(grad.astype(bf16), gate, up, hidden, acts_two, wg, wu, wd)
+        grad_acts_two, ffn_grads[l] = done[0], done[1:4]
         grad_norm, grad_gain_two = norm_backward(
             grad_acts_two, normed_two, scale_two, gains_two[l]
         )

time: 1870 us -> 1420 us (0.76)
  waiting for transfers between devices: 836 us -> 115 us
  Pallas kernels: 415 us -> 767 us
  matrix products: 182 us -> 109 us
    all_gather x10 -> x0, waiting for transfers between devices: 375 us -> none  [the longest x6 242 us: on_device(): lax.all_gather(w[l], 'gx', axis=0, tiled=True)]
    reduce_scatter x6 -> x0, waiting for transfers between devices: 350 us -> none  [scatter_x(): lax.psum_scatter(weight_grad.astype(bf16), 'gx', scatter_dimension=0, til...]
    pallas_call x2 -> x3, Pallas kernels: 208 us -> 418 us  [the longest x2 257 us: forward_ffn(): pl.pallas_call(functools.partial(forward_kernel, extra), out_shape=[jax.S...]
    pallas_call x2, Pallas kernels: 207 us -> 350 us  [backward_ffn(): pl.pallas_call(backward_kernel, out_shape=[jax.ShapeDtypeStruct((rows, wi...]
    reduce_scatter x2, waiting for transfers between devices: 0.04 us -> 73.7 us  [scatter_attention(): pack = lax.psum_scatter(pack, 'gx', scatter_dimension=0)]
    dot_general x42 -> x36, matrix products: 182 us -> 109 us  [dot(): return jnp.einsum(pattern, left, right, preferred_element_type=f32)]
    reduce_scatter x2, waiting for transfers between devices: 61.3 us -> 11.8 us  [scatter_attention(): pack = lax.psum_scatter(pack, 'gy', scatter_dimension=0).astype(f32)]
    all_to_all x2 -> x0, waiting for transfers between devices: 28.3 us -> none  [the longest x1 28.3 us: on_device(): lax.all_to_all(cotangent, 'gy', split_axis=1, concat_axis=0, tiled=True)]
  transfers between devices with their start and end apart: 28 -> 10, of which waited for: 21 -> 5; matrix products, arithmetic and copies ran while one was open for 20% -> 17% of each run, Pallas kernels for 0% -> 0%
where the time goes in v3:
time: 1420 us; the launch traced here: 1410 us
  Pallas kernels  767 us (54%)
  local copies, waits for them, and re-layouts  219 us (15%)
  waiting for transfers between devices  115 us (8%)
  other arithmetic  110 us (8%)
  matrix products  109 us (8%)
  blocking collectives  53.2 us (4%)
  starting transfers between devices  21.2 us (1%)
  between operations  15.9 us (1%)
    pallas_call x2, Pallas kernels, backward_ffn(): pl.pallas_call(backward_kernel, out_shape=[jax.ShapeDtypeStruct((rows, wi...  350 us
    pallas_call x2, Pallas kernels, forward_ffn(): pl.pallas_call(functools.partial(forward_kernel, extra), out_shape=[jax.S...  257 us
    pallas_call x1, Pallas kernels, opening(): pl.pallas_call(opening_kernel, out_shape=out, in_specs=[ANY] * 8, out_spe...  161 us
    dot_general x36, matrix products, dot(): return jnp.einsum(pattern, left, right, preferred_element_type=f32)  109 us
    reduce_scatter x2, waiting for transfers between devices, scatter_attention(): pack = lax.psum_scatter(pack, 'gx', scatter_dimension=0)  73.7 us
    reshape x12, local copies, waits for them, and re-layouts, scatter_attention(): grad.reshape(devices_x, D // devices_x, devices_y, -1).transpose(0, 2, 1, 3)  65 us
    transpose x12, local copies, waits for them, and re-layouts, unpack_attention(): part = pack[..., start:start + size].transpose(0, 2, 1, 3)  53.6 us
    psum x1, blocking collectives, on_device(): small = lax.psum(small, ('gx', 'gy'))  53.2 us
  transfers between devices with their start and end apart: 10, of which 5 were waited for; matrix products, arithmetic and copies ran while one was open for 17% of the time, Pallas kernels for 0%

profile of v3, /device:TPU:9, one launch (start us, length us, event | category | flops | bytes accessed | tf_op | source)
XLA Modules:
  0.0 1410.5 jit_solution(14890984111947280232)
XLA Ops:
  14.3 161.1 %opening.1 = (bf16[4,384,256]{2,1,0:T(8,128)(2,1)}, bf16[4,384,256]{2,1,0:T(8,128)(2,1)}, f32[4,8,1280]{2,1,0:T(8,128)}, bf16[4,192,896]{2,1,0:T(8,128)(2,1)}, b...) custom-call(bf16[384,1024]{1,0:T(8,128)(2,1)} %refs_0_.1, ...), custom_call_target="tpu_custom_call" | custom-call | tf_op jit(solution)/shard_map/opening/pallas_call | solution.py:396
  199.5 8.8 slice_bitcast_fusion.2
  214.6 6.2 copy.135
  256.9 145.4 %ffn_forward.2 = (f32[256,1536]{1,0:T(8,128)}, bf16[2,768,1024]{2,1,0:T(8,128)(2,1)}, bf16[4,256,2240]{2,1,0:T(8,128)(2,1)}, bf16[4,256,2240]{2,1,0:T(8,128)(2,1...) custom-call(bf16[256,1536]{1,0:T(8,128)(2,1)} %multiply_convert_fusi, ...), custom_call_target="tpu_custom_call" | custom-call | flops 21139292160 | bytes 41943040 | tf_op jit(solution)/shard_map/ffn_forward/pallas_call | solution.py:674
  424.6 7.0 slice_bitcast_fusion
  431.6 6.0 copy.144
  456.5 9.5 all-gather.5.cloned.1.call-done
  484.4 111.4 %ffn_forward.3 = (f32[256,1536]{1,0:T(8,128)}, bf16[2,768,1024]{2,1,0:T(8,128)(2,1)}, bf16[4,256,2240]{2,1,0:T(8,128)(2,1)}, bf16[4,256,2240]{2,1,0:T(8,128)(2,1)}, bf16[4,256,2240]{2,1,0:T(8,128)(2,1)}) custom-call(bf16[256,1536]{1,0:T(8,128)(2,1)} %multiply_convert_fusion.refs_0_, bf16[1536,2240]{1,0:T(8,128)(2,1)} %bitcast.557, ...), custom_call_target="tpu_custom_call" | custom-call | flops 21139292160 | bytes 41943040 | tf_op jit(solution)/shard_map/ffn_forward/pallas_call | solution.py:674
  599.5 173.8 %ffn_backward.2 = (f32[256,1536]{1,0:T(8,128)}, f32[192,2240]{1,0:T(8,128)}, f32[192,2240]{1,0:T(8,128)}, f32[192,2240]{1,0:T(8,128)}, bf16[3,768,2240]{2,1,0:T(...) custom-call(bf16[256,1536]{1,0:T(8,128)(2,1)} %fusion.56.grad_ref, ...), custom_call_target="tpu_custom_call" | custom-call | flops 42278584320 | bytes 41943040 | tf_op jit(solution)/shard_map/ffn_backward/pallas_call | solution.py:978
  787.2 8.3 fusion.48
  795.5 9.3 fusion.3
  804.9 6.7 fusion.5
  820.0 9.3 reshape.536
  829.3 5.6 copy.228
  842.6 19.9 %reduce-scatter.7.cloned.1.call-done = bf16[256,512]{0,1:T(8,128)(2,1)} async-done(((bf16[1024,512]{0,1:T(8,128)(2,1)}), bf16[256,512]{0,1:T(8,128)(2,1)}) %reduce-scatter.7.cloned.1.call-update) | async-done | bytes 262160 | tf_op jit(solution)/shard_map/reduce_scatter | solution.py:1165
  870.6 175.8 %ffn_backward.3 = (f32[256,1536]{1,0:T(8,128)}, f32[192,2240]{1,0:T(8,128)}, f32[192,2240]{1,0:T(8,128)}, f32[192,2240]{1,0:T(8,128)}, bf16[3,768,2240]{2,1,0:T(...) custom-call(bf16[256,1536]{1,0:T(8,128)(2,1)} %get-tuple-element.140.grad_ref, ...), custom_call_target="tpu_custom_call" | custom-call | flops 42278584320 | bytes 41943040 | tf_op jit(solution)/shard_map/ffn_backward/pallas_call | solution.py:978
  1056.3 8.3 fusion.45
  1064.6 9.4 fusion
  1074.0 6.7 fusion.2
  1110.5 9.1 reshape.533
  1124.3 6.9 pad_maximum_fusion.1
  1136.5 9.2 reshape.531
  1145.7 5.7 copy.230
  1155.0 9.6 reshape.528
  1164.6 5.7 copy.231
  1185.2 11.5 pad_maximum_fusion
  1198.8 15.8 %all-to-all-start = ((bf16[4,384,256]{1,2,0:T(8,128)(2,1)}), bf16[4,384,256]{1,2,0:T(8,128)(2,1)S(1)}, u32[]{:S(2)}, u32[]{:S(2)}) async-start(bf16[4,384,256]{1,2,0:T(8,128)(2,1)} %bitcast.459), calls=%async_computation | async-start | bytes 1572864 | tf_op jit(solution)/shard_map/all_to_all | solution.py:1112
  1214.6 15.7 %reduce-scatter.15.cloned.1.call-done = bf16[1,4,192,896]{3,2,1,0:T(8,128)(2,1)} async-done(((bf16[8,4,192,896]{3,2,1,0:T(8,128)(2,1)}), bf16[1,4,192,896]{3,2,1,0:T(8,128)(2,1)}) %reduce-scatter.15.cloned.1.call-update) | async-done | bytes 1376272 | tf_op jit(solution)/shard_map/reduce_scatter | solution.py:84
  1244.9 5.3 pad_maximum_fusion.2
  1259.8 58.0 %reduce-scatter.11.cloned.1.call-done = bf16[1,4,192,896]{3,2,1,0:T(8,128)(2,1)} async-done(((bf16[8,4,192,896]{3,2,1,0:T(8,128)(2,1)}), bf16[1,4,192,896]{3,2,1,0:T(8,128)(2,1)}) %reduce-scatter.11.cloned.1.call-update) | async-done | bytes 1376272 | tf_op jit(solution)/shard_map/reduce_scatter | solution.py:84
  1329.8 53.2 %psum.7 = f32[4,2,1280]{2,0,1:T(4,128)S(1)} all-reduce(f32[4,2,1280]{2,0,1:T(4,128)S(1)} %pad_maximum_fusion.21), channel_id=1, replica_groups=mesh['gx'=8,'gy'=4] {'gx','gy'}, use_global_device_ids=true, to_apply=%region_30.31 | all-reduce | flops 10240 | bytes 81920 | tf_op jit(solution)/shard_map/psum | solution.py:1203
  1387.2 11.8 reduce-scatter.13.cloned.1.call-done
  (450 shorter events, 288.6 us)
Async XLA Ops:
  7.2 231.3 %all-gather.3.cloned.1.call-start = ((), (), s32[]{:S(2)}) async-start(), calls=%async_computation.8 | async-start | bytes 1310720 | tf_op jit(solution)/shard_map/all_gather | solution.py:1068
  179.0 9.8 copy-start.70
  180.7 69.8 %copy-start.3 = (f32[1536,256]{0,1:T(8,128)}, f32[1536,256]{0,1:T(8,128)S(1)}, u32[]{:S(2)}) copy-start(f32[1536,256]{0,1:T(8,128)S(1)} %copy.200) | copy-start | bytes 4718596
  189.0 39.3 %copy-start.5 = (bf16[256,1536]{1,0:T(8,128)(2,1)}, bf16[256,1536]{1,0:T(8,128)(2,1)S(1)}, u32[]{:S(2)}) copy-start(bf16[256,1536]{1,0:T(8,128)(2,1)S(1)} %multiply_convert_fusion.3) | copy-start | bytes 2359300
  199.2 9.0 copy-start.64
  199.2 266.8 %all-gather.5.cloned.1.call-start = ((), (), s32[]{:S(2)}) async-start(), calls=%async_computation.9 | async-start | bytes 1310720 | tf_op jit(solution)/shard_map/all_gather | solution.py:1068
  210.9 203.9 %copy-start.74 = (f32[1536]{0:T(1024)}, f32[1536]{0:T(1024)S(1)}, u32[]{:S(2)}) copy-start(f32[1536]{0:T(1024)S(1)} %mul.459) | copy-start | bytes 18436
  211.0 43.8 %copy-start.72 = (f32[1536]{0:T(1024)}, f32[1536]{0:T(1024)S(1)}, u32[]{:S(2)}) copy-start(f32[1536]{0:T(1024)S(1)} %mul.453) | copy-start | bytes 18436
  214.6 9.1 slice-start.10
  254.7 147.6 %copy-start.88 = (f32[256]{0:T(256)}, f32[256]{0:T(256)S(1)}, u32[]{:S(2)}) copy-start(f32[256]{0:T(256)S(1)} %add_rsqrt_fusion.2) | copy-start | bytes 3076
  404.5 73.4 %copy-start.9 = (f32[256,1536]{1,0:T(8,128)}, f32[256,1536]{1,0:T(8,128)S(1)}, u32[]{:S(2)}) copy-start(f32[256,1536]{1,0:T(8,128)S(1)} %get-tuple-element.143) | copy-start | bytes 4718596
  404.5 10.4 copy-start.90
  424.4 438.1 %reduce-scatter.7.cloned.1.call-start = ((), (), s32[]{:S(2)}) async-start(), calls=%async_computation.10 | async-start | bytes 1310720 | tf_op jit(solution)/shard_map/reduce_scatter | solution.py:1165
  779.7 35.6 %copy-start.17 = (f32[256,1536]{1,0:T(8,128)}, f32[256,1536]{1,0:T(8,128)S(1)}, u32[]{:S(2)}) copy-start(f32[256,1536]{1,0:T(8,128)S(1)} %get-tuple-element.152) | copy-start | bytes 4718596
  787.2 17.7 %slice-start.3 = ((s8[12582912]{0:T(1024)(128)(4,1)}), s8[4194304]{0:T(1024)(128)(4,1)S(1)}, s32[]{:S(2)}) async-start(s8[12582912]{0:T(1024)(128)(4,1)} %bitcast.463), calls=%async_computation.19 | async-start | bytes 8388608
  787.2 17.7 %slice-start.4 = ((s8[12582912]{0:T(1024)(128)(4,1)}), s8[4194304]{0:T(1024)(128)(4,1)S(1)}, s32[]{:S(2)}) async-start(s8[12582912]{0:T(1024)(128)(4,1)} %bitcast.463), calls=%async_computation.20 | async-start | bytes 8388608
  795.5 9.3 slice-start.5
  815.2 355.1 %reduce-scatter.9.cloned.1.call-start = ((), (), s32[]{:S(2)}) async-start(), calls=%async_computation.11 | async-start | bytes 1310720 | tf_op jit(solution)/shard_map/reduce_scatter | solution.py:1165
  820.0 15.0 %slice-start.6 = ((s8[6291456]{0:T(1024)(128)(4,1)}), s8[2097152]{0:T(1024)(128)(4,1)S(1)}, s32[]{:S(2)}) async-start(s8[6291456]{0:T(1024)(128)(4,1)} %bitcast.465), calls=%async_computation.22 | async-start | bytes 4194304
  870.6 175.8 %copy-start.73 = (f32[1536]{0:T(1024)S(1)}, f32[1536]{0:T(1024)}, u32[]{:S(2)}) copy-start(f32[1536]{0:T(1024)} %copy-done.72) | copy-start | bytes 18436
  870.6 175.8 %copy-start.89 = (f32[256]{0:T(256)S(1)}, f32[256]{0:T(256)}, u32[]{:S(2)}) copy-start(f32[256]{0:T(256)} %copy-done.88) | copy-start | bytes 3076
  1056.3 17.7 %slice-start = ((s8[12582912]{0:T(1024)(128)(4,1)}), s8[4194304]{0:T(1024)(128)(4,1)S(1)}, s32[]{:S(2)}) async-start(s8[12582912]{0:T(1024)(128)(4,1)} %bitcast.461), calls=%async_computation.16 | async-start | bytes 8388608
  1056.3 17.7 %slice-start.1 = ((s8[12582912]{0:T(1024)(128)(4,1)}), s8[4194304]{0:T(1024)(128)(4,1)S(1)}, s32[]{:S(2)}) async-start(s8[12582912]{0:T(1024)(128)(4,1)} %bitcast.461), calls=%async_computation.17 | async-start | bytes 8388608
  1064.5 9.4 slice-start.2
  1086.1 144.2 %reduce-scatter.15.cloned.1.call-start = ((), (), s32[]{:S(2)}) async-start(), calls=%async_computation.14 | async-start | bytes 12386304 | tf_op jit(solution)/shard_map/reduce_scatter | solution.py:84
  1110.5 12.6 slice-start.8
  1131.2 186.6 %reduce-scatter.11.cloned.1.call-start = ((), (), s32[]{:S(2)}) async-start(), calls=%async_computation.12 | async-start | bytes 12386304 | tf_op jit(solution)/shard_map/reduce_scatter | solution.py:84
  1198.8 31.8 %copy-start.80 = (f32[1536]{0:T(1024)S(1)}, f32[1536]{0:T(1024)}, u32[]{:S(2)}) copy-start(f32[1536]{0:T(1024)} %get-tuple-element.120) | copy-start | bytes 18436
  1198.8 32.4 %all-to-all-start = ((bf16[4,384,256]{1,2,0:T(8,128)(2,1)}), bf16[4,384,256]{1,2,0:T(8,128)(2,1)S(1)}, u32[]{:S(2)}, u32[]{:S(2)}) async-start(bf16[4,384,256]{1,2,0:T(8,128)(2,1)} %bitcast.459), calls=%async_computation | async-start | bytes 1572864 | tf_op jit(solution)/shard_map/all_to_all | solution.py:1112
  1214.6 171.4 %reduce-scatter.17.cloned.1.call-start = ((), (), s32[]{:S(2)}) async-start(), calls=%async_computation.15 | async-start | bytes 1720320 | tf_op jit(solution)/shard_map/reduce_scatter | solution.py:85
  1230.4 168.6 %reduce-scatter.13.cloned.1.call-start = ((), (), s32[]{:S(2)}) async-start(), calls=%async_computation.13 | async-start | bytes 1720320 | tf_op jit(solution)/shard_map/reduce_scatter | solution.py:85
  1320.6 63.7 %all-to-all-start.1 = ((bf16[4,384,256]{1,2,0:T(8,128)(2,1)}), bf16[4,384,256]{1,2,0:T(8,128)(2,1)S(1)}, u32[]{:S(2)}, u32[]{:S(2)}) async-start(bf16[4,384,256]{1,2,0:T(8,128)(2,1)} %bitcast.458), calls=%async_computation.3 | async-start | bytes 1572864 | tf_op jit(solution)/shard_map/all_to_all | solution.py:1112
  (91 other events, 300.3 us)
Sparse Core Ops, SparseCore 0:
  199.4 26.1 all-gather.2
  424.5 41.4 all-gather.4
  815.4 47.1 reduce-scatter.6
  1086.2 40.1 reduce-scatter.8
  1131.3 98.9 reduce-scatter.14
  1233.8 83.9 reduce-scatter.10
  1320.1 48.0 reduce-scatter.16
  1370.6 28.3 reduce-scatter.12

commit v4 on v3

--- a/solution.py
+++ b/solution.py
@@ -65,50 +65,24 @@
     return scale * (scaled - normed * project), grad_gain
 
 
-def unpack_attention(pack, sizes):
-    full, start = [], 0
-    for size in sizes:
-        part = pack[..., start : start + size].transpose(0, 2, 1, 3)
-        full.append(part.reshape(D, -1))
-        start += size
-    return full
-
-
-def scatter_attention(grads, devices_x, devices_y):
-    parts = [
-        grad.reshape(devices_x, D // devices_x, devices_y, -1).transpose(0, 2, 1, 3)
-        for grad in grads
-    ]
-    sizes = [part.shape[-1] for part in parts]
-    pack = jnp.concatenate(parts, axis=-1)
-    pack = lax.psum_scatter(pack, "gx", scatter_dimension=0)
-    pack = lax.psum_scatter(pack, "gy", scatter_dimension=0).astype(f32)
+def split_columns(blocks, sizes):
     out, start = [], 0
     for size in sizes:
-        out.append(pack[:, start : start + size])
+        out.append(blocks[:, :, start : start + size].reshape(blocks.shape[0], -1))
         start += size
     return out
+
+
+def turn(tokens_major):
+    count, width = tokens_major.shape
+    devices = lax.axis_size("gx")
+    blocks = tokens_major.T.reshape(devices // 2, 2, width // devices, count)
+    return blocks.transpose(1, 0, 2, 3).reshape(2, width // 2, count)
 
 
 def score_block(q_rot, k_rot, allowed):
     scores = dot("qkgd,skd->kgqs", q_rot, k_rot) * (1.0 / math.sqrt(HEAD_DIM))
     return jnp.where(allowed, scores, -1e30)
-
-
-FF_CHUNK = 512
-PIECES = 4
-
-
-def spans(total):
-    return [(start, min(FF_CHUNK, total - start)) for start in range(0, total, FF_CHUNK)]
-
-
-def nn(left, right):
-    return lax.dot_general(left, right, (((1,), (0,)), ((), ())), preferred_element_type=f32)
-
-
-def nt(left, right):
-    return lax.dot_general(left, right, (((1,), (1,)), ((), ())), preferred_element_type=f32)
 
 
 def wait_for(ref, sem):
@@ -165,6 +139,9 @@
 
     def part(self, i, k, h):
         full = self.items[i][1]
+        if len(full.shape) == 4:
+            half = full.shape[0] // 2
+            return full.at[pl.ds(h * half, half), k]
         half = full.shape[1] // 2
         return full.at[k, pl.ds(h * half, half)]
 
@@ -186,7 +163,9 @@
 
     def place(self, i):
         own, full = self.items[i]
-        return pltpu.make_async_copy(own, full.at[lax.axis_index("gx")], self.local.at[i])
+        gx = lax.axis_index("gx")
+        here = full.at[:, gx] if len(full.shape) == 4 else full.at[gx]
+        return pltpu.make_async_copy(own, here, self.local.at[i])
 
     def begin(self, i):
         gx = lax.axis_index("gx")
@@ -277,14 +256,17 @@
 
 
 class Exchange:
-    def __init__(self, own, full, sems):
+    def __init__(self, own, full, sems, apart=False):
         self.own, self.full, (self.local, self.send_sem, self.recv_sem) = own, full, sems
+        self.apart = apart
 
     def begin(self):
         gx, me, size = lax.axis_index("gx"), lax.axis_index("gy"), lax.axis_size("gy")
         width = self.full.shape[2]
 
         def columns(k):
+            if self.apart:
+                return self.own.at[k]
             return self.own.at[:, pl.ds(pl.multiple_of(k * width, width), width)]
 
         self.place = pltpu.make_async_copy(columns(me), self.full.at[me], self.local)
@@ -332,55 +314,61 @@
 
 
 def opening_kernel(*refs):
-    ins, outs, sems = refs[:8], refs[8:17], refs[17:]
-    resid, cot, small, pack_a, pack_b, wg, wu, wd = ins
-    resid_out, cot_out, small_out, line_a, line_b, attn, gate, up, down = outs
+    ins, outs, sems = refs[:10], refs[10:22], refs[22:]
+    resid, cot, small, qkv_a, o_a, qkv_b, o_b, wg, wu, wd = ins
+    resid_out, cot_out, small_out = outs[:3]
+    lines, (qkv, o, gate, up, down) = outs[3:7], outs[7:]
     me, size = lax.axis_index("gy"), lax.axis_size("gy")
-    partner, others = places()
-    near = list(square()[:2]) if lax.axis_size("gx") == 8 else others
+    owns = (qkv_a, o_a, qkv_b, o_b, small)
     chains = [
         Chain(own, full, sems[3 * k : 3 * k + 3])
-        for k, (own, full) in enumerate(((pack_a, line_a), (pack_b, line_b), (small, small_out)))
+        for k, (own, full) in enumerate(zip(owns, list(lines) + [small_out]))
     ]
     swaps = [
-        Exchange(own, full, sems[9 + 3 * k : 12 + 3 * k])
+        Exchange(own, full, sems[15 + 3 * k : 18 + 3 * k])
         for k, (own, full) in enumerate(((resid, resid_out), (cot, cot_out)))
     ]
-    spread = Spread(
-        [(line_a, attn), (wg.at[0], gate), (wu.at[0], up), (wd.at[0], down)], sems[15:18]
-    )
-    greet([partner] + near, [lax.rem(me + d, size) for d in range(1, size)])
-    chains[0].begin()
-    chains[2].begin()
-    spread.begin(1)
+    items = [(lines[0], qkv), (lines[1], o), (wg.at[0], gate), (wu.at[0], up), (wd.at[0], down)]
+    spread = Spread(items, sems[21:24])
+    greet([spread.partner] + spread.near, [lax.rem(me + d, size) for d in range(1, size)])
+    for k in (0, 1, 4):
+        chains[k].begin()
+    spread.begin(2)
     for t in range(1, size):
         chains[0].relay(t)
+        chains[1].relay(t)
     chains[0].close()
     spread.begin(0)
+    chains[1].close()
+    spread.begin(1)
     swaps[0].begin()
     for t in range(1, size):
+        chains[4].relay(t)
+    spread.begin(3)
+    chains[2].begin()
+    chains[3].begin()
+    spread.relay(2)
+    for t in range(1, size):
         chains[2].relay(t)
-    spread.begin(2)
-    chains[1].begin()
-    spread.relay(1)
-    for t in range(1, size):
-        chains[1].relay(t)
-    spread.begin(3)
+        chains[3].relay(t)
+    spread.begin(4)
     swaps[1].begin()
-    spread.relay(0)
-    spread.finish(1)
-    spread.relay(2)
-    spread.finish(0)
+    for i in (0, 1):
+        spread.relay(i)
+    spread.finish(2)
     spread.relay(3)
-    spread.finish(2)
-    spread.finish(3)
-    for i in (1, 2, 3, 0):
+    for i in (0, 1):
+        spread.finish(i)
+    spread.relay(4)
+    for i in (3, 4):
+        spread.finish(i)
+    for i in range(5):
         spread.close(i)
-    for part in chains[1:] + swaps:
+    for part in chains[2:] + swaps:
         part.close()
 
 
-def opening(resid, cot, small, pack_a, pack_b, wg, wu, wd):
+def opening(resid, cot, small, lines, wg, wu, wd):
     devices, size = lax.axis_size("gx"), lax.axis_size("gy")
     count = resid.shape[1] // size
 
@@ -388,20 +376,35 @@
         return jax.ShapeDtypeStruct(dims, kind)
 
     blocks = shape(size, resid.shape[0], count)
-    line = shape(size, *pack_a.shape)
     weight = shape(devices, *wg.shape[1:])
-    packed = shape(devices, size, *pack_a.shape)
-    out = [blocks, blocks, shape(size, *small.shape, kind=f32), line, line, packed] + [weight] * 3
-
+    out = [blocks, blocks, shape(size, *small.shape, kind=f32)]
+    out += [shape(size, *line.shape) for line in lines]
+    out += [shape(size, devices, *line.shape) for line in lines[:2]] + [weight] * 3
     return pl.pallas_call(
         opening_kernel,
         out_shape=out,
-        in_specs=[ANY] * 8,
-        out_specs=[ANY] * 9,
-        scratch_shapes=chain_scratch() * 3 + exchange_scratch() * 2 + spread_scratch(4),
+        in_specs=[ANY] * 10,
+        out_specs=[ANY] * 12,
+        scratch_shapes=chain_scratch() * 5 + exchange_scratch() * 2 + spread_scratch(5),
         compiler_params=pltpu.CompilerParams(collective_id=2, has_side_effects=True),
         name="opening",
-    )(resid, cot, small, pack_a, pack_b, wg, wu, wd)
+    )(resid, cot, small, *lines, wg, wu, wd)
+
+
+FF_CHUNK = 512
+PIECES = 4
+
+
+def spans(total):
+    return [(start, min(FF_CHUNK, total - start)) for start in range(0, total, FF_CHUNK)]
+
+
+def nn(left, right):
+    return lax.dot_general(left, right, (((1,), (0,)), ((), ())), preferred_element_type=f32)
+
+
+def nt(left, right):
+    return lax.dot_general(left, right, (((1,), (1,)), ((), ())), preferred_element_type=f32)
 
 
 def line_pass(own_ref, own, gathered, part, outb, inb, sems, load, finish, peers=(), plan={}):
@@ -571,25 +574,24 @@
 
 
 ORDER = {
-    ("step", 0): "b0",
-    ("step", 2): "b1",
-    ("hop", 0): "r0 r1 b2",
-    ("hop", 1): "f0 f1 b3",
+    ("step", 0): (("begin", 0), ("begin", 1)),
+    ("step", 2): (("begin", 2),),
+    ("hop", 0): (("relay", 0), ("relay", 1), ("relay", 2), ("begin", 3)),
+    ("hop", 1): (("finish", 0), ("finish", 1), ("finish", 2), ("begin", 4)),
 }
-REST = "r2 r3 f2 f3 c0 c1 c2 c3"
-VERBS = {"b": "begin", "r": "relay", "f": "finish", "c": "close"}
-
-
-def schedule(spread, size):
-    def run(text):
+REST = (("relay", 3), ("relay", 4), ("finish", 3), ("finish", 4))
+
+
+def schedule(spread):
+    def run(steps):
         def act():
-            for word in text.split():
-                getattr(spread, VERBS[word[0]])(int(word[1]))
+            for verb, i in steps:
+                getattr(spread, verb)(i)
 
         return act
 
-    plan = {key: run(text) for key, text in ORDER.items()}
-    return plan, [(VERBS[word[0]], int(word[1])) for word in REST.split()]
+    plan = {key: run(steps) for key, steps in ORDER.items()}
+    return plan, REST + tuple(("close", i) for i in range(len(spread.items)))
 
 
 def forward_kernel(extra, *refs):
@@ -602,12 +604,12 @@
     wg, wu, wd, gate, up, hidden, turned, w_sem, out_sem = scratch[LINE : LINE + 9]
     peers, spread = [], None
     if extra:
-        items = [(r if r.shape == w.shape[1:] else r.at[1], w) for r, w in zip(shards, wholes)]
+        items = [(r if len(w.shape) == 4 else r.at[1], w) for r, w in zip(shards, wholes)]
         spread = Spread(items, scratch[LINE + 9 :])
         partner, others = places()
         peers = [partner] + (list(square()[:2]) if spread.four else others)
 
-    plan, rest = schedule(spread, lax.axis_size("gy")) if extra else ({}, ())
+    plan, rest = schedule(spread) if extra else ({}, ())
     loads = [
         pltpu.make_async_copy(src, dst, w_sem.at[k])
         for k, (src, dst) in enumerate(((wg_ref, wg), (wu_ref, wu), (wd_ref, wd)))
@@ -668,7 +670,9 @@
     wide = jax.ShapeDtypeStruct((size, rows, hidden), bf16)
     extra = len(shards)
     wholes = [
-        jax.ShapeDtypeStruct((devices,) + (s.shape if k == 0 else s.shape[1:]), bf16)
+        jax.ShapeDtypeStruct(
+            (size, devices) + s.shape[1:] if k < 2 else (devices,) + s.shape[1:], bf16
+        )
         for k, s in enumerate(shards)
     ]
     return pl.pallas_call(
@@ -1003,6 +1007,326 @@
     )(grad, gate, up, hidden, turned, wg, wu, wd)
 
 
+class Fold:
+    def __init__(self, lhs, rhs, bufs, sems):
+        self.lhs, self.rhs = lhs, rhs
+        self.up, self.low, self.a_in, self.r_in, self.c_in, self.z_out, self.z_in = bufs
+        (
+            self.a_send,
+            self.a_recv,
+            self.r_send,
+            self.r_recv,
+            self.c_send,
+            self.c_recv,
+            self.z_send,
+            self.z_recv,
+        ) = sems
+        self.gx, self.gy = lax.axis_index("gx"), lax.axis_index("gy")
+        self.core, self.size = lax.rem(self.gx, 2), lax.axis_size("gy")
+        self.chips = lax.axis_size("gx") // 2
+        self.r = self.low.shape[2] // self.chips
+        self.four = self.chips == 4
+        self.partner, self.others = places()
+        self.near = list(square()[:2]) if self.four else self.others
+
+    def product(self, m, which, z):
+        return [nn(left[which], right[z]) for left, right in zip(self.lhs[m], self.rhs[m])]
+
+    def remote(self, src, dst, send, recv, gx, gy):
+        return pltpu.make_async_remote_copy(
+            src_ref=src,
+            dst_ref=dst,
+            send_sem=send,
+            recv_sem=recv,
+            device_id=(gx, gy),
+            device_id_type=MESH,
+        )
+
+    def block(self, m, device, start=0, size=None):
+        size = self.r if size is None else size
+        first = (device // 2) * self.r + start
+        return self.low.at[m, :, pl.ds(pl.multiple_of(first, 16), size)]
+
+    def swap(self, m, z):
+        return self.remote(
+            self.up.at[m, z],
+            self.a_in.at[m, z],
+            self.a_send.at[m, z],
+            self.a_recv.at[m, z],
+            self.partner,
+            self.gy,
+        )
+
+    def first(self, m):
+        for z in range(self.size):
+            left, right = self.product(m, 1 - self.core, z)
+            edge = left.shape[1]
+            self.up[m, z, :, :edge] = left.astype(bf16)
+            self.up[m, z, :, edge:] = right.astype(bf16)
+            self.swap(m, z).start()
+
+    def corner(self, m, h):
+        side, along, across = square()
+        half = self.r // 2
+        return self.remote(
+            self.block(m, across, h * half, half),
+            self.r_in.at[m, h],
+            self.r_send.at[m, h],
+            self.r_recv.at[m, h],
+            along if h else side,
+            self.gy,
+        )
+
+    def second(self, m):
+        for z in range(self.size):
+            left, right = self.product(m, self.core, z)
+            edge = left.shape[1]
+            self.swap(m, z).wait_recv()
+            came = self.a_in[m, z].astype(f32)
+            self.low[m, z, :, :edge] = (left + came[:, :edge]).astype(bf16)
+            self.low[m, z, :, edge:] = (right + came[:, edge:]).astype(bf16)
+        if self.four:
+            for h in range(2):
+                self.corner(m, h).start()
+
+    def hand(self, m, k):
+        return self.remote(
+            self.block(m, self.near[k]),
+            self.c_in.at[m, k],
+            self.c_send.at[m, k],
+            self.c_recv.at[m, k],
+            self.near[k],
+            self.gy,
+        )
+
+    def third(self, m):
+        if self.four:
+            side, along, _ = square()
+            half = self.r // 2
+            for h, device in ((0, along), (1, side)):
+                self.corner(m, h).wait_recv()
+                here = self.block(m, device, h * half, half)
+                here[...] = (here[...].astype(f32) + self.r_in[m, h].astype(f32)).astype(bf16)
+        for k in range(len(self.near)):
+            self.hand(m, k).start()
+
+    def down_line(self, m, d):
+        target = lax.rem(self.gy + d, self.size)
+        return self.remote(
+            self.z_out.at[m, target],
+            self.z_in.at[m, self.gy],
+            self.z_send.at[m, d],
+            self.z_recv.at[m, self.gy],
+            self.gx,
+            target,
+        )
+
+    def fourth(self, m):
+        for k in range(len(self.near)):
+            self.hand(m, k).wait_recv()
+        mine = self.block(m, self.gx)
+        for z in range(self.size):
+            total = mine[z].astype(f32)
+            for k in range(len(self.near)):
+                total = total + self.c_in[m, k, z].astype(f32)
+            self.z_out[m, z] = total.astype(bf16)
+        for d in range(1, self.size):
+            self.down_line(m, d).start()
+
+    def fifth(self, m, out):
+        total = self.z_out[m, self.gy].astype(f32)
+        for d in range(1, self.size):
+            z = lax.rem(self.gy + d, self.size)
+            wait_for(self.z_in.at[m, z], self.z_recv.at[m, z])
+            total = total + self.z_in[m, z].astype(f32)
+        out[m] = total
+
+    def drain(self, m):
+        for z in range(self.size):
+            self.swap(m, z).wait_send()
+        if self.four:
+            for h in range(2):
+                self.corner(m, h).wait_send()
+        for k in range(len(self.near)):
+            self.hand(m, k).wait_send()
+        for d in range(1, self.size):
+            self.down_line(m, d).wait_send()
+
+
+class Total:
+    def __init__(self, own, line_in, pair, pair_in, chip_in, sems):
+        self.own, self.line_in, self.pair = own, line_in, pair
+        self.pair_in, self.chip_in = pair_in, chip_in
+        self.l_send, self.l_recv, self.p_send, self.p_recv, self.g_send, self.g_recv = sems
+        self.gx, self.gy = lax.axis_index("gx"), lax.axis_index("gy")
+        self.size, self.chips = lax.axis_size("gy"), lax.axis_size("gx") // 2
+        self.partner, self.others = places()
+
+    def remote(self, src, dst, send, recv, gx, gy):
+        return pltpu.make_async_remote_copy(
+            src_ref=src,
+            dst_ref=dst,
+            send_sem=send,
+            recv_sem=recv,
+            device_id=(gx, gy),
+            device_id_type=MESH,
+        )
+
+    def line(self, d):
+        target = lax.rem(self.gy + d, self.size)
+        return self.remote(
+            self.own.at[target],
+            self.line_in.at[self.gy],
+            self.l_send.at[d],
+            self.l_recv.at[self.gy],
+            self.gx,
+            target,
+        )
+
+    def across(self):
+        return self.remote(
+            self.pair.at[0], self.pair_in, self.p_send, self.p_recv, self.partner, self.gy
+        )
+
+    def chip(self, k):
+        return self.remote(
+            self.pair.at[1],
+            self.chip_in.at[self.gx // 2],
+            self.g_send.at[k],
+            self.g_recv.at[self.gx // 2],
+            self.others[k],
+            self.gy,
+        )
+
+    def begin(self):
+        for d in range(1, self.size):
+            self.line(d).start()
+
+    def middle(self):
+        total = self.own[self.gy]
+        for d in range(1, self.size):
+            z = lax.rem(self.gy + d, self.size)
+            wait_for(self.line_in.at[z], self.l_recv.at[z])
+            total = total + self.line_in[z]
+        self.pair[0] = total
+        self.across().start()
+
+    def later(self):
+        self.across().wait_recv()
+        self.pair[1] = self.pair[0] + self.pair_in[...]
+        self.chip_in[self.gx // 2] = self.pair[1]
+        for k in range(self.chips - 1):
+            self.chip(k).start()
+
+    def close(self, out):
+        for k in range(self.chips - 1):
+            q = self.others[k] // 2
+            wait_for(self.chip_in.at[q], self.g_recv.at[q])
+        total = self.chip_in[0]
+        for q in range(1, self.chips):
+            total = total + self.chip_in[q]
+        out[...] = total
+        for d in range(1, self.size):
+            self.line(d).wait_send()
+        self.across().wait_send()
+        for k in range(self.chips - 1):
+            self.chip(k).wait_send()
+
+
+def closing_kernel(layers, *refs):
+    operands, refs = refs[: 4 * layers], refs[4 * layers :]
+    small, out_rows, grad_rows = refs[:3]
+    grads, small_out, out_blocks, grad_blocks = refs[3:7]
+    scratch = refs[7:]
+    lhs = [operands[4 * m : 4 * m + 2] for m in range(layers)]
+    rhs = [operands[4 * m + 2 : 4 * m + 4] for m in range(layers)]
+    fold = Fold(lhs, rhs, scratch[:7], scratch[7:15])
+    total = Total(small, *scratch[15:19], scratch[19:25])
+    swaps = [
+        Exchange(own, full, scratch[25 + 3 * k : 28 + 3 * k], True)
+        for k, (own, full) in enumerate(((grad_rows, grad_blocks), (out_rows, out_blocks)))
+    ]
+    me, size = lax.axis_index("gy"), lax.axis_size("gy")
+    greet([fold.partner] + fold.others, [lax.rem(me + d, size) for d in range(1, size)])
+    total.begin()
+    for m in range(layers):
+        fold.first(m)
+    for swap in swaps:
+        swap.begin()
+    fold.second(0)
+    total.middle()
+    for m in range(1, layers):
+        fold.second(m)
+    total.later()
+    for m in range(layers):
+        fold.third(m)
+    for m in range(layers):
+        fold.fourth(m)
+    total.close(small_out)
+    for m in range(layers):
+        fold.fifth(m, grads)
+    for m in range(layers):
+        fold.drain(m)
+    for swap in swaps:
+        swap.close()
+
+
+def closing(operands, small, out_rows, grad_rows):
+    layers = len(operands) // 4
+    devices, size = lax.axis_size("gx"), lax.axis_size("gy")
+    half = operands[0].shape[1]
+    chips = devices // 2
+    r, near = half // chips, 2 if chips == 4 else chips - 1
+    c = operands[2].shape[2] + operands[3].shape[2]
+    vmem, dma = pltpu.VMEM, pltpu.SemaphoreType.DMA
+    row = small.shape[1:]
+    local = pl.BlockSpec(memory_space=pltpu.VMEM)
+    blocks = jax.ShapeDtypeStruct(out_rows.shape, bf16)
+    return pl.pallas_call(
+        functools.partial(closing_kernel, layers),
+        out_shape=[
+            jax.ShapeDtypeStruct((layers, r, c), f32),
+            jax.ShapeDtypeStruct(row, f32),
+            blocks,
+            blocks,
+        ],
+        in_specs=[local] * (len(operands) + 1) + [ANY] * 2,
+        out_specs=[local] * 2 + [ANY] * 2,
+        scratch_shapes=[
+            vmem((layers, size, half, c), bf16),
+            vmem((layers, size, half, c), bf16),
+            vmem((layers, size, half, c), bf16),
+            vmem((layers, 2, size, r // 2, c), bf16),
+            vmem((layers, near, size, r, c), bf16),
+            vmem((layers, size, r, c), bf16),
+            vmem((layers, size, r, c), bf16),
+            dma((layers, size)),
+            dma((layers, size)),
+            dma((layers, 2)),
+            dma((layers, 2)),
+            dma((layers, near)),
+            dma((layers, near)),
+            dma((layers, size)),
+            dma((layers, size)),
+            vmem((size,) + row, f32),
+            vmem((2,) + row, f32),
+            vmem(row, f32),
+            vmem((chips,) + row, f32),
+            dma((size,)),
+            dma((size,)),
+            dma,
+            dma,
+            dma((chips,)),
+            dma((chips,)),
+        ]
+        + exchange_scratch() * 2,
+        compiler_params=pltpu.CompilerParams(
+            collective_id=4, has_side_effects=True, vmem_limit_bytes=VMEM_LIMIT
+        ),
+        name="closing",
+    )(*operands, small, out_rows, grad_rows)
+
+
 def on_device(
     residual_in,
     w_query,
@@ -1019,7 +1343,6 @@
     w_down,
     cotangent,
 ):
-    devices_x = lax.axis_size("gx")
     devices_y = lax.axis_size("gy")
     rows_tok = residual_in.shape[1]
     count = rows_tok // devices_y
@@ -1033,14 +1356,15 @@
     small = jnp.concatenate([gain_attn, gain_ffn, b_query, b_key, b_value], axis=1)
     small_sizes = [v.shape[1] for v in (gain_attn, gain_ffn, b_query, b_key, b_value)]
     small = jnp.pad(small.astype(f32), ((0, 8 - LAYERS), (0, 0)))
-    packs = [
-        jnp.concatenate([w[l] for w in (w_query, w_key, w_value, w_output)], axis=1)
-        for l in range(LAYERS)
-    ]
-    pack_sizes = [w.shape[2] for w in (w_query, w_key, w_value, w_output)]
-    opened = opening(residual_in, cotangent, small, *packs, w_gate, w_up, w_down)
-    resid, cot, small, _, line_next, attn_pack = opened[:6]
-    ffn_full = [[w.reshape(D, -1) for w in opened[6:]], None]
+    lines = []
+    for l in range(LAYERS):
+        lines += [jnp.concatenate([w_query[l], w_key[l], w_value[l]], axis=1), w_output[l]]
+    part_sizes = (w_query.shape[2], w_key.shape[2], w_value.shape[2])
+    opened = opening(residual_in, cotangent, small, lines, w_gate, w_up, w_down)
+    resid, cot, small = opened[:3]
+    lines_next = opened[5:7]
+    attn_full = [[w.reshape(devices_y, D, -1) for w in opened[7:9]], None]
+    ffn_full = [[w.reshape(D, -1) for w in opened[9:]], None]
     small = small[:, :LAYERS].transpose(1, 0, 2)
     vectors, start = [], 0
     for size in small_sizes:
@@ -1050,17 +1374,20 @@
 
     resid = resid.reshape(D, count).astype(f32).T
     cot = cot.reshape(D, count)
-    attn_full = [unpack_attention(attn_pack, pack_sizes), None]
 
     kept = []
     for l in range(LAYERS):
-        wq, wk, wv, wo = attn_full[l]
+        w_qkv, w_out = attn_full[l]
         wg, wu, wd = ffn_full[l]
         normed_one, scale_one = rms_parts(resid)
         acts_one = (normed_one * gains_one[l]).astype(bf16)
-        queries = dot("td,dq->tq", acts_one, wq) + bias_q[l]
-        keys = dot("td,dq->tq", acts_one, wk) + bias_k[l]
-        values = (dot("td,dq->tq", acts_one, wv) + bias_v[l]).astype(bf16)
+        queries, keys, values = split_columns(
+            jnp.stack([dot("td,dq->tq", acts_one, w_qkv[z]) for z in range(devices_y)], axis=1),
+            part_sizes,
+        )
+        queries = queries + bias_q[l]
+        keys = keys + bias_k[l]
+        values = (values + bias_v[l]).astype(bf16)
         q_rot = rotate(queries.reshape(count, HEADS, HEAD_DIM), cosine, sine).astype(bf16)
         q_rot = q_rot.reshape(count, KV_HEADS, GROUP, HEAD_DIM)
         k_rot = rotate(keys.reshape(count, KV_HEADS, HEAD_DIM), cosine, sine).astype(bf16)
@@ -1076,14 +1403,17 @@
         soft = (expo / total).astype(bf16)
         log_total = top + jnp.log(total)
         mixed = dot("kgqs,skd->qkgd", soft, v_heads).reshape(count, -1).astype(bf16)
-        middle = resid + dot("tq,dq->td", mixed, wo)
+        mixed = mixed.reshape(count, devices_y, -1)
+        middle = resid
+        for z in range(devices_y):
+            middle = middle + dot("tq,dq->td", mixed[:, z], w_out[z])
         normed_two, scale_two = rms_parts(middle)
         acts_two = (normed_two * gains_two[l]).astype(bf16)
         if l == 0:
-            shards = (line_next, w_gate, w_up, w_down)
+            shards = (*lines_next, w_gate, w_up, w_down)
             done = forward_ffn(acts_two, wg, wu, wd, shards)
-            attn_full[1] = unpack_attention(done[5], pack_sizes)
-            ffn_full[1] = [w.reshape(D, -1) for w in done[6:]]
+            attn_full[1] = [w.reshape(devices_y, D, -1) for w in done[5:7]]
+            ffn_full[1] = [w.reshape(D, -1) for w in done[7:]]
         else:
             done = forward_ffn(acts_two, wg, wu, wd)
         part, acts_two, gate, up, hidden = done[:5]
@@ -1107,12 +1437,6 @@
         )
         resid = middle + part
 
-    def to_blocks(tokens_major):
-        flipped = tokens_major.astype(bf16).T
-        out = lax.all_to_all(flipped, "gy", split_axis=0, concat_axis=1, tiled=True)
-        return out.astype(f32)
-
-    output = to_blocks(resid)
     grad = cot.astype(f32).T + 2.0 * penalty * resid
     attn_grads = [None] * LAYERS
     ffn_grads = [None] * LAYERS
@@ -1135,7 +1459,7 @@
             up,
             hidden,
         ) = kept[l]
-        wq, wk, wv, wo = attn_full[l]
+        w_qkv, w_out = attn_full[l]
         wg, wu, wd = ffn_full[l]
         done = backward_ffn(grad.astype(bf16), gate, up, hidden, acts_two, wg, wu, wd)
         grad_acts_two, ffn_grads[l] = done[0], done[1:4]
@@ -1144,8 +1468,9 @@
         )
         grad_mid = grad + grad_norm
         grad_branch = grad_mid.astype(bf16)
-        grad_wo = dot("td,tq->dq", grad_branch, mixed)
-        grad_mixed = dot("td,dq->tq", grad_branch, wo).astype(bf16)
+        grad_mixed = jnp.concatenate(
+            [dot("td,dq->tq", grad_branch, w_out[z]) for z in range(devices_y)], axis=1
+        ).astype(bf16)
         grad_heads = grad_mixed.reshape(count, KV_HEADS, GROUP, HEAD_DIM)
         scores = score_block(q_rot, k_rot, allowed)
         soft_full = jnp.exp(scores - log_total)
@@ -1167,24 +1492,18 @@
         grad_k = rotate_back(both[:, :half].reshape(count, KV_HEADS, HEAD_DIM), cosine, sine)
         grad_k = grad_k.reshape(count, -1).astype(bf16)
         grad_v = both[:, half:].astype(bf16)
-        grad_acts_one = (
-            dot("tq,dq->td", grad_q, wq)
-            + dot("tq,dq->td", grad_k, wk)
-            + dot("tq,dq->td", grad_v, wv)
-        )
-        attn_grads[l] = scatter_attention(
-            [
-                g.astype(bf16)
-                for g in (
-                    dot("td,tq->dq", acts_one, grad_q),
-                    dot("td,tq->dq", acts_one, grad_k),
-                    dot("td,tq->dq", acts_one, grad_v),
-                    grad_wo,
-                )
-            ],
-            devices_x,
-            devices_y,
-        )
+        grad_qkv = jnp.concatenate(
+            [g.reshape(count, devices_y, -1) for g in (grad_q, grad_k, grad_v)], axis=2
+        ).transpose(1, 0, 2)
+        grad_acts_one = dot("tq,dq->td", grad_qkv[0], w_qkv[0])
+        for z in range(1, devices_y):
+            grad_acts_one = grad_acts_one + dot("tq,dq->td", grad_qkv[z], w_qkv[z])
+        attn_grads[l] = [
+            turn(acts_one),
+            turn(grad_branch),
+            grad_qkv,
+            mixed.transpose(1, 0, 2),
+        ]
         grad_norm, grad_gain_one = norm_backward(
             grad_acts_one, normed_one, scale_one, gains_one[l]
         )
@@ -1200,8 +1519,22 @@
             )
         ]
     small = jnp.stack([jnp.concatenate(v, axis=1) for v in small_grads], axis=1)
-    small = lax.psum(small, ("gx", "gy"))
-    small = lax.dynamic_index_in_dim(small, lax.axis_index("gy"), 0, keepdims=False)
+    small = jnp.pad(small, ((0, 0), (0, 8 - LAYERS), (0, 0)))
+
+    def to_rows(tokens_major):
+        return tokens_major.astype(bf16).T.reshape(devices_y, -1, count)
+
+    def from_blocks(blocks):
+        return blocks.transpose(1, 0, 2).reshape(-1, rows_tok).astype(f32)
+
+    attn_sums, small, output, grad_input = closing(
+        attn_grads[0] + attn_grads[1], small, to_rows(resid), to_rows(grad)
+    )
+    small = small[:LAYERS]
+    attn_out, start = [], 0
+    for size in part_sizes + (w_output.shape[2],):
+        attn_out.append(attn_sums[:, :, start : start + size])
+        start += size
     small_out, start = [], 0
     for size in small_sizes:
         small_out.append(small[:, start : start + size])
@@ -1211,15 +1544,15 @@
         return jnp.stack([part[k] for part in parts])
 
     return (
-        output,
-        to_blocks(grad),
-        stack(attn_grads, 0),
-        stack(attn_grads, 1),
-        stack(attn_grads, 2),
+        from_blocks(output),
+        from_blocks(grad_input),
+        attn_out[0],
+        attn_out[1],
+        attn_out[2],
         small_out[2],
         small_out[3],
         small_out[4],
-        stack(attn_grads, 3),
+        attn_out[3],
         small_out[0],
         small_out[1],
         stack(ffn_grads, 0),

time: 1420 us -> 1290 us (0.908)
  Pallas kernels: 767 us -> 903 us
  local copies, waits for them, and re-layouts: 219 us -> 117 us
  blocking collectives: 53.2 us -> 0 us
  waiting for transfers between devices: 115 us -> 66.4 us
  matrix products: 109 us -> 80.8 us
  starting transfers between devices: 21.2 us -> 0.74 us
  other arithmetic: 110 us -> 93.9 us
    pallas_call x1 -> x2, Pallas kernels: 161 us -> 305 us  [the longest x1 162 us: opening(): pl.pallas_call(opening_kernel, out_shape=out, in_specs=[ANY] * 10, out_sp...]
    reduce_scatter x4 -> x0, waiting for transfers between devices: 85.5 us -> none  [the longest x2 73.7 us: scatter_attention(): pack = lax.psum_scatter(pack, 'gx', scatter_dimension=0)]
    reshape x16 -> x6, local copies, waits for them, and re-layouts: 74.2 us -> 7.11 us  [the longest x2 4.63 us: on_device(): grad_qrot.reshape(count, HEADS, HEAD_DIM)]
    psum x1 -> x0, blocking collectives: 53.2 us -> none  [on_device(): small = lax.psum(small, ('gx', 'gy'))]
    transpose x16 -> x8, local copies, waits for them, and re-layouts: 65.5 us -> 15.9 us  [the longest x3 7.17 us: turn(): blocks = tokens_major.T.reshape(devices // 2, 2, width // devices, count)]
    dot_general x36 -> x44, matrix products: 109 us -> 80.8 us  [dot(): return jnp.einsum(pattern, left, right, preferred_element_type=f32)]
    slice x3 -> x15, local copies, waits for them, and re-layouts: 2.24 us -> 30.1 us  [the longest x2 9.89 us: on_device(): middle = middle + dot('tq,dq->td', mixed[:, z], w_out[z])]
    all_to_all x2 -> x0, starting transfers between devices: 20.4 us -> none  [to_blocks(): out = lax.all_to_all(flipped, 'gy', split_axis=0, concat_axis=1, tiled=True)]
  transfers between devices with their start and end apart: 10 -> 4, of which waited for: 5 -> 4; matrix products, arithmetic and copies ran while one was open for 17% -> 7% of each run, Pallas kernels for 0% -> 0%
where the time goes in v4:
time: 1290 us; the launch traced here: 1280 us
  Pallas kernels  903 us (70%)
  local copies, waits for them, and re-layouts  117 us (9%)
  other arithmetic  93.9 us (7%)
  matrix products  80.8 us (6%)
  waiting for transfers between devices  66.4 us (5%)
  between operations  15.9 us (1%)
    pallas_call x2, Pallas kernels, backward_ffn(): pl.pallas_call(backward_kernel, out_shape=[jax.ShapeDtypeStruct((rows, wi...  348 us
    pallas_call x2, Pallas kernels, forward_ffn(): pl.pallas_call(functools.partial(forward_kernel, extra), out_shape=[jax.S...  250 us
    pallas_call x1, Pallas kernels, opening(): pl.pallas_call(opening_kernel, out_shape=out, in_specs=[ANY] * 10, out_sp...  162 us
    pallas_call x1, Pallas kernels, closing(): pl.pallas_call(functools.partial(closing_kernel, layers), out_shape=[jax....  143 us
    dot_general x44, matrix products, dot(): return jnp.einsum(pattern, left, right, preferred_element_type=f32)  80.8 us
    unnamed x244, local copies, waits for them, and re-layouts  36.6 us
    reduce_scatter x2, waiting for transfers between devices, on_device(): lax.psum_scatter(both, 'gy', scatter_dimension=0, tiled=True).astype(f32)  36.5 us
    all_gather x2, waiting for transfers between devices, on_device(): both = lax.all_gather(both, 'gy', axis=0, tiled=True)  29.8 us
  transfers between devices with their start and end apart: 4, of which 4 were waited for; matrix products, arithmetic and copies ran while one was open for 7% of the time, Pallas kernels for 0%

profile of v4, /device:TPU:9, one launch (start us, length us, event | category | flops | bytes accessed | tf_op | source)
XLA Modules:
  0.0 1277.3 jit_solution(4884147920555401675)
XLA Ops:
  14.3 161.6 %opening.1 = (bf16[4,384,256]{2,1,0:T(8,128)(2,1)}, bf16[4,384,256]{2,1,0:T(8,128)(2,1)}, f32[4,8,1280]{2,1,0:T(8,128)}, bf16[4,192,512]{2,1,0:T(8,128)(2,1)}, b...) custom-call(bf16[384,1024]{1,0:T(8,128)(2,1)} %refs_0_.1, ...), custom_call_target="tpu_custom_call" | custom-call | tf_op jit(solution)/shard_map/opening/pallas_call | solution.py:383
  179.7 3.6 fusion.81
  205.3 5.0 fusion.83
  210.3 6.3 all-gather.3.cloned.1.call-done
  224.6 3.6 fusion.30
  235.4 147.3 %ffn_forward.2 = (f32[256,1536]{1,0:T(8,128)}, bf16[2,768,1024]{2,1,0:T(8,128)(2,1)}, bf16[4,256,2240]{2,1,0:T(8,128)(2,1)}, bf16[4,256,2240]{2,1,0:T(8,128)(2,1...) custom-call(bf16[256,1536]{1,0:T(8,128)(2,1)} %multiply_convert_fusi, ...), custom_call_target="tpu_custom_call" | custom-call | flops 21139292160 | bytes 41943040 | tf_op jit(solution)/shard_map/ffn_forward/pallas_call | solution.py:678
  384.8 3.2 fusion.80
  398.4 2.6 fusion.28
  405.6 3.0 copy.81
  412.1 4.9 fusion.82
  417.0 23.5 %all-gather.5.cloned.1.call-done = bf16[1024,512]{0,1:T(8,128)(2,1)} async-done(((bf16[256,512]{0,1:T(8,128)(2,1)}), bf16[1024,512]{0,1:T(8,128)(2,1)}) %all-gather.5.cloned.1.call-update) | async-done | bytes 1048592 | tf_op jit(solution)/shard_map/all_gather | solution.py:1395
  448.6 3.7 fusion.29
  459.3 102.7 %ffn_forward.3 = (f32[256,1536]{1,0:T(8,128)}, bf16[2,768,1024]{2,1,0:T(8,128)(2,1)}, bf16[4,256,2240]{2,1,0:T(8,128)(2,1)}, bf16[4,256,2240]{2,1,0:T(8,128)(2,1)}, bf16[4,256,2240]{2,1,0:T(8,128)(2,1)}) custom-call(bf16[256,1536]{1,0:T(8,128)(2,1)} %multiply_convert_fusion.refs_0_, bf16[1536,2240]{1,0:T(8,128)(2,1)} %bitcast.605, ...), custom_call_target="tpu_custom_call" | custom-call | flops 21139292160 | bytes 41943040 | tf_op jit(solution)/shard_map/ffn_forward/pallas_call | solution.py:678
  562.0 3.7 fusion.49.grad_ref
  565.7 172.0 %ffn_backward.2 = (f32[256,1536]{1,0:T(8,128)}, f32[192,2240]{1,0:T(8,128)}, f32[192,2240]{1,0:T(8,128)}, f32[192,2240]{1,0:T(8,128)}, bf16[3,768,2240]{2,1,0:T(...) custom-call(bf16[256,1536]{1,0:T(8,128)(2,1)} %fusion.49.grad_ref, ...), custom_call_target="tpu_custom_call" | custom-call | flops 42278584320 | bytes 41943040 | tf_op jit(solution)/shard_map/ffn_backward/pallas_call | solution.py:982
  740.6 4.1 fusion.79
  751.7 8.5 fusion.42
  760.2 9.3 fusion.3
  769.5 6.7 fusion.5
  786.8 4.9 bitcast_multiply_fusion.7
  794.7 3.0 copy.92
  797.7 3.0 copy.90
  806.4 2.6 add_convert_fusion.2
  809.0 23.0 %reduce-scatter.3.cloned.1.call-done = bf16[256,512]{0,1:T(8,128)(2,1)} async-done(((bf16[1024,512]{0,1:T(8,128)(2,1)}), bf16[256,512]{0,1:T(8,128)(2,1)}) %reduce-scatter.3.cloned.1.call-update) | async-done | bytes 262160 | tf_op jit(solution)/shard_map/reduce_scatter | solution.py:1490
  846.5 176.0 %ffn_backward.3 = (f32[256,1536]{1,0:T(8,128)}, f32[192,2240]{1,0:T(8,128)}, f32[192,2240]{1,0:T(8,128)}, f32[192,2240]{1,0:T(8,128)}, bf16[3,768,2240]{2,1,0:T(...) custom-call(bf16[256,1536]{1,0:T(8,128)(2,1)} %get-tuple-element.142.grad_ref, ...), custom_call_target="tpu_custom_call" | custom-call | flops 42278584320 | bytes 41943040 | tf_op jit(solution)/shard_map/ffn_backward/pallas_call | solution.py:982
  1031.5 8.2 fusion.39
  1039.7 9.4 fusion
  1049.1 6.8 fusion.2
  1071.0 3.0 convert_reduce_fusion.1
  1074.3 3.1 add_convert_fusion.1
  1086.1 13.5 %reduce-scatter.5.cloned.1.call-done = bf16[256,512]{0,1:T(8,128)(2,1)} async-done(((bf16[1024,512]{0,1:T(8,128)(2,1)}), bf16[256,512]{0,1:T(8,128)(2,1)}) %reduce-scatter.5.cloned.1.call-update) | async-done | bytes 262160 | tf_op jit(solution)/shard_map/reduce_scatter | solution.py:1490
  1114.1 143.0 %closing.1 = (f32[2,192,896]{2,1,0:T(8,128)}, f32[8,1280]{1,0:T(8,128)}, bf16[4,384,256]{2,1,0:T(8,128)(2,1)}, bf16[4,384,256]{2,1,0:T(8,128)(2,1)}) custom-call(bf16[2,768,256]{2,1,0:T(8,128)(2,1)} %bitcast.563, bf16[2,768,256]{2,1,0:T(8,128)(2,1)} %bitcast.559, bf16[4,256,512]{2,1,0:T(8,128)(2,1)} %copy-done.31, bf16[4,256,384]{2,1,0:T(8,128)(2,1)} %bitcast.554, ...), custom_call_target="tpu_custom_call" | custom-call | tf_op jit(solution)/shard_map/closing/pallas_call | solution.py:1285
  (449 shorter events, 186.7 us)
Async XLA Ops:
  7.2 209.4 %all-gather.3.cloned.1.call-start = ((), (), s32[]{:S(2)}) async-start(), calls=%async_computation.2 | async-start | bytes 1310720 | tf_op jit(solution)/shard_map/all_gather | solution.py:1395
  179.5 48.8 %copy-start.2 = (f32[1536,256]{0,1:T(8,128)}, f32[1536,256]{0,1:T(8,128)S(1)}, u32[]{:S(2)}) copy-start(f32[1536,256]{0,1:T(8,128)S(1)} %copy.148) | copy-start | bytes 4718596
  189.4 14.3 %copy-start.32 = (f32[256,128]{0,1:T(8,128)}, f32[256,128]{0,1:T(8,128)S(1)}, u32[]{:S(2)}) copy-start(f32[256,128]{0,1:T(8,128)S(1)} %get-tuple-element.204) | copy-start | bytes 393220
  190.3 250.2 %all-gather.5.cloned.1.call-start = ((), (), s32[]{:S(2)}) async-start(), calls=%async_computation.3 | async-start | bytes 1310720 | tf_op jit(solution)/shard_map/all_gather | solution.py:1395
  194.3 38.8 %copy-start.100 = (f32[1536]{0:T(1024)}, f32[1536]{0:T(1024)S(1)}, u32[]{:S(2)}) copy-start(f32[1536]{0:T(1024)S(1)} %mul.456) | copy-start | bytes 18436
  205.3 12.5 copy-start.36
  217.8 4.8 copy-start.82
  220.0 4.6 copy-start
  220.0 4.6 copy-start.96
  222.6 5.7 copy-start.102
  233.1 149.5 %copy-start.107 = (f32[256]{0:T(256)}, f32[256]{0:T(256)S(1)}, u32[]{:S(2)}) copy-start(f32[256]{0:T(256)S(1)} %add_rsqrt_fusion.2) | copy-start | bytes 3076
  397.9 434.1 %reduce-scatter.3.cloned.1.call-start = ((), (), s32[]{:S(2)}) async-start(), calls=%async_computation.4 | async-start | bytes 1310720 | tf_op jit(solution)/shard_map/reduce_scatter | solution.py:1490
  412.1 29.7 %copy-start.38 = (bf16[256,2,6,128]{0,3,2,1:T(8,128)(2,1)}, bf16[256,2,6,128]{0,3,2,1:T(8,128)(2,1)S(1)}, u32[]{:S(2)}) copy-start(bf16[256,2,6,128]{0,3,2,1:T(8,128)(2,1)S(1)} %fusion.23) | copy-start | bytes 2359300
  441.8 4.7 copy-start.84
  444.0 4.6 copy-start.1
  751.7 8.5 copy-start.85
  751.7 17.8 %slice-start.3 = ((s8[12582912]{0:T(1024)(128)(4,1)}), s8[4194304]{0:T(1024)(128)(4,1)S(1)}, s32[]{:S(2)}) async-start(s8[12582912]{0:T(1024)(128)(4,1)} %bitcast.485), calls=%async_computation.9 | async-start | bytes 8388608
  751.7 17.8 %slice-start.4 = ((s8[12582912]{0:T(1024)(128)(4,1)}), s8[4194304]{0:T(1024)(128)(4,1)S(1)}, s32[]{:S(2)}) async-start(s8[12582912]{0:T(1024)(128)(4,1)} %bitcast.485), calls=%async_computation.10 | async-start | bytes 8388608
  760.2 9.3 slice-start.5
  769.5 6.7 copy-start.39
  779.9 319.7 %reduce-scatter.5.cloned.1.call-start = ((), (), s32[]{:S(2)}) async-start(), calls=%async_computation.5 | async-start | bytes 1310720 | tf_op jit(solution)/shard_map/reduce_scatter | solution.py:1490
  809.0 26.9 %copy-start.34 = (f32[256,128]{0,1:T(8,128)S(1)}, f32[256,128]{0,1:T(8,128)}, u32[]{:S(2)}) copy-start(f32[256,128]{0,1:T(8,128)} %copy-done.32) | copy-start | bytes 393220
  846.5 176.0 %copy-start.6 = (f32[256,1536]{1,0:T(8,128)S(1)}, f32[256,1536]{1,0:T(8,128)}, u32[]{:S(2)}) copy-start(f32[256,1536]{1,0:T(8,128)} %copy-done.5) | copy-start | bytes 4718596
  846.5 176.0 %copy-start.101 = (f32[1536]{0:T(1024)S(1)}, f32[1536]{0:T(1024)}, u32[]{:S(2)}) copy-start(f32[1536]{0:T(1024)} %copy-done.100) | copy-start | bytes 18436
  846.5 176.0 %copy-start.108 = (f32[256]{0:T(256)S(1)}, f32[256]{0:T(256)}, u32[]{:S(2)}) copy-start(f32[256]{0:T(256)} %copy-done.107) | copy-start | bytes 3076
  1031.4 8.3 copy-start.83
  1031.4 17.7 %slice-start = ((s8[12582912]{0:T(1024)(128)(4,1)}), s8[4194304]{0:T(1024)(128)(4,1)S(1)}, s32[]{:S(2)}) async-start(s8[12582912]{0:T(1024)(128)(4,1)} %bitcast.483), calls=%async_computation.6 | async-start | bytes 8388608
  1031.5 17.6 %slice-start.1 = ((s8[12582912]{0:T(1024)(128)(4,1)}), s8[4194304]{0:T(1024)(128)(4,1)S(1)}, s32[]{:S(2)}) async-start(s8[12582912]{0:T(1024)(128)(4,1)} %bitcast.483), calls=%async_computation.7 | async-start | bytes 8388608
  1039.7 9.4 slice-start.2
  1049.1 6.8 copy-start.37
  1086.1 14.8 %copy-start.35 = (f32[256,128]{0,1:T(8,128)S(1)}, f32[256,128]{0,1:T(8,128)}, u32[]{:S(2)}) copy-start(f32[256,128]{0,1:T(8,128)} %copy-done.32) | copy-start | bytes 393220
  1257.1 6.3 copy-start.94
  (90 other events, 204.0 us)
Sparse Core Ops, SparseCore 0:
  190.4 26.0 all-gather.2
  398.1 42.4 all-gather.4
  780.0 51.9 reduce-scatter.2
  1061.5 38.0 reduce-scatter.4

commit v5 on v4

--- a/solution.py
+++ b/solution.py
@@ -43,12 +43,6 @@
     return tensor * cosine + turned * sine_table
 
 
-def rotate_back(tensor, cosine, sine_table):
-    half = tensor.shape[-1] // 2
-    moved = tensor * sine_table
-    return tensor * cosine + jnp.concatenate([moved[..., half:], -moved[..., :half]], -1)
-
-
 def dot(pattern, left, right):
     return jnp.einsum(pattern, left, right, preferred_element_type=f32)
 
@@ -56,13 +50,6 @@
 def rms_parts(resid):
     scale = lax.rsqrt(jnp.mean(resid * resid, axis=1, keepdims=True) + epsilon)
     return resid * scale, scale
-
-
-def norm_backward(grad_normed, normed, scale, gain):
-    grad_gain = jnp.sum(grad_normed * normed, axis=0)
-    scaled = grad_normed * gain
-    project = jnp.mean(scaled * normed, axis=1, keepdims=True)
-    return scale * (scaled - normed * project), grad_gain
 
 
 def split_columns(blocks, sizes):
@@ -71,13 +58,6 @@
         out.append(blocks[:, :, start : start + size].reshape(blocks.shape[0], -1))
         start += size
     return out
-
-
-def turn(tokens_major):
-    count, width = tokens_major.shape
-    devices = lax.axis_size("gx")
-    blocks = tokens_major.T.reshape(devices // 2, 2, width // devices, count)
-    return blocks.transpose(1, 0, 2, 3).reshape(2, width // 2, count)
 
 
 def score_block(q_rot, k_rot, allowed):
@@ -704,7 +684,8 @@
 
 
 class Reduce:
-    def __init__(self, lhs, rhs, bufs, abuf, fbuf, ftail, a_all, r_all, c_all, outs, sems):
+    def __init__(self, lhs, rhs, bufs, abuf, fbuf, ftail, a_all, r_all, c_all, outs, late, sems):
+        self.late = late
         self.lhs, self.rhs, self.bufs, self.outs = lhs, rhs, bufs, outs
         self.abuf, self.fbuf, self.ftail = abuf, fbuf, ftail
         self.a_all, self.r_all, self.c_all = a_all, r_all, c_all
@@ -784,9 +765,17 @@
             mine = self.product(m, self.core, at)
             fetch.wait()
             self.bufs[m][self.half :, at] = (mine + landed[...].astype(f32)).astype(bf16)
-        if self.four:
+        if m in self.late:
+            self.keep(m).start()
+        elif self.four:
             for h in range(2):
                 self.corner(m, h).start()
+
+    def keep(self, m):
+        kept = self.outs[m]
+        return pltpu.make_async_copy(
+            self.bufs[m].at[pl.ds(self.half, self.half)], kept, self.local.at[max(len(self.near), 2)]
+        )
 
     def hand(self, m, k):
         target = self.near[k]
@@ -859,7 +848,137 @@
         dma((count, 2)),
         dma((count, near)),
         dma((count, near)),
-        dma((near,)),
+        dma((max(near, 2) + 1,)),
+    ]
+
+
+class Tail:
+    def __init__(self, b_all, r_all, c_all, outs, abuf, fbuf, ftail, sems):
+        self.b_all, self.r_all, self.c_all, self.outs = b_all, r_all, c_all, outs
+        self.abuf, self.fbuf, self.ftail = abuf, fbuf, ftail
+        self.r_send, self.r_recv, self.c_send, self.c_recv, self.local = sems
+        gx, self.gy = lax.axis_index("gx"), lax.axis_index("gy")
+        self.chip, chips = gx // 2, lax.axis_size("gx") // 2
+        self.r = b_all.shape[1] // chips
+        self.part = self.r // 2
+        self.space = b_all.shape[1] // b_all.shape[0]
+        self.four = chips == 4
+        self.near = list(square()[:2]) if self.four else places()[1]
+
+    def remote(self, src, dst, send, recv, target):
+        return pltpu.make_async_remote_copy(
+            src_ref=src,
+            dst_ref=dst,
+            send_sem=send,
+            recv_sem=recv,
+            device_id=(target, self.gy),
+            device_id_type=MESH,
+        )
+
+    def held(self, i, chip, h):
+        first = pl.multiple_of(chip * self.r + h * self.part, 16)
+        return self.b_all.at[i, pl.ds(first, self.part)]
+
+    def slot(self, i, k):
+        return self.abuf.at[pl.ds(i * self.space + k * self.part, self.part)]
+
+    def corner(self, i, h):
+        side, along, across = square()
+        return self.remote(
+            self.held(i, across // 2, h),
+            self.r_all.at[i, h],
+            self.r_send.at[i, h],
+            self.r_recv.at[i, h],
+            along if h else side,
+        )
+
+    def hand(self, i, k, h):
+        target = self.near[k]
+        summed = self.four and k != h
+        return self.remote(
+            self.slot(i, 2 + h) if summed else self.held(i, target // 2, h),
+            self.c_all.at[i, k, h],
+            self.c_send.at[i, k, h],
+            self.c_recv.at[i, k, h],
+            target,
+        )
+
+    def hands(self):
+        return [(k, h) for k in range(len(self.near)) for h in range(2)]
+
+    def begin(self, i):
+        if self.four:
+            for h in range(2):
+                self.corner(i, h).start()
+
+    def middle(self, i):
+        if self.four:
+            side, along, _ = square()
+            for h, device in ((0, along), (1, side)):
+                self.corner(i, h).wait_recv()
+                came, mine = self.slot(i, h), self.slot(i, 2 + h)
+                fetches = [
+                    pltpu.make_async_copy(self.r_all.at[i, h], came, self.local.at[0]),
+                    pltpu.make_async_copy(self.held(i, device // 2, h), mine, self.local.at[1]),
+                ]
+                for fetch in fetches:
+                    fetch.start()
+                for fetch in fetches:
+                    fetch.wait()
+                mine[...] = (mine[...].astype(f32) + came[...].astype(f32)).astype(bf16)
+        for k, h in self.hands():
+            self.hand(i, k, h).start()
+
+    def close(self, i):
+        if self.four:
+            for h in range(2):
+                self.corner(i, h).wait_send()
+        for k, h in self.hands():
+            self.hand(i, k, h).wait_send()
+        count = len(self.near)
+        for h in range(2):
+            fetches = [
+                pltpu.make_async_copy(
+                    self.held(i, self.chip, h), self.slot(i, count), self.local.at[count]
+                )
+            ]
+            for k in range(count):
+                self.hand(i, k, h).wait_recv()
+                fetches.append(
+                    pltpu.make_async_copy(
+                        self.c_all.at[i, k, h], self.slot(i, k), self.local.at[k]
+                    )
+                )
+            for fetch in fetches:
+                fetch.start()
+            for fetch in fetches:
+                fetch.wait()
+            for start, width in spans(self.abuf.shape[1]):
+                at = slice(start, start + width)
+                total = self.slot(i, 0)[:, at].astype(f32)
+                for k in range(1, count + 1):
+                    total = total + self.slot(i, k)[:, at].astype(f32)
+                stage = self.fbuf if width == FF_CHUNK else self.ftail
+                stage[: self.part] = total
+                store = pltpu.make_async_copy(
+                    stage.at[pl.ds(0, self.part)],
+                    self.outs[i].at[pl.ds(h * self.part, self.part), at],
+                    self.local.at[0],
+                )
+                store.start()
+                store.wait()
+
+
+def tail_scratch(count):
+    devices = lax.axis_size("gx")
+    near = 2 if devices == 8 else devices // 2 - 1
+    dma = pltpu.SemaphoreType.DMA
+    return [
+        dma((count, 2)),
+        dma((count, 2)),
+        dma((count, near, 2)),
+        dma((count, near, 2)),
+        dma((near + 1,)),
     ]
 
 
@@ -875,20 +994,39 @@
         turned[k % 2, q * r : (q + 1) * r, at] = flipped[k * r : (k + 1) * r]
 
 
-AFTER = (
-    ("hop", 0, "first", 0),
-    ("hop", 1, "second", 0),
-    ("hop", 1, "first", 1),
-    ("hop", 2, "third", 0),
-    ("hop", 2, "second", 1),
-)
-
-
-def backward_kernel(
-    grad_ref, gate_ref, up_ref, hidden_ref, turned_ref, wg_ref, wu_ref, wd_ref, *refs
-):
-    sum_ref, og, ou, od, a_all, r_all, c_all = refs[:7]
-    scratch = refs[7:]
+AFTER = {
+    0: (("first", 0),),
+    1: (("second", 0), ("swap", 0), ("first", 1)),
+    2: (("third", 0), ("second", 1)),
+}
+WHOLE_END = (("first", 2), ("third", 1), ("second", 2), ("fourth", 0), ("third", 2))
+WHOLE_END += (("fourth", 1), ("fourth", 2), ("drain", 0), ("drain", 1), ("drain", 2))
+LATE_END = (("kept", 1), ("first", 2), ("second", 2), ("fourth", 0), ("kept", 2))
+LATE_END += (("sent", 1), ("sent", 2), ("drain", 0))
+
+
+TAIL_BEGIN, TAIL_MIDDLE = ("step", 0), ("step", 2)
+
+
+def both(one, other):
+    def act():
+        one()
+        other()
+
+    return act
+
+
+def backward_kernel(late, tails, *refs):
+    grad_ref, gate_ref, up_ref, hidden_ref, turned_ref, wg_ref, wu_ref, wd_ref = refs[:8]
+    held, refs = refs[8 : 8 + (tails > 0)], refs[8 + (tails > 0) :]
+    sum_ref, refs = refs[0], refs[1:]
+    if late:
+        od, b_all, a_all, r_all, c_all = refs[:5]
+        outs, refs = (od, b_all.at[0], b_all.at[1]), refs[5:]
+    else:
+        og, ou, od, a_all, r_all, c_all = refs[:6]
+        outs, refs = (od, og, ou), refs[6:]
+    tail_refs, scratch = refs[: tails + 2 * (tails > 0)], refs[tails + 2 * (tails > 0) :]
     gathered, part, outb, inb = scratch[:4]
     sems = scratch[4:LINE]
     wg, wu, wd, gate, up, hidden, turned, w_sem = scratch[LINE : LINE + 8]
@@ -921,9 +1059,22 @@
         a_all,
         r_all,
         c_all,
-        (od, og, ou),
-        scratch[LINE + 11 :],
+        outs,
+        late,
+        scratch[LINE + 11 : LINE + 18],
     )
+    tail = None
+    if tails:
+        tail = Tail(
+            held[0],
+            tail_refs[tails],
+            tail_refs[tails + 1],
+            tail_refs[:tails],
+            abuf,
+            fbuf,
+            ftail,
+            scratch[LINE + 18 :],
+        )
 
     def finish(b):
         block = gathered[b]
@@ -945,66 +1096,85 @@
             else:
                 part[...] += p
 
-    def swap_operand():
-        copy = pltpu.make_async_copy(turned_ref, turned, w_sem.at[0])
-        copy.start()
-        copy.wait()
-
-    def work(when):
+    def run(verb, m):
+        if verb == "swap":
+            copy = pltpu.make_async_copy(turned_ref, turned, w_sem.at[0])
+            copy.start()
+            copy.wait()
+        elif verb == "kept":
+            reduce.keep(m).wait()
+        elif verb == "sent":
+            for j, at in reduce.columns():
+                reduce.swap(m, j, at).wait_send()
+        else:
+            getattr(reduce, verb)(m)
+
+    def work(t):
         def act():
-            for name, t, verb, m in AFTER:
-                if t == when:
-                    getattr(reduce, verb)(m)
-                    if verb == "second" and m == 0:
-                        swap_operand()
+            if tail is not None and t == 1:
+                for i in range(tails):
+                    tail.close(i)
+            for verb, m in AFTER[t]:
+                run(verb, m)
+
+        return act
+
+    def each(verb):
+        def act():
+            for i in range(tails):
+                getattr(tail, verb)(i)
 
         return act
 
     peers = [reduce.partner] + reduce.near
     plan = {("hop", t): work(t) for t in range(3)}
+    if tails:
+        for key, act in ((TAIL_BEGIN, each("begin")), (TAIL_MIDDLE, each("middle"))):
+            old = plan.get(key)
+            plan[key] = act if old is None else both(act, old)
     line_pass(grad_ref, sum_ref, gathered, part, outb, inb, sems, load, finish, peers, plan)
-    reduce.first(2)
-    reduce.third(1)
-    reduce.second(2)
-    reduce.fourth(0)
-    reduce.third(2)
-    reduce.fourth(1)
-    reduce.fourth(2)
-    for m in range(3):
-        reduce.drain(m)
-
-
-def backward_ffn(grad, gate, up, hidden, turned, wg, wu, wd):
+    for verb, m in LATE_END if late else WHOLE_END:
+        run(verb, m)
+
+
+def backward_ffn(grad, gate, up, hidden, turned, wg, wu, wd, late=False, held=None):
     rows, width = grad.shape
     devices, size, wide = lax.axis_size("gx"), lax.axis_size("gy"), wg.shape[1]
     near = 2 if devices == 8 else devices // 2 - 1
-    mine = jax.ShapeDtypeStruct((width // devices, wide), f32)
+    r = width // devices
+    mine = jax.ShapeDtypeStruct((r, wide), f32)
+
+    def between(*dims):
+        return jax.ShapeDtypeStruct(dims + (wide,), bf16)
+
+    count = 1 if late else 3
+    out = [jax.ShapeDtypeStruct((rows, width), f32)]
+    out += [mine, between(2, width // 2)] if late else [mine] * 3
+    out += [between(3, width // 2), between(count, 2, r // 2), between(count, near, r)]
+    tails = 0 if held is None else held.shape[0]
+    if tails:
+        out += [mine] * tails
+        out += [between(tails, 2, r // 2), between(tails, near, 2, r // 2)]
+    extra = [held] if tails else []
     return pl.pallas_call(
-        backward_kernel,
-        out_shape=[
-            jax.ShapeDtypeStruct((rows, width), f32),
-            mine,
-            mine,
-            mine,
-            jax.ShapeDtypeStruct((3, width // 2, wide), bf16),
-            jax.ShapeDtypeStruct((3, 2, width // devices // 2, wide), bf16),
-            jax.ShapeDtypeStruct((3, near, width // devices, wide), bf16),
-        ],
-        in_specs=[ANY] * 8,
-        out_specs=[pl.BlockSpec(memory_space=pltpu.VMEM)] + [ANY] * 6,
+        functools.partial(backward_kernel, (1, 2) if late else (), tails),
+        out_shape=out,
+        in_specs=[ANY] * (8 + len(extra)),
+        out_specs=[pl.BlockSpec(memory_space=pltpu.VMEM)] + [ANY] * (len(out) - 1),
         scratch_shapes=line_scratch(size, rows, width)
         + [pltpu.VMEM((width, wide), bf16)] * 3
         + [pltpu.VMEM((size, rows, wide), bf16)] * 3
         + [pltpu.VMEM((2, width // 2, size * rows), bf16), pltpu.SemaphoreType.DMA((6,))]
-        + reduce_scratch(width, wide),
+        + reduce_scratch(width, wide)
+        + (tail_scratch(tails) if tails else []),
         compiler_params=pltpu.CompilerParams(
-            collective_id=1, has_side_effects=True, vmem_limit_bytes=VMEM_LIMIT
+            collective_id=1 if late else 5, has_side_effects=True, vmem_limit_bytes=VMEM_LIMIT
         ),
         cost_estimate=pl.CostEstimate(
             flops=12 * size * rows * width * wide, bytes_accessed=40 << 20, transcendentals=0
         ),
         name="ffn_backward",
-    )(grad, gate, up, hidden, turned, wg, wu, wd)
+    )(grad, gate, up, hidden, turned, wg, wu, wd, *extra)
 
 
 class Fold:
@@ -1327,6 +1497,197 @@
     )(*operands, small, out_rows, grad_rows)
 
 
+def swing(value, cosine, turned_sine):
+    return value * cosine + pltpu.roll(value, HEAD_DIM // 2, 1) * turned_sine
+
+
+def tile_columns(value, tables):
+    heads = value.shape[1] // HEAD_DIM
+    parts = [swing(value[:, k * HEAD_DIM : (k + 1) * HEAD_DIM], *tables) for k in range(heads)]
+    return jnp.concatenate(parts, axis=1)
+
+
+def store_split(block, turned):
+    width = block.shape[1]
+    devices = lax.axis_size("gx")
+    r = width // devices
+    flipped = block.T
+    for k in range(devices):
+        q = k // 2
+        turned[k % 2, q * r : (q + 1) * r] = flipped[k * r : (k + 1) * r]
+
+
+def norm_pull(grad, normed, scale, gain):
+    row = jnp.sum(grad * normed, axis=0, keepdims=True)
+    scaled = grad * gain
+    project = jnp.mean(scaled * normed, axis=1, keepdims=True)
+    return row, scale * (scaled - normed * project)
+
+
+def attention_pull_kernel(*refs):
+    (grad, grad_ffn, norm_b, scale_b, gain_b, norm_a, scale_a, gain_a) = refs[:8]
+    acts, q, k, v, lse, cosine, sine, qkv_ref, out_ref = refs[8:17]
+    grad_out, grad_low, acts_turned, branch_turned, gqkv, small = refs[17:23]
+    qkv, wout, heads, branch, dq, dk_sum, dv_sum, kv_out, kv_in, total = refs[23:33]
+    w_sem, kv_send, kv_recv = refs[33:]
+    gx, me, size = lax.axis_index("gx"), lax.axis_index("gy"), lax.axis_size("gy")
+    count, rows = q.shape[0], k.shape[0]
+    loads = [
+        pltpu.make_async_copy(out_ref, wout, w_sem.at[0]),
+        pltpu.make_async_copy(qkv_ref, qkv, w_sem.at[1]),
+    ]
+    for load in loads:
+        load.start()
+    greet([], [lax.rem(me + d, size) for d in range(1, size)])
+    small[...] = jnp.zeros_like(small)
+    row, pulled = norm_pull(grad_ffn[...], norm_b[...], scale_b[...], gain_b[...])
+    small[1:2] = row
+    branch[...] = grad[...] + pulled
+    low = branch[...].astype(bf16)
+    store_split(low, branch_turned)
+    store_split(acts[...], acts_turned)
+    loads[0].wait()
+    cq = wout.shape[2]
+    heads[...] = jnp.concatenate([nn(low, wout[z]) for z in range(size)], axis=1).astype(bf16)
+
+    query = me * count + lax.broadcasted_iota(jnp.int32, (rows, count), 1)
+    key = lax.broadcasted_iota(jnp.int32, (rows, count), 0)
+    allowed = key <= query
+    if rows > LEN:
+        allowed = jnp.logical_and(allowed, key // LEN == query // LEN)
+    factor = 1.0 / math.sqrt(HEAD_DIM)
+    tables = (cosine[...], sine[...])
+
+    def kv_copy(g, d):
+        target = lax.rem(me + d, size)
+        return pltpu.make_async_remote_copy(
+            src_ref=kv_out.at[g, target],
+            dst_ref=kv_in.at[g, me],
+            send_sem=kv_send.at[g, d],
+            recv_sem=kv_recv.at[g, me],
+            device_id=(gx, target),
+            device_id_type=MESH,
+        )
+
+    for g in range(KV_HEADS):
+        span = slice(g * HEAD_DIM, (g + 1) * HEAD_DIM)
+        kg, vg = k[:, span], v[:, span]
+        turned_k = kg.T
+        dk_sum[...] = jnp.zeros_like(dk_sum)
+        dv_sum[...] = jnp.zeros_like(dv_sum)
+
+        def head(i, carry):
+            h = g * GROUP + i
+            at = pl.ds(pl.multiple_of(h * HEAD_DIM, HEAD_DIM), HEAD_DIM)
+            qh, dh = q[:, at], heads[:, at]
+            scores = jnp.where(allowed, nt(kg, qh) * factor, -1e30)
+            p = jnp.exp(scores - lse[pl.ds(h, 1), :])
+            dp = nt(vg, dh)
+            inner = jnp.sum(p * dp, axis=0, keepdims=True)
+            ds = (p * (dp - inner)).astype(bf16)
+            dv_sum[...] += nn(p.astype(bf16), dh)
+            dk_sum[...] += nn(ds, qh)
+            dq[:, at] = swing(nn(turned_k, ds).T * factor, *tables).astype(bf16)
+            return carry
+
+        lax.fori_loop(0, GROUP, head, 0)
+        for z in range(size):
+            at = slice(z * count, (z + 1) * count)
+            kv_out[g, z, :, :HEAD_DIM] = (dk_sum[at] * factor).astype(bf16)
+            kv_out[g, z, :, HEAD_DIM:] = dv_sum[at].astype(bf16)
+        for d in range(1, size):
+            kv_copy(g, d).start()
+
+    loads[1].wait()
+    apart = cq % HEAD_DIM == 0
+    if apart:
+        for z in range(size):
+            p = nt(dq[:, z * cq : (z + 1) * cq], qkv[z, :, :cq])
+            if z == 0:
+                total[...] = p
+            else:
+                total[...] += p
+    dks, dvs = [], []
+    for g in range(KV_HEADS):
+        summed = kv_out[g, me].astype(f32)
+        for d in range(1, size):
+            z = lax.rem(me + d, size)
+            wait_for(kv_in.at[g, z], kv_recv.at[g, z])
+            summed = summed + kv_in[g, z].astype(f32)
+        dks.append(swing(summed[:, :HEAD_DIM], *tables).astype(bf16).astype(f32))
+        dvs.append(summed[:, HEAD_DIM:].astype(bf16).astype(f32))
+    dk, dv = jnp.concatenate(dks, axis=1), jnp.concatenate(dvs, axis=1)
+    ck = dk.shape[1] // size
+    for z in range(size):
+        at = slice(z * ck, (z + 1) * ck)
+        kv = jnp.concatenate([dk[:, at], dv[:, at]], axis=1)
+        if apart:
+            kv = kv.astype(bf16)
+            gqkv[z, :, :cq] = dq[:, z * cq : (z + 1) * cq]
+            gqkv[z, :, cq:] = kv
+            total[...] += nt(kv, qkv[z, :, cq:])
+        else:
+            mine = dq[:, z * cq : (z + 1) * cq].astype(f32)
+            gqkv[z] = jnp.concatenate([mine, kv], axis=1).astype(bf16)
+            p = nt(gqkv[z], qkv[z])
+            if z == 0:
+                total[...] = p
+            else:
+                total[...] += p
+    row, pulled = norm_pull(total[...], norm_a[...], scale_a[...], gain_a[...])
+    small[0:1] = row
+    small[2:3] = jnp.sum(dq[...].astype(f32), axis=0, keepdims=True)
+    width = dk.shape[1]
+    small[3:4, :width] = jnp.sum(dk, axis=0, keepdims=True)
+    small[4:5, :width] = jnp.sum(dv, axis=0, keepdims=True)
+    final = branch[...] + pulled
+    grad_out[...] = final
+    grad_low[...] = final.astype(bf16)
+    for g in range(KV_HEADS):
+        for d in range(1, size):
+            kv_copy(g, d).wait_send()
+
+
+def attention_pull(vectors, acts, q, k, v, lse, tables, qkv, wout):
+    count, width = acts.shape
+    size, rows = lax.axis_size("gy"), k.shape[0]
+    local = pl.BlockSpec(memory_space=pltpu.VMEM)
+    vmem, dma = pltpu.VMEM, pltpu.SemaphoreType.DMA
+    turned = jax.ShapeDtypeStruct((2, width // 2, count), bf16)
+    return pl.pallas_call(
+        attention_pull_kernel,
+        out_shape=[
+            jax.ShapeDtypeStruct((count, width), f32),
+            jax.ShapeDtypeStruct((count, width), bf16),
+            turned,
+            turned,
+            jax.ShapeDtypeStruct((size, count, qkv.shape[2]), bf16),
+            jax.ShapeDtypeStruct((8, width), f32),
+        ],
+        in_specs=[local] * 15 + [ANY] * 2,
+        out_specs=[local] * 6,
+        scratch_shapes=[
+            vmem(qkv.shape, bf16),
+            vmem(wout.shape, bf16),
+            vmem((count, width), bf16),
+            vmem((count, width), f32),
+            vmem((count, width), bf16),
+            vmem((rows, HEAD_DIM), f32),
+            vmem((rows, HEAD_DIM), f32),
+            vmem((KV_HEADS, size, count, 2 * HEAD_DIM), bf16),
+            vmem((KV_HEADS, size, count, 2 * HEAD_DIM), bf16),
+            vmem((count, width), f32),
+            dma((2,)),
+            dma((KV_HEADS, size)),
+            dma((KV_HEADS, size)),
+        ],
+        compiler_params=pltpu.CompilerParams(
+            collective_id=6, has_side_effects=True, vmem_limit_bytes=VMEM_LIMIT
+        ),
+        name="attention_pull",
+    )(*vectors, acts, q, k, v, lse, *tables, qkv, wout)
+
+
 def on_device(
     residual_in,
     w_query,
@@ -1389,6 +1750,7 @@
         keys = keys + bias_k[l]
         values = (values + bias_v[l]).astype(bf16)
         q_rot = rotate(queries.reshape(count, HEADS, HEAD_DIM), cosine, sine).astype(bf16)
+        q_flat = q_rot.reshape(count, -1)
         q_rot = q_rot.reshape(count, KV_HEADS, GROUP, HEAD_DIM)
         k_rot = rotate(keys.reshape(count, KV_HEADS, HEAD_DIM), cosine, sine).astype(bf16)
         both = jnp.concatenate([k_rot.reshape(count, -1), values], axis=1)
@@ -1422,10 +1784,10 @@
                 normed_one,
                 scale_one,
                 acts_one,
-                q_rot,
-                k_rot,
-                v_heads,
-                log_total,
+                q_flat,
+                both[:, :half],
+                both[:, half:],
+                log_total.reshape(HEADS, count),
                 mixed,
                 normed_two,
                 scale_two,
@@ -1438,6 +1800,12 @@
         resid = middle + part
 
     grad = cot.astype(f32).T + 2.0 * penalty * resid
+    grad_low = grad.astype(bf16)
+    side = cosine[:, 0, : HEAD_DIM // 2], sine[:, 0, : HEAD_DIM // 2]
+    tables = (
+        jnp.concatenate([side[0], side[0]], axis=1),
+        jnp.concatenate([side[1], -side[1]], axis=1),
+    )
     attn_grads = [None] * LAYERS
     ffn_grads = [None] * LAYERS
     small_grads = [None] * LAYERS
@@ -1461,62 +1829,27 @@
         ) = kept[l]
         w_qkv, w_out = attn_full[l]
         wg, wu, wd = ffn_full[l]
-        done = backward_ffn(grad.astype(bf16), gate, up, hidden, acts_two, wg, wu, wd)
-        grad_acts_two, ffn_grads[l] = done[0], done[1:4]
-        grad_norm, grad_gain_two = norm_backward(
-            grad_acts_two, normed_two, scale_two, gains_two[l]
-        )
-        grad_mid = grad + grad_norm
-        grad_branch = grad_mid.astype(bf16)
-        grad_mixed = jnp.concatenate(
-            [dot("td,dq->tq", grad_branch, w_out[z]) for z in range(devices_y)], axis=1
-        ).astype(bf16)
-        grad_heads = grad_mixed.reshape(count, KV_HEADS, GROUP, HEAD_DIM)
-        scores = score_block(q_rot, k_rot, allowed)
-        soft_full = jnp.exp(scores - log_total)
-        soft = soft_full.astype(bf16)
-        grad_soft = dot("qkgd,skd->kgqs", grad_heads, v_heads)
-        inner = jnp.sum(soft_full * grad_soft, axis=-1, keepdims=True)
-        grad_scores = (soft_full * (grad_soft - inner)).astype(bf16)
-        grad_values = dot("kgqs,qkgd->skd", soft, grad_heads)
-        factor = 1.0 / math.sqrt(HEAD_DIM)
-        grad_qrot = dot("kgqs,skd->qkgd", grad_scores, k_rot) * factor
-        grad_krot = dot("kgqs,qkgd->skd", grad_scores, q_rot) * factor
-        grad_q = rotate_back(grad_qrot.reshape(count, HEADS, HEAD_DIM), cosine, sine)
-        grad_q = grad_q.reshape(count, -1).astype(bf16)
-        both = jnp.concatenate(
-            [grad_krot.reshape(rows_tok, -1), grad_values.reshape(rows_tok, -1)], axis=1
-        ).astype(bf16)
-        both = lax.psum_scatter(both, "gy", scatter_dimension=0, tiled=True).astype(f32)
-        half = both.shape[1] // 2
-        grad_k = rotate_back(both[:, :half].reshape(count, KV_HEADS, HEAD_DIM), cosine, sine)
-        grad_k = grad_k.reshape(count, -1).astype(bf16)
-        grad_v = both[:, half:].astype(bf16)
-        grad_qkv = jnp.concatenate(
-            [g.reshape(count, devices_y, -1) for g in (grad_q, grad_k, grad_v)], axis=2
-        ).transpose(1, 0, 2)
-        grad_acts_one = dot("tq,dq->td", grad_qkv[0], w_qkv[0])
-        for z in range(1, devices_y):
-            grad_acts_one = grad_acts_one + dot("tq,dq->td", grad_qkv[z], w_qkv[z])
-        attn_grads[l] = [
-            turn(acts_one),
-            turn(grad_branch),
-            grad_qkv,
-            mixed.transpose(1, 0, 2),
-        ]
-        grad_norm, grad_gain_one = norm_backward(
-            grad_acts_one, normed_one, scale_one, gains_one[l]
-        )
-        grad = grad_mid + grad_norm
+        operands = (grad_low, gate, up, hidden, acts_two, wg, wu, wd)
+        if l == LAYERS - 1:
+            done = backward_ffn(*operands, late=True)
+            grad_down, held = done[1:3]
+        else:
+            done = backward_ffn(*operands, held=held)
+            ffn_grads[l] = done[1:4]
+            ffn_grads[l + 1] = [*done[7:9], grad_down]
+        grad_acts_two = done[0]
+        vectors = [grad, grad_acts_two, normed_two, scale_two, gains_two[l][None]]
+        vectors += [normed_one, scale_one, gains_one[l][None]]
+        done = attention_pull(
+            vectors, acts_one, q_rot, k_rot, v_heads, log_total, tables, w_qkv, w_out
+        )
+        grad, grad_low = done[:2]
+        attn_grads[l] = [*done[2:5], mixed.transpose(1, 0, 2)]
+        rows = done[5]
+        width = k_rot.shape[1]
         small_grads[l] = [
             v.reshape(devices_y, -1)
-            for v in (
-                grad_gain_one,
-                grad_gain_two,
-                jnp.sum(grad_q.astype(f32), axis=0),
-                jnp.sum(grad_k.astype(f32), axis=0),
-                jnp.sum(grad_v.astype(f32), axis=0),
-            )
+            for v in (rows[0], rows[1], rows[2], rows[3, :width], rows[4, :width])
         ]
     small = jnp.stack([jnp.concatenate(v, axis=1) for v in small_grads], axis=1)
     small = jnp.pad(small, ((0, 0), (0, 8 - LAYERS), (0, 0)))
@@ -1528,7 +1861,7 @@
         return blocks.transpose(1, 0, 2).reshape(-1, rows_tok).astype(f32)
 
     attn_sums, small, output, grad_input = closing(
-        attn_grads[0] + attn_grads[1], small, to_rows(resid), to_rows(grad)
+        attn_grads[0] + attn_grads[1], small, to_rows(resid), to_rows(grad_low)
     )
     small = small[:LAYERS]
     attn_out, start = [], 0

time: 1290 us -> 1240 us (0.961)
  Pallas kernels: 903 us -> 989 us
  matrix products: 80.8 us -> 27.7 us
  waiting for transfers between devices: 66.4 us -> 20 us
  other arithmetic: 93.9 us -> 65.1 us
    pallas_call x2 -> x4, Pallas kernels: 348 us -> 438 us  [the longest x2 340 us: backward_ffn(): pl.pallas_call(functools.partial(backward_kernel, (1, 2) if late else (),...]
    dot_general x44 -> x20, matrix products: 80.8 us -> 27.7 us  [dot(): return jnp.einsum(pattern, left, right, preferred_element_type=f32)]
    reduce_scatter x2 -> x0, waiting for transfers between devices: 36.5 us -> none  [on_device(): lax.psum_scatter(both, 'gy', scatter_dimension=0, tiled=True).astype(f32)]
    convert_element_type x10 -> x1, other arithmetic: 31.7 us -> 4.11 us  [on_device(): grad_low = grad.astype(bf16)]
    unnamed x244 -> x154, local copies, waits for them, and re-layouts: 36.6 us -> 14.2 us
    transpose x6 -> x0, local copies, waits for them, and re-layouts: 13.5 us -> none  [the longest x3 7.17 us: turn(): blocks = tokens_major.T.reshape(devices // 2, 2, width // devices, count)]
  transfers between devices with their start and end apart: 4 -> 2, of which waited for: 4 -> 1; matrix products, arithmetic and copies ran while one was open for 7% -> 5% of each run, Pallas kernels for 0% -> 0%
where the time goes in v5:
time: 1240 us; the launch traced here: 1230 us
  Pallas kernels  989 us (80%)
  local copies, waits for them, and re-layouts  111 us (9%)
  other arithmetic  65.1 us (5%)
  matrix products  27.7 us (2%)
  waiting for transfers between devices  20 us (2%)
  between operations  15.4 us (1%)
    pallas_call x2, Pallas kernels, backward_ffn(): pl.pallas_call(functools.partial(backward_kernel, (1, 2) if late else (),...  340 us
    pallas_call x2, Pallas kernels, forward_ffn(): pl.pallas_call(functools.partial(forward_kernel, extra), out_shape=[jax.S...  247 us
    pallas_call x1, Pallas kernels, opening(): pl.pallas_call(opening_kernel, out_shape=out, in_specs=[ANY] * 10, out_sp...  162 us
    pallas_call x1, Pallas kernels, closing(): pl.pallas_call(functools.partial(closing_kernel, layers), out_shape=[jax....  142 us
    pallas_call x2, Pallas kernels, attention_pull(): pl.pallas_call(attention_pull_kernel, out_shape=[jax.ShapeDtypeStruct((co...  97.8 us
    dot_general x20, matrix products, dot(): return jnp.einsum(pattern, left, right, preferred_element_type=f32)  27.7 us
  transfers between devices with their start and end apart: 2, of which 1 were waited for; matrix products, arithmetic and copies ran while one was open for 5% of the time, Pallas kernels for 0%

profile of v5, /device:TPU:9, one launch (start us, length us, event | category | flops | bytes accessed | tf_op | source)
XLA Modules:
  0.0 1228.5 jit_solution(11599974526456051603)
XLA Ops:
  13.7 161.6 %opening.1 = (bf16[4,384,256]{2,1,0:T(8,128)(2,1)}, bf16[4,384,256]{2,1,0:T(8,128)(2,1)}, f32[4,8,1280]{2,1,0:T(8,128)}, bf16[4,192,512]{2,1,0:T(8,128)(2,1)}, b...) custom-call(bf16[384,1024]{1,0:T(8,128)(2,1)} %refs_0_.1, ...), custom_call_target="tpu_custom_call" | custom-call | tf_op jit(solution)/shard_map/opening/pallas_call | solution.py:363
  180.6 3.2 fusion.46
  208.8 2.3 pad_maximum_fusion.6
  225.3 2.8 copy.132
  229.3 3.0 copy.89
  233.0 3.1 copy.117
  240.1 4.6 fusion.48
  244.7 2.2 fusion.52
  251.0 3.8 fusion.2
  254.8 2.5 fusion
  257.4 4.1 fusion.12
  268.0 145.9 %ffn_forward.2 = (f32[256,1536]{1,0:T(8,128)}, bf16[2,768,1024]{2,1,0:T(8,128)(2,1)}, bf16[4,256,2240]{2,1,0:T(8,128)(2,1)}, bf16[4,256,2240]{2,1,0:T(8,128)(2,1...) custom-call(bf16[256,1536]{1,0:T(8,128)(2,1)} %get-tuple-element.168, ...), custom_call_target="tpu_custom_call" | custom-call | flops 21139292160 | bytes 41943040 | tf_op jit(solution)/shard_map/ffn_forward/pallas_call | solution.py:658
  415.6 3.8 fusion.45
  434.8 2.9 copy.131
  437.7 2.1 maximum_multiply_fusion.3
  439.8 3.2 copy.91
  448.9 5.0 fusion.47
  455.3 2.1 add_convert_fusion
  457.4 20.0 %all-gather.5.cloned.1.call-done = bf16[1024,512]{1,0:T(8,128)(2,1)} async-done(((bf16[256,512]{1,0:T(8,128)(2,1)}), bf16[1024,512]{1,0:T(8,128)(2,1)}) %all-gather.5.cloned.1.call-update) | async-done | bytes 1048592 | tf_op jit(solution)/shard_map/all_gather | solution.py:1757
  477.4 2.2 fusion.51
  481.6 3.4 fusion.3
  485.0 3.0 fusion.1
  490.4 6.8 fusion.11
  504.6 101.4 %ffn_forward.3 = (f32[256,1536]{1,0:T(8,128)}, bf16[2,768,1024]{2,1,0:T(8,128)(2,1)}, bf16[4,256,2240]{2,1,0:T(8,128)(2,1)}, bf16[4,256,2240]{2,1,0:T(8,128)(2,1)}, bf16[4,256,2240]{2,1,0:T(8,128)(2,1)}) custom-call(bf16[256,1536]{1,0:T(8,128)(2,1)} %get-tuple-element.162.refs_0_, bf16[1536,2240]{1,0:T(8,128)(2,1)} %bitcast.336, ...), custom_call_target="tpu_custom_call" | custom-call | flops 21139292160 | bytes 41943040 | tf_op jit(solution)/shard_map/ffn_forward/pallas_call | solution.py:658
  606.0 4.1 fusion.44
  610.1 141.2 %ffn_backward.2 = (f32[256,1536]{1,0:T(8,128)}, f32[192,2240]{1,0:T(8,128)}, bf16[2,768,2240]{2,1,0:T(8,128)(2,1)}, bf16[3,768,2240]{2,1,0:T(8,128)(2,1)}, bf16[...) custom-call(bf16[256,1536]{1,0:T(8,128)(2,1)} %get-tuple-element.160.refs_0_, ...), custom_call_target="tpu_custom_call" | custom-call | flops 42278584320 | bytes 41943040 | tf_op jit(solution)/shard_map/ffn_backward/pallas_call | solution.py:1159
  751.3 49.9 %attention_pull.2 = (f32[256,1536]{1,0:T(8,128)}, bf16[256,1536]{1,0:T(8,128)(2,1)}, bf16[2,768,256]{2,1,0:T(8,128)(2,1)}, bf16[2,768,256]{2,1,0:T(8,128)(2,1)},...) custom-call(f32[256,1536]{1,0:T(8,128)} %get-tuple-element.161.refs_0_, f32[256,1536]{1,0:T(8,128)} %get-tuple-element.84.refs_1_, ...), custom_call_target="tpu_custom_call" | custom-call | tf_op jit(solution)/shard_map/attention_pull/pallas_call | solution.py:1657
  801.2 199.1 %ffn_backward.3 = (f32[256,1536]{1,0:T(8,128)}, f32[192,2240]{1,0:T(8,128)}, f32[192,2240]{1,0:T(8,128)}, f32[192,2240]{1,0:T(8,128)}, bf16[3,768,2240]{2,1,0:T(...) custom-call(bf16[256,1536]{1,0:T(8,128)(2,1)} %get-tuple-element.86., ...), custom_call_target="tpu_custom_call" | custom-call | flops 42278584320 | bytes 41943040 | tf_op jit(solution)/shard_map/ffn_backward/pallas_call | solution.py:1159
  1000.3 47.9 %attention_pull.3 = (f32[256,1536]{1,0:T(8,128)}, bf16[256,1536]{1,0:T(8,128)(2,1)}, bf16[2,768,256]{2,1,0:T(8,128)(2,1)}, bf16[2,768,256]{2,1,0:T(8,128)(2,1)},...) custom-call(f32[256,1536]{1,0:T(8,128)} %get-tuple-element.85.refs_0_, f32[256,1536]{1,0:T(8,128)} %get-tuple-element.92.refs_1_, ...), custom_call_target="tpu_custom_call" | custom-call | tf_op jit(solution)/shard_map/attention_pull/pallas_call | solution.py:1657
  1056.6 141.9 %closing.1 = (f32[2,192,896]{2,1,0:T(8,128)}, f32[8,1280]{1,0:T(8,128)}, bf16[4,384,256]{2,1,0:T(8,128)(2,1)}, bf16[4,384,256]{2,1,0:T(8,128)(2,1)}) custom-call(bf16[2,768,256]{2,1,0:T(8,128)(2,1)} %get-tuple-element.93.refs_0_, bf16[2,768,256]{2,1,0:T(8,128)(2,1)} %get-tuple-element.94.refs_1_, bf16[4,256,512]{2,1,0:T(8,128)(2,1)} %get-tuple-element.95.refs_2_, ...), custom_call_target="tpu_custom_call" | custom-call | tf_op jit(solution)/shard_map/closing/pallas_call | solution.py:1455
  1198.5 2.4 fusion.49
  1211.9 4.2 pad_maximum_fusion.2
  (309 shorter events, 127.2 us)
Async XLA Ops:
  7.2 4.9 copy-start.70
  7.2 4.9 copy-start.71
  7.2 4.9 copy-start.72
  7.2 4.9 copy-start.68
  7.2 4.9 copy-start.69
  7.2 237.5 %all-gather.3.cloned.1.call-start = ((), (), s32[]{:S(2)}) async-start(), calls=%async_computation | async-start | bytes 1310720 | tf_op jit(solution)/shard_map/all_gather | solution.py:1757
  206.6 4.5 copy-start.34
  208.5 268.9 %all-gather.5.cloned.1.call-start = ((), (), s32[]{:S(2)}) async-start(), calls=%async_computation.1 | async-start | bytes 1310720 | tf_op jit(solution)/shard_map/all_gather | solution.py:1757
  213.1 4.5 copy-start.41
  217.7 10.3 copy-start.19
  220.1 4.5 copy-start.65
  233.0 4.6 copy-start.60
  233.0 5.6 copy-start.56
  257.4 4.1 copy-start.50
  448.9 5.1 copy-start.13
  448.9 5.1 copy-start.14
  448.9 5.1 copy-start.15
  448.9 5.8 copy-start.16
  448.9 6.4 copy-start.17
  448.9 6.4 copy-start.52
  448.9 6.4 copy-start.53
  457.4 24.2 %copy-start.10 = (f32[256,12,64]{0,2,1:T(8,128)S(1)}, f32[256,12,64]{0,2,1:T(8,128)}, u32[]{:S(2)}) copy-start(f32[256,12,64]{0,2,1:T(8,128)} %get-tuple-element.195) | copy-start | bytes 2359300
  457.4 24.2 %copy-start.12 = (f32[256,12,64]{0,2,1:T(8,128)S(1)}, f32[256,12,64]{0,2,1:T(8,128)}, u32[]{:S(2)}) copy-start(f32[256,12,64]{0,2,1:T(8,128)} %get-tuple-element.196) | copy-start | bytes 2359300
  485.0 4.6 copy-start
  485.0 5.2 copy-start.28
  490.4 6.9 copy-start.4
  490.4 6.9 copy-start.24
  1000.3 51.5 %copy-start.30 = (bf16[2,128,6,256]{3,1,2,0:T(8,128)(2,1)S(1)}, bf16[2,128,6,256]{3,1,2,0:T(8,128)(2,1)}, u32[]{:S(2)}) copy-start(bf16[2,128,6,256]{3,1,2,0:T(8,128)(2,1)} %copy-done.29) | copy-start | bytes 2359300
  1048.3 5.3 copy-start.44
  1198.5 6.3 copy-start.46
  1211.9 4.2 copy-start.39
  1211.9 4.2 copy-start.40
  (43 other events, 105.5 us)
Sparse Core Ops, SparseCore 0:
  208.6 27.0 all-gather.2
  434.8 42.5 all-gather.4

commit v6 on v5

--- a/solution.py
+++ b/solution.py
@@ -32,37 +32,9 @@
     cosine = jnp.cos(angles)
     sine_table = jnp.sin(angles)
     return (
-        jnp.concatenate([cosine, cosine], -1)[:, None, :],
-        jnp.concatenate([sine_table, sine_table], -1)[:, None, :],
+        jnp.concatenate([cosine, cosine], -1),
+        jnp.concatenate([sine_table, -sine_table], -1),
     )
-
-
-def rotate(tensor, cosine, sine_table):
-    half = tensor.shape[-1] // 2
-    turned = jnp.concatenate([-tensor[..., half:], tensor[..., :half]], -1)
-    return tensor * cosine + turned * sine_table
-
-
-def dot(pattern, left, right):
-    return jnp.einsum(pattern, left, right, preferred_element_type=f32)
-
-
-def rms_parts(resid):
-    scale = lax.rsqrt(jnp.mean(resid * resid, axis=1, keepdims=True) + epsilon)
-    return resid * scale, scale
-
-
-def split_columns(blocks, sizes):
-    out, start = [], 0
-    for size in sizes:
-        out.append(blocks[:, :, start : start + size].reshape(blocks.shape[0], -1))
-        start += size
-    return out
-
-
-def score_block(q_rot, k_rot, allowed):
-    scores = dot("qkgd,skd->kgqs", q_rot, k_rot) * (1.0 / math.sqrt(HEAD_DIM))
-    return jnp.where(allowed, scores, -1e30)
 
 
 def wait_for(ref, sem):
@@ -1688,6 +1660,146 @@
     )(*vectors, acts, q, k, v, lse, *tables, qkv, wout)
 
 
+def greet_line():
+    gx, me, last = lax.axis_index("gx"), lax.axis_index("gy"), lax.axis_size("gy") - 1
+    barrier = pltpu.get_barrier_semaphore()
+
+    @pl.when(me > 0)
+    def _():
+        pl.semaphore_signal(barrier, inc=1, device_id=(gx, me - 1), device_id_type=MESH)
+
+    @pl.when(me < last)
+    def _():
+        pl.semaphore_signal(barrier, inc=1, device_id=(gx, me + 1), device_id_type=MESH)
+
+    pl.semaphore_wait(barrier, jnp.where(jnp.logical_and(me > 0, me < last), 2, 1))
+
+
+def attention_push_kernel(*refs):
+    x, gain_a, gain_b, bq, bk, bv, cosine, sine, qkv_ref, out_ref = refs[:10]
+    middle, norm_a, scale_a, acts_a, q, k_all, v_all, lse = refs[10:18]
+    mixed, norm_b, scale_b, acts_b = refs[18:22]
+    qkv, wout, kv_own, kv_all, flat, w_sem = refs[22:28]
+    me, size = lax.axis_index("gy"), lax.axis_size("gy")
+    count, rows = x.shape[0], k_all.shape[0]
+    loads = [
+        pltpu.make_async_copy(qkv_ref, qkv, w_sem.at[0]),
+        pltpu.make_async_copy(out_ref, wout, w_sem.at[1]),
+    ]
+    for load in loads:
+        load.start()
+    chain = Chain(kv_own, kv_all, refs[28:31])
+    greet_line()
+    value = x[...]
+    scale = lax.rsqrt(jnp.mean(value * value, axis=1, keepdims=True) + epsilon)
+    scale_a[...] = scale
+    norm_a[...] = value * scale
+    acts_a[...] = (norm_a[...] * gain_a[...]).astype(bf16)
+    loads[0].wait()
+    cq, width = wout.shape[2], k_all.shape[1]
+    ck = width // size
+    tables = (cosine[...], sine[...])
+    apart = cq % HEAD_DIM == 0
+    if apart:
+        kv = [nn(acts_a[...], qkv[z, :, cq:]) for z in range(size)]
+    else:
+        both = [nn(acts_a[...], qkv[z]) for z in range(size)]
+        kv = [part[:, cq:] for part in both]
+    keys = jnp.concatenate([part[:, :ck] for part in kv], axis=1) + bk[...]
+    values = jnp.concatenate([part[:, ck:] for part in kv], axis=1) + bv[...]
+    kv_own[:, :width] = tile_columns(keys, tables).astype(bf16)
+    kv_own[:, width:] = values.astype(bf16)
+    chain.begin()
+    if apart:
+        for z in range(size):
+            at = slice(z * cq, (z + 1) * cq)
+            mine = nn(acts_a[...], qkv[z, :, :cq]) + bq[:, at]
+            q[:, at] = tile_columns(mine, tables).astype(bf16)
+            if z:
+                chain.relay(z)
+    else:
+        mine = jnp.concatenate([part[:, :cq] for part in both], axis=1) + bq[...]
+        q[...] = tile_columns(mine, tables).astype(bf16)
+        for t in range(1, size):
+            chain.relay(t)
+    chain.close()
+    k_all[...] = kv_all[:, :, :width].reshape(rows, width)
+    v_all[...] = kv_all[:, :, width:].reshape(rows, width)
+
+    query = me * count + lax.broadcasted_iota(jnp.int32, (rows, count), 1)
+    key = lax.broadcasted_iota(jnp.int32, (rows, count), 0)
+    allowed = key <= query
+    if rows > LEN:
+        allowed = jnp.logical_and(allowed, key // LEN == query // LEN)
+    factor = 1.0 / math.sqrt(HEAD_DIM)
+    for g in range(KV_HEADS):
+        span = slice(g * HEAD_DIM, (g + 1) * HEAD_DIM)
+        kg, turned_v = k_all[:, span], v_all[:, span].T
+
+        def head(i, carry):
+            h = g * GROUP + i
+            at = pl.ds(pl.multiple_of(h * HEAD_DIM, HEAD_DIM), HEAD_DIM)
+            scores = jnp.where(allowed, nt(kg, q[:, at]) * factor, -1e30)
+            top = jnp.max(scores, axis=0, keepdims=True)
+            expo = jnp.exp(scores - top)
+            total = jnp.sum(expo, axis=0, keepdims=True)
+            lse[pl.ds(h, 1), :] = top + jnp.log(total)
+            soft = (expo * (1.0 / total)).astype(bf16)
+            flat[:, at] = nn(turned_v, soft).T.astype(bf16)
+            return carry
+
+        lax.fori_loop(0, GROUP, head, 0)
+    loads[1].wait()
+    middle[...] = x[...]
+    for z in range(size):
+        at = slice(z * cq, (z + 1) * cq)
+        if apart:
+            mixed[z] = flat[:, at]
+        else:
+            mixed[z] = flat[:, at].astype(f32).astype(bf16)
+        middle[...] += nt(mixed[z], wout[z])
+    value = middle[...]
+    scale = lax.rsqrt(jnp.mean(value * value, axis=1, keepdims=True) + epsilon)
+    scale_b[...] = scale
+    norm_b[...] = value * scale
+    acts_b[...] = (norm_b[...] * gain_b[...]).astype(bf16)
+
+
+def attention_push(x, vectors, tables, qkv, wout, rows):
+    count, width = x.shape
+    size = lax.axis_size("gy")
+    kvd = KV_HEADS * HEAD_DIM
+    local = pl.BlockSpec(memory_space=pltpu.VMEM)
+    vmem = pltpu.VMEM
+
+    def shape(*dims, kind=bf16):
+        return jax.ShapeDtypeStruct(dims, kind)
+
+    normed = [shape(count, width, kind=f32), shape(count, 1, kind=f32), shape(count, width)]
+    out = [shape(count, width, kind=f32), *normed, shape(count, HEADS * HEAD_DIM)]
+    out += [shape(rows, kvd), shape(rows, kvd), shape(HEADS, count, kind=f32)]
+    out += [shape(size, count, wout.shape[2]), *normed]
+    return pl.pallas_call(
+        attention_push_kernel,
+        out_shape=out,
+        in_specs=[local] * 8 + [ANY] * 2,
+        out_specs=[local] * 12,
+        scratch_shapes=[
+            vmem(qkv.shape, bf16),
+            vmem(wout.shape, bf16),
+            vmem((count, 2 * kvd), bf16),
+            vmem((size, count, 2 * kvd), bf16),
+            vmem((count, HEADS * HEAD_DIM), bf16),
+            pltpu.SemaphoreType.DMA((2,)),
+        ]
+        + chain_scratch(),
+        compiler_params=pltpu.CompilerParams(
+            collective_id=7, has_side_effects=True, vmem_limit_bytes=VMEM_LIMIT
+        ),
+        name="attention_push",
+    )(x, *vectors, *tables, qkv, wout)
+
+
 def on_device(
     residual_in,
     w_query,
@@ -1708,11 +1820,7 @@
     rows_tok = residual_in.shape[1]
     count = rows_tok // devices_y
     q_index = lax.axis_index("gy") * count + jnp.arange(count, dtype=jnp.int32)
-    k_index = jnp.arange(rows_tok, dtype=jnp.int32)
-    allowed = (q_index[:, None] // LEN == k_index[None, :] // LEN) & (
-        k_index[None, :] <= q_index[:, None]
-    )
-    cosine, sine = rope_tables(q_index % LEN, HEAD_DIM)
+    cos_table, sin_table = rope_tables(q_index % LEN, HEAD_DIM)
 
     small = jnp.concatenate([gain_attn, gain_ffn, b_query, b_key, b_value], axis=1)
     small_sizes = [v.shape[1] for v in (gain_attn, gain_ffn, b_query, b_key, b_value)]
@@ -1740,37 +1848,10 @@
     for l in range(LAYERS):
         w_qkv, w_out = attn_full[l]
         wg, wu, wd = ffn_full[l]
-        normed_one, scale_one = rms_parts(resid)
-        acts_one = (normed_one * gains_one[l]).astype(bf16)
-        queries, keys, values = split_columns(
-            jnp.stack([dot("td,dq->tq", acts_one, w_qkv[z]) for z in range(devices_y)], axis=1),
-            part_sizes,
-        )
-        queries = queries + bias_q[l]
-        keys = keys + bias_k[l]
-        values = (values + bias_v[l]).astype(bf16)
-        q_rot = rotate(queries.reshape(count, HEADS, HEAD_DIM), cosine, sine).astype(bf16)
-        q_flat = q_rot.reshape(count, -1)
-        q_rot = q_rot.reshape(count, KV_HEADS, GROUP, HEAD_DIM)
-        k_rot = rotate(keys.reshape(count, KV_HEADS, HEAD_DIM), cosine, sine).astype(bf16)
-        both = jnp.concatenate([k_rot.reshape(count, -1), values], axis=1)
-        both = lax.all_gather(both, "gy", axis=0, tiled=True)
-        half = both.shape[1] // 2
-        k_rot = both[:, :half].reshape(rows_tok, KV_HEADS, HEAD_DIM)
-        v_heads = both[:, half:].reshape(rows_tok, KV_HEADS, HEAD_DIM)
-        scores = score_block(q_rot, k_rot, allowed)
-        top = jnp.max(scores, axis=-1, keepdims=True)
-        expo = jnp.exp(scores - top)
-        total = jnp.sum(expo, axis=-1, keepdims=True)
-        soft = (expo / total).astype(bf16)
-        log_total = top + jnp.log(total)
-        mixed = dot("kgqs,skd->qkgd", soft, v_heads).reshape(count, -1).astype(bf16)
-        mixed = mixed.reshape(count, devices_y, -1)
-        middle = resid
-        for z in range(devices_y):
-            middle = middle + dot("tq,dq->td", mixed[:, z], w_out[z])
-        normed_two, scale_two = rms_parts(middle)
-        acts_two = (normed_two * gains_two[l]).astype(bf16)
+        vectors = [v[l][None] for v in (gains_one, gains_two, bias_q, bias_k, bias_v)]
+        done = attention_push(resid, vectors, (cos_table, -sin_table), w_qkv, w_out, rows_tok)
+        middle, normed_one, scale_one, acts_one, q_rot, k_rot, v_heads, log_total = done[:8]
+        mixed, normed_two, scale_two, acts_two = done[8:]
         if l == 0:
             shards = (*lines_next, w_gate, w_up, w_down)
             done = forward_ffn(acts_two, wg, wu, wd, shards)
@@ -1784,10 +1865,10 @@
                 normed_one,
                 scale_one,
                 acts_one,
-                q_flat,
-                both[:, :half],
-                both[:, half:],
-                log_total.reshape(HEADS, count),
+                q_rot,
+                k_rot,
+                v_heads,
+                log_total,
                 mixed,
                 normed_two,
                 scale_two,
@@ -1801,11 +1882,6 @@
 
     grad = cot.astype(f32).T + 2.0 * penalty * resid
     grad_low = grad.astype(bf16)
-    side = cosine[:, 0, : HEAD_DIM // 2], sine[:, 0, : HEAD_DIM // 2]
-    tables = (
-        jnp.concatenate([side[0], side[0]], axis=1),
-        jnp.concatenate([side[1], -side[1]], axis=1),
-    )
     attn_grads = [None] * LAYERS
     ffn_grads = [None] * LAYERS
     small_grads = [None] * LAYERS
@@ -1841,10 +1917,10 @@
         vectors = [grad, grad_acts_two, normed_two, scale_two, gains_two[l][None]]
         vectors += [normed_one, scale_one, gains_one[l][None]]
         done = attention_pull(
-            vectors, acts_one, q_rot, k_rot, v_heads, log_total, tables, w_qkv, w_out
+            vectors, acts_one, q_rot, k_rot, v_heads, log_total, (cos_table, sin_table), w_qkv, w_out
         )
         grad, grad_low = done[:2]
-        attn_grads[l] = [*done[2:5], mixed.transpose(1, 0, 2)]
+        attn_grads[l] = [*done[2:5], mixed]
         rows = done[5]
         width = k_rot.shape[1]
         small_grads[l] = [

time: 1240 us -> 1150 us (0.927)
  Pallas kernels: 989 us -> 1080 us
  local copies, waits for them, and re-layouts: 111 us -> 30.5 us
  other arithmetic: 65.1 us -> 24.5 us
  matrix products: 27.7 us -> 0 us
  waiting for transfers between devices: 20 us -> 0 us
  between operations: 15.4 us -> 1.34 us
    pallas_call x0 -> x2, Pallas kernels: none -> 93.1 us  [attention_push(): pl.pallas_call(attention_push_kernel, out_shape=out, in_specs=[local] * 8...]
    dot_general x20 -> x0, matrix products: 27.7 us -> none  [dot(): return jnp.einsum(pattern, left, right, preferred_element_type=f32)]
    slice x14 -> x6, local copies, waits for them, and re-layouts: 29.8 us -> 3.29 us  [on_device(): v[l][None]]
    all_gather x2 -> x0, waiting for transfers between devices: 20 us -> none  [on_device(): both = lax.all_gather(both, 'gy', axis=0, tiled=True)]
    mul x11 -> x0, local copies, waits for them, and re-layouts: 13.8 us -> none  [the longest x7 12 us: rotate(): return tensor * cosine + turned * sine_table]
    reshape x10 -> x0, local copies, waits for them, and re-layouts: 13.8 us -> none  [the longest x6 7.62 us: split_columns(): out.append(blocks[:, :, start:start + size].reshape(blocks.shape[0], -1))]
  transfers between devices with their start and end apart: 2 -> 0, of which waited for: 1 -> 0; matrix products, arithmetic and copies ran while one was open for 5% -> 0% of each run, Pallas kernels for 0% -> 0%
where the time goes in v6:
time: 1150 us; the launch traced here: 1140 us
  Pallas kernels  1080 us (94%)
  local copies, waits for them, and re-layouts  30.5 us (3%)
  other arithmetic  24.5 us (2%)
    pallas_call x2, Pallas kernels, backward_ffn(): pl.pallas_call(functools.partial(backward_kernel, (1, 2) if late else (),...  337 us
    pallas_call x2, Pallas kernels, forward_ffn(): pl.pallas_call(functools.partial(forward_kernel, extra), out_shape=[jax.S...  245 us
    pallas_call x1, Pallas kernels, opening(): pl.pallas_call(opening_kernel, out_shape=out, in_specs=[ANY] * 10, out_sp...  162 us
    pallas_call x1, Pallas kernels, closing(): pl.pallas_call(functools.partial(closing_kernel, layers), out_shape=[jax....  141 us
    pallas_call x2, Pallas kernels, attention_pull(): pl.pallas_call(attention_pull_kernel, out_shape=[jax.ShapeDtypeStruct((co...  102 us
    pallas_call x2, Pallas kernels, attention_push(): pl.pallas_call(attention_push_kernel, out_shape=out, in_specs=[local] * 8...  93.1 us

profile of v6, /device:TPU:9, one launch (start us, length us, event | category | flops | bytes accessed | tf_op | source)
XLA Modules:
  0.0 1136.8 jit_solution(15346843982956724188)
XLA Ops:
  4.2 1.0 slice_bitcast_fusion.1
  7.4 0.9 fusion.4
  8.2 161.6 %opening.1 = (bf16[4,384,256]{2,1,0:T(8,128)(2,1)}, bf16[4,384,256]{2,1,0:T(8,128)(2,1)}, f32[4,8,1280]{2,1,0:T(8,128)}, bf16[4,192,512]{2,1,0:T(8,128)(2,1)}, b...) custom-call(bf16[384,1024]{1,0:T(8,128)(2,1)} %refs_0_.1, ...), custom_call_target="tpu_custom_call" | custom-call | tf_op jit(solution)/shard_map/opening/pallas_call | solution.py:335
  169.9 0.9 slice_bitcast_fusion.4
  174.1 1.2 bitcast_convert_fusion.1
  175.8 1.2 bitcast_convert_fusion
  177.1 1.6 copy.53
  178.7 38.1 %attention_push.2 = (f32[256,1536]{1,0:T(8,128)}, f32[256,1536]{1,0:T(8,128)}, f32[256,1]{1,0:T(8,128)}, bf16[256,1536]{1,0:T(8,128)(2,1)}, bf16[256,1536]{1,0:T...) custom-call(f32[256,1536]{1,0:T(8,128)} %bitcast.67, ...), custom_call_target="tpu_custom_call" | custom-call | tf_op jit(solution)/shard_map/attention_push/pallas_call | solution.py:1782
  216.8 145.7 %ffn_forward.2 = (f32[256,1536]{1,0:T(8,128)}, bf16[2,768,1024]{2,1,0:T(8,128)(2,1)}, bf16[4,256,2240]{2,1,0:T(8,128)(2,1)}, bf16[4,256,2240]{2,1,0:T(8,128)(2,1...) custom-call(bf16[256,1536]{1,0:T(8,128)(2,1)} %get-tuple-element.93., ...), custom_call_target="tpu_custom_call" | custom-call | flops 21139292160 | bytes 41943040 | tf_op jit(solution)/shard_map/ffn_forward/pallas_call | solution.py:630
  362.5 3.2 add.36.refs_0_
  365.7 55.0 %attention_push.3 = (f32[256,1536]{1,0:T(8,128)}, f32[256,1536]{1,0:T(8,128)}, f32[256,1]{1,0:T(8,128)}, bf16[256,1536]{1,0:T(8,128)(2,1)}, bf16[256,1536]{1,0:T...) custom-call(f32[256,1536]{1,0:T(8,128)} %add.36.refs_0_, ...), custom_call_target="tpu_custom_call" | custom-call | tf_op jit(solution)/shard_map/attention_push/pallas_call | solution.py:1782
  420.7 99.6 %ffn_forward.3 = (f32[256,1536]{1,0:T(8,128)}, bf16[2,768,1024]{2,1,0:T(8,128)(2,1)}, bf16[4,256,2240]{2,1,0:T(8,128)(2,1)}, bf16[4,256,2240]{2,1,0:T(8,128)(2,1)}, bf16[4,256,2240]{2,1,0:T(8,128)(2,1)}) custom-call(bf16[256,1536]{1,0:T(8,128)(2,1)} %get-tuple-element.103.refs_0_, bf16[1536,2240]{1,0:T(8,128)(2,1)} %bitcast.97, bf16[1536,2240]{1,0:T(8,128)(2,1)} %bitcast.99, ...), custom_call_target="tpu_custom_call" | custom-call | flops 21139292160 | bytes 41943040 | tf_op jit(solution)/shard_map/ffn_forward/pallas_call | solution.py:630
  520.3 4.1 fusion.3
  524.3 140.4 %ffn_backward.2 = (f32[256,1536]{1,0:T(8,128)}, f32[192,2240]{1,0:T(8,128)}, bf16[2,768,2240]{2,1,0:T(8,128)(2,1)}, bf16[3,768,2240]{2,1,0:T(8,128)(2,1)}, bf16[...) custom-call(bf16[256,1536]{1,0:T(8,128)(2,1)} %get-tuple-element.202.refs_0_, ...), custom_call_target="tpu_custom_call" | custom-call | flops 42278584320 | bytes 41943040 | tf_op jit(solution)/shard_map/ffn_backward/pallas_call | solution.py:1131
  664.7 53.5 %attention_pull.2 = (f32[256,1536]{1,0:T(8,128)}, bf16[256,1536]{1,0:T(8,128)(2,1)}, bf16[2,768,256]{2,1,0:T(8,128)(2,1)}, bf16[2,768,256]{2,1,0:T(8,128)(2,1)},...) custom-call(f32[256,1536]{1,0:T(8,128)} %get-tuple-element.203.refs_0_, f32[256,1536]{1,0:T(8,128)} %get-tuple-element.112.refs_1_, ...), custom_call_target="tpu_custom_call" | custom-call | tf_op jit(solution)/shard_map/attention_pull/pallas_call | solution.py:1629
  718.2 196.8 %ffn_backward.3 = (f32[256,1536]{1,0:T(8,128)}, f32[192,2240]{1,0:T(8,128)}, f32[192,2240]{1,0:T(8,128)}, f32[192,2240]{1,0:T(8,128)}, bf16[3,768,2240]{2,1,0:T(...) custom-call(bf16[256,1536]{1,0:T(8,128)(2,1)} %get-tuple-element.123, ...), custom_call_target="tpu_custom_call" | custom-call | flops 42278584320 | bytes 41943040 | tf_op jit(solution)/shard_map/ffn_backward/pallas_call | solution.py:1131
  915.0 48.5 %attention_pull.3 = (f32[256,1536]{1,0:T(8,128)}, bf16[256,1536]{1,0:T(8,128)(2,1)}, bf16[2,768,256]{2,1,0:T(8,128)(2,1)}, bf16[2,768,256]{2,1,0:T(8,128)(2,1)},...) custom-call(f32[256,1536]{1,0:T(8,128)} %get-tuple-element.122.refs_0_, f32[256,1536]{1,0:T(8,128)} %get-tuple-element.129.refs_1_, ...), custom_call_target="tpu_custom_call" | custom-call | tf_op jit(solution)/shard_map/attention_pull/pallas_call | solution.py:1629
  963.5 3.5 pad_maximum_fusion
  967.8 1.0 slice_reduce_fusion.3
  969.8 1.0 slice_reduce_fusion
  971.9 2.3 copy.45
  974.2 1.2 copy.44
  975.3 141.4 %closing.1 = (f32[2,192,896]{2,1,0:T(8,128)}, f32[8,1280]{1,0:T(8,128)}, bf16[4,384,256]{2,1,0:T(8,128)(2,1)}, bf16[4,384,256]{2,1,0:T(8,128)(2,1)}) custom-call(bf16[2,768,256]{2,1,0:T(8,128)(2,1)} %get-tuple-element.139.refs_0_, bf16[2,768,256]{2,1,0:T(8,128)(2,1)} %get-tuple-element.140.refs_1_, bf16[4,256,512]{2,1,0:T(8,128)(2,1)} %get-tuple-element.141.refs_2_, ...), custom_call_target="tpu_custom_call" | custom-call | tf_op jit(solution)/shard_map/closing/pallas_call | solution.py:1427
  1116.8 1.4 fusion.10
  1118.2 1.3 fusion.9
  1119.5 1.2 fusion.6
  1120.7 2.3 fusion.5
  1125.2 1.6 copy.48
  1126.8 1.3 convert_bitcast_fusion
  1128.6 1.6 copy.49
  1130.2 4.2 pad_maximum_fusion.2
  1134.4 2.0 pad_maximum_fusion.1
  (54 shorter events, 14.9 us)
Async XLA Ops:
  0.6 5.4 copy-start.5
  915.0 48.5 %copy-start.3 = (f32[192,2240]{1,0:T(8,128)S(1)}, f32[192,2240]{1,0:T(8,128)}, u32[]{:S(2)}) copy-start(f32[192,2240]{1,0:T(8,128)} %get-tuple-element.154) | copy-start | bytes 5160964
  967.0 7.2 copy-start
  1119.5 5.1 copy-start.4
  1130.2 4.2 copy-start.1
  1130.2 4.2 copy-start.2

commit v7 on v6

--- a/solution.py
+++ b/solution.py
@@ -266,10 +266,10 @@
 
 
 def opening_kernel(*refs):
-    ins, outs, sems = refs[:10], refs[10:22], refs[22:]
-    resid, cot, small, qkv_a, o_a, qkv_b, o_b, wg, wu, wd = ins
+    ins, outs, sems = refs[:9], refs[9:20], refs[20:]
+    resid, cot, small, qkv_a, o_a, qkv_b, o_b, wg, wu = ins
     resid_out, cot_out, small_out = outs[:3]
-    lines, (qkv, o, gate, up, down) = outs[3:7], outs[7:]
+    lines, (qkv, o, gate, up) = outs[3:7], outs[7:]
     me, size = lax.axis_index("gy"), lax.axis_size("gy")
     owns = (qkv_a, o_a, qkv_b, o_b, small)
     chains = [
@@ -280,7 +280,7 @@
         Exchange(own, full, sems[15 + 3 * k : 18 + 3 * k])
         for k, (own, full) in enumerate(((resid, resid_out), (cot, cot_out)))
     ]
-    items = [(lines[0], qkv), (lines[1], o), (wg.at[0], gate), (wu.at[0], up), (wd.at[0], down)]
+    items = [(lines[0], qkv), (lines[1], o), (wg.at[0], gate), (wu.at[0], up)]
     spread = Spread(items, sems[21:24])
     greet([spread.partner] + spread.near, [lax.rem(me + d, size) for d in range(1, size)])
     for k in (0, 1, 4):
@@ -296,31 +296,28 @@
     swaps[0].begin()
     for t in range(1, size):
         chains[4].relay(t)
+    spread.relay(2)
     spread.begin(3)
     chains[2].begin()
     chains[3].begin()
-    spread.relay(2)
+    for i in (0, 1):
+        spread.relay(i)
+    swaps[1].begin()
     for t in range(1, size):
         chains[2].relay(t)
         chains[3].relay(t)
-    spread.begin(4)
-    swaps[1].begin()
-    for i in (0, 1):
-        spread.relay(i)
     spread.finish(2)
-    spread.relay(3)
     for i in (0, 1):
         spread.finish(i)
-    spread.relay(4)
-    for i in (3, 4):
-        spread.finish(i)
-    for i in range(5):
+    spread.relay(3)
+    spread.finish(3)
+    for i in range(4):
         spread.close(i)
     for part in chains[2:] + swaps:
         part.close()
 
 
-def opening(resid, cot, small, lines, wg, wu, wd):
+def opening(resid, cot, small, lines, wg, wu):
     devices, size = lax.axis_size("gx"), lax.axis_size("gy")
     count = resid.shape[1] // size
 
@@ -331,16 +328,16 @@
     weight = shape(devices, *wg.shape[1:])
     out = [blocks, blocks, shape(size, *small.shape, kind=f32)]
     out += [shape(size, *line.shape) for line in lines]
-    out += [shape(size, devices, *line.shape) for line in lines[:2]] + [weight] * 3
+    out += [shape(size, devices, *line.shape) for line in lines[:2]] + [weight] * 2
     return pl.pallas_call(
         opening_kernel,
         out_shape=out,
-        in_specs=[ANY] * 10,
-        out_specs=[ANY] * 12,
-        scratch_shapes=chain_scratch() * 5 + exchange_scratch() * 2 + spread_scratch(5),
+        in_specs=[ANY] * 9,
+        out_specs=[ANY] * 11,
+        scratch_shapes=chain_scratch() * 5 + exchange_scratch() * 2 + spread_scratch(4),
         compiler_params=pltpu.CompilerParams(collective_id=2, has_side_effects=True),
         name="opening",
-    )(resid, cot, small, *lines, wg, wu, wd)
+    )(resid, cot, small, *lines, wg, wu)
 
 
 FF_CHUNK = 512
@@ -529,9 +526,9 @@
     ("step", 0): (("begin", 0), ("begin", 1)),
     ("step", 2): (("begin", 2),),
     ("hop", 0): (("relay", 0), ("relay", 1), ("relay", 2), ("begin", 3)),
-    ("hop", 1): (("finish", 0), ("finish", 1), ("finish", 2), ("begin", 4)),
+    ("hop", 1): (("finish", 0), ("finish", 1), ("finish", 2)),
 }
-REST = (("relay", 3), ("relay", 4), ("finish", 3), ("finish", 4))
+REST = (("relay", 3), ("finish", 3))
 
 
 def schedule(spread):
@@ -1660,7 +1657,7 @@
     )(*vectors, acts, q, k, v, lse, *tables, qkv, wout)
 
 
-def greet_line():
+def greet_line(gx_peers=()):
     gx, me, last = lax.axis_index("gx"), lax.axis_index("gy"), lax.axis_size("gy") - 1
     barrier = pltpu.get_barrier_semaphore()
 
@@ -1672,10 +1669,23 @@
     def _():
         pl.semaphore_signal(barrier, inc=1, device_id=(gx, me + 1), device_id_type=MESH)
 
-    pl.semaphore_wait(barrier, jnp.where(jnp.logical_and(me > 0, me < last), 2, 1))
-
-
-def attention_push_kernel(*refs):
+    for peer in gx_peers:
+        pl.semaphore_signal(barrier, inc=1, device_id=(peer, me), device_id_type=MESH)
+    count = jnp.where(jnp.logical_and(me > 0, me < last), 2, 1)
+    pl.semaphore_wait(barrier, count + len(gx_peers))
+
+
+PUSH_PLAN = {
+    "chained": ("begin",),
+    "group0": ("relay",),
+    "group1": ("finish",),
+    "end": ("close",),
+}
+
+
+def attention_push_kernel(layer, *refs):
+    shard_ref, whole_ref = refs[10], refs[23]
+    refs = refs[:10] + refs[11:23] + refs[24:]
     x, gain_a, gain_b, bq, bk, bv, cosine, sine, qkv_ref, out_ref = refs[:10]
     middle, norm_a, scale_a, acts_a, q, k_all, v_all, lse = refs[10:18]
     mixed, norm_b, scale_b, acts_b = refs[18:22]
@@ -1689,7 +1699,14 @@
     for load in loads:
         load.start()
     chain = Chain(kv_own, kv_all, refs[28:31])
-    greet_line()
+    spread = Spread([(shard_ref.at[layer], whole_ref)], refs[31:34])
+
+    def move(name):
+        for verb in PUSH_PLAN.get(name, ()):
+            getattr(spread, verb)(0)
+
+    greet_line([spread.partner] + spread.near)
+    move("greeted")
     value = x[...]
     scale = lax.rsqrt(jnp.mean(value * value, axis=1, keepdims=True) + epsilon)
     scale_a[...] = scale
@@ -1710,6 +1727,7 @@
     kv_own[:, :width] = tile_columns(keys, tables).astype(bf16)
     kv_own[:, width:] = values.astype(bf16)
     chain.begin()
+    move("chained")
     if apart:
         for z in range(size):
             at = slice(z * cq, (z + 1) * cq)
@@ -1723,6 +1741,7 @@
         for t in range(1, size):
             chain.relay(t)
     chain.close()
+    move("relayed")
     k_all[...] = kv_all[:, :, :width].reshape(rows, width)
     v_all[...] = kv_all[:, :, width:].reshape(rows, width)
 
@@ -1749,6 +1768,7 @@
             return carry
 
         lax.fori_loop(0, GROUP, head, 0)
+        move("group%d" % g)
     loads[1].wait()
     middle[...] = x[...]
     for z in range(size):
@@ -1763,9 +1783,10 @@
     scale_b[...] = scale
     norm_b[...] = value * scale
     acts_b[...] = (norm_b[...] * gain_b[...]).astype(bf16)
-
-
-def attention_push(x, vectors, tables, qkv, wout, rows):
+    move("end")
+
+
+def attention_push(x, vectors, tables, qkv, wout, rows, shard, layer):
     count, width = x.shape
     size = lax.axis_size("gy")
     kvd = KV_HEADS * HEAD_DIM
@@ -1779,11 +1800,12 @@
     out = [shape(count, width, kind=f32), *normed, shape(count, HEADS * HEAD_DIM)]
     out += [shape(rows, kvd), shape(rows, kvd), shape(HEADS, count, kind=f32)]
     out += [shape(size, count, wout.shape[2]), *normed]
+    out += [shape(lax.axis_size("gx"), *shard.shape[1:])]
     return pl.pallas_call(
-        attention_push_kernel,
+        functools.partial(attention_push_kernel, layer),
         out_shape=out,
-        in_specs=[local] * 8 + [ANY] * 2,
-        out_specs=[local] * 12,
+        in_specs=[local] * 8 + [ANY] * 3,
+        out_specs=[local] * 12 + [ANY],
         scratch_shapes=[
             vmem(qkv.shape, bf16),
             vmem(wout.shape, bf16),
@@ -1792,12 +1814,13 @@
             vmem((count, HEADS * HEAD_DIM), bf16),
             pltpu.SemaphoreType.DMA((2,)),
         ]
-        + chain_scratch(),
+        + chain_scratch()
+        + spread_scratch(1),
         compiler_params=pltpu.CompilerParams(
-            collective_id=7, has_side_effects=True, vmem_limit_bytes=VMEM_LIMIT
+            collective_id=7 + layer, has_side_effects=True, vmem_limit_bytes=VMEM_LIMIT
         ),
         name="attention_push",
-    )(x, *vectors, *tables, qkv, wout)
+    )(x, *vectors, *tables, qkv, wout, shard)
 
 
 def on_device(
@@ -1829,7 +1852,7 @@
     for l in range(LAYERS):
         lines += [jnp.concatenate([w_query[l], w_key[l], w_value[l]], axis=1), w_output[l]]
     part_sizes = (w_query.shape[2], w_key.shape[2], w_value.shape[2])
-    opened = opening(residual_in, cotangent, small, lines, w_gate, w_up, w_down)
+    opened = opening(residual_in, cotangent, small, lines, w_gate, w_up)
     resid, cot, small = opened[:3]
     lines_next = opened[5:7]
     attn_full = [[w.reshape(devices_y, D, -1) for w in opened[7:9]], None]
@@ -1847,13 +1870,17 @@
     kept = []
     for l in range(LAYERS):
         w_qkv, w_out = attn_full[l]
-        wg, wu, wd = ffn_full[l]
         vectors = [v[l][None] for v in (gains_one, gains_two, bias_q, bias_k, bias_v)]
-        done = attention_push(resid, vectors, (cos_table, -sin_table), w_qkv, w_out, rows_tok)
+        done = attention_push(
+            resid, vectors, (cos_table, -sin_table), w_qkv, w_out, rows_tok, w_down, l
+        )
         middle, normed_one, scale_one, acts_one, q_rot, k_rot, v_heads, log_total = done[:8]
-        mixed, normed_two, scale_two, acts_two = done[8:]
+        mixed, normed_two, scale_two, acts_two = done[8:12]
+        wg, wu = ffn_full[l]
+        wd = done[12].reshape(D, -1)
+        ffn_full[l] = (wg, wu, wd)
         if l == 0:
-            shards = (*lines_next, w_gate, w_up, w_down)
+            shards = (*lines_next, w_gate, w_up)
             done = forward_ffn(acts_two, wg, wu, wd, shards)
             attn_full[1] = [w.reshape(devices_y, D, -1) for w in done[5:7]]
             ffn_full[1] = [w.reshape(D, -1) for w in done[7:]]

time: 1150 us -> 1120 us (0.974)
  Pallas kernels: 1080 us -> 1050 us
    pallas_call x2, Pallas kernels: 245 us -> 228 us  [forward_ffn(): pl.pallas_call(functools.partial(forward_kernel, extra), out_shape=[jax.S...]
where the time goes in v7:
time: 1120 us; the launch traced here: 1110 us
  Pallas kernels  1050 us (94%)
  local copies, waits for them, and re-layouts  30.5 us (3%)
  other arithmetic  24.5 us (2%)
    pallas_call x2, Pallas kernels, backward_ffn(): pl.pallas_call(functools.partial(backward_kernel, (1, 2) if late else (),...  336 us
    pallas_call x2, Pallas kernels, forward_ffn(): pl.pallas_call(functools.partial(forward_kernel, extra), out_shape=[jax.S...  228 us
    pallas_call x1, Pallas kernels, closing(): pl.pallas_call(functools.partial(closing_kernel, layers), out_shape=[jax....  142 us
    pallas_call x1, Pallas kernels, opening(): pl.pallas_call(opening_kernel, out_shape=out, in_specs=[ANY] * 9, out_spe...  135 us
    pallas_call x2, Pallas kernels, attention_push(): pl.pallas_call(functools.partial(attention_push_kernel, layer), out_shape...  112 us
    pallas_call x2, Pallas kernels, attention_pull(): pl.pallas_call(attention_pull_kernel, out_shape=[jax.ShapeDtypeStruct((co...  100 us

profile of v7, /device:TPU:9, one launch (start us, length us, event | category | flops | bytes accessed | tf_op | source)
XLA Modules:
  0.0 1109.0 jit_solution(3650242515876899374)
XLA Ops:
  4.2 1.0 slice_bitcast_fusion.1
  7.4 0.9 fusion.4
  8.2 134.6 %opening.1 = (bf16[4,384,256]{2,1,0:T(8,128)(2,1)}, bf16[4,384,256]{2,1,0:T(8,128)(2,1)}, f32[4,8,1280]{2,1,0:T(8,128)}, bf16[4,192,512]{2,1,0:T(8,128)(2,1)}, b...) custom-call(bf16[384,1024]{1,0:T(8,128)(2,1)} %refs_0_.1, ...), custom_call_target="tpu_custom_call" | custom-call | tf_op jit(solution)/shard_map/opening/pallas_call | solution.py:332
  142.8 0.9 slice_bitcast_fusion.4
  147.0 1.2 bitcast_convert_fusion.1
  148.7 1.2 bitcast_convert_fusion
  150.0 1.6 copy.53
  151.6 47.3 %attention_push.2 = (f32[256,1536]{1,0:T(8,128)}, f32[256,1536]{1,0:T(8,128)}, f32[256,1]{1,0:T(8,128)}, bf16[256,1536]{1,0:T(8,128)(2,1)}, bf16[256,1536]{1,0:T...) custom-call(f32[256,1536]{1,0:T(8,128)} %bitcast.65, ...), custom_call_target="tpu_custom_call" | custom-call | tf_op jit(solution)/shard_map/attention_push/pallas_call | solution.py:1804
  198.9 121.3 %ffn_forward.2 = (f32[256,1536]{1,0:T(8,128)}, bf16[2,768,1024]{2,1,0:T(8,128)(2,1)}, bf16[4,256,2240]{2,1,0:T(8,128)(2,1)}, bf16[4,256,2240]{2,1,0:T(8,128)(2,1...) custom-call(bf16[256,1536]{1,0:T(8,128)(2,1)} %get-tuple-element.93., ...), custom_call_target="tpu_custom_call" | custom-call | flops 21139292160 | bytes 41943040 | tf_op jit(solution)/shard_map/ffn_forward/pallas_call | solution.py:627
  320.3 3.2 add.36.refs_0_
  323.5 64.9 %attention_push.3 = (f32[256,1536]{1,0:T(8,128)}, f32[256,1536]{1,0:T(8,128)}, f32[256,1]{1,0:T(8,128)}, bf16[256,1536]{1,0:T(8,128)(2,1)}, bf16[256,1536]{1,0:T...) custom-call(f32[256,1536]{1,0:T(8,128)} %add.36.refs_0_, ...), custom_call_target="tpu_custom_call" | custom-call | tf_op jit(solution)/shard_map/attention_push/pallas_call | solution.py:1804
  388.4 106.6 %ffn_forward.3 = (f32[256,1536]{1,0:T(8,128)}, bf16[2,768,1024]{2,1,0:T(8,128)(2,1)}, bf16[4,256,2240]{2,1,0:T(8,128)(2,1)}, bf16[4,256,2240]{2,1,0:T(8,128)(2,1)}, bf16[4,256,2240]{2,1,0:T(8,128)(2,1)}) custom-call(bf16[256,1536]{1,0:T(8,128)(2,1)} %get-tuple-element.103.refs_0_, bf16[1536,2240]{1,0:T(8,128)(2,1)} %bitcast.99, ...), custom_call_target="tpu_custom_call" | custom-call | flops 21139292160 | bytes 41943040 | tf_op jit(solution)/shard_map/ffn_forward/pallas_call | solution.py:627
  495.0 4.1 fusion.3
  499.1 140.1 %ffn_backward.2 = (f32[256,1536]{1,0:T(8,128)}, f32[192,2240]{1,0:T(8,128)}, bf16[2,768,2240]{2,1,0:T(8,128)(2,1)}, bf16[3,768,2240]{2,1,0:T(8,128)(2,1)}, bf16[...) custom-call(bf16[256,1536]{1,0:T(8,128)(2,1)} %get-tuple-element.202.refs_0_, ...), custom_call_target="tpu_custom_call" | custom-call | flops 42278584320 | bytes 41943040 | tf_op jit(solution)/shard_map/ffn_backward/pallas_call | solution.py:1128
  639.2 51.4 %attention_pull.2 = (f32[256,1536]{1,0:T(8,128)}, bf16[256,1536]{1,0:T(8,128)(2,1)}, bf16[2,768,256]{2,1,0:T(8,128)(2,1)}, bf16[2,768,256]{2,1,0:T(8,128)(2,1)},...) custom-call(f32[256,1536]{1,0:T(8,128)} %get-tuple-element.203.refs_0_, f32[256,1536]{1,0:T(8,128)} %get-tuple-element.112.refs_1_, ...), custom_call_target="tpu_custom_call" | custom-call | tf_op jit(solution)/shard_map/attention_pull/pallas_call | solution.py:1626
  690.6 196.0 %ffn_backward.3 = (f32[256,1536]{1,0:T(8,128)}, f32[192,2240]{1,0:T(8,128)}, f32[192,2240]{1,0:T(8,128)}, f32[192,2240]{1,0:T(8,128)}, bf16[3,768,2240]{2,1,0:T(...) custom-call(bf16[256,1536]{1,0:T(8,128)(2,1)} %get-tuple-element.123, ...), custom_call_target="tpu_custom_call" | custom-call | flops 42278584320 | bytes 41943040 | tf_op jit(solution)/shard_map/ffn_backward/pallas_call | solution.py:1128
  886.6 48.6 %attention_pull.3 = (f32[256,1536]{1,0:T(8,128)}, bf16[256,1536]{1,0:T(8,128)(2,1)}, bf16[2,768,256]{2,1,0:T(8,128)(2,1)}, bf16[2,768,256]{2,1,0:T(8,128)(2,1)},...) custom-call(f32[256,1536]{1,0:T(8,128)} %get-tuple-element.122.refs_0_, f32[256,1536]{1,0:T(8,128)} %get-tuple-element.129.refs_1_, ...), custom_call_target="tpu_custom_call" | custom-call | tf_op jit(solution)/shard_map/attention_pull/pallas_call | solution.py:1626
  935.2 3.5 pad_maximum_fusion
  939.5 1.0 slice_reduce_fusion.3
  941.5 1.0 slice_reduce_fusion
  943.6 2.3 copy.45
  945.9 1.2 copy.44
  947.0 141.9 %closing.1 = (f32[2,192,896]{2,1,0:T(8,128)}, f32[8,1280]{1,0:T(8,128)}, bf16[4,384,256]{2,1,0:T(8,128)(2,1)}, bf16[4,384,256]{2,1,0:T(8,128)(2,1)}) custom-call(bf16[2,768,256]{2,1,0:T(8,128)(2,1)} %get-tuple-element.139.refs_0_, bf16[2,768,256]{2,1,0:T(8,128)(2,1)} %get-tuple-element.140.refs_1_, bf16[4,256,512]{2,1,0:T(8,128)(2,1)} %get-tuple-element.141.refs_2_, ...), custom_call_target="tpu_custom_call" | custom-call | tf_op jit(solution)/shard_map/closing/pallas_call | solution.py:1424
  1089.0 1.4 fusion.10
  1090.4 1.3 fusion.9
  1091.7 1.2 fusion.6
  1092.9 2.3 fusion.5
  1097.4 1.6 copy.48
  1099.0 1.3 convert_bitcast_fusion
  1100.8 1.6 copy.49
  1102.4 4.2 pad_maximum_fusion.2
  1106.6 2.0 pad_maximum_fusion.1
  (54 shorter events, 14.9 us)
Async XLA Ops:
  0.6 5.4 copy-start.5
  886.6 48.6 %copy-start.3 = (f32[192,2240]{1,0:T(8,128)S(1)}, f32[192,2240]{1,0:T(8,128)}, u32[]{:S(2)}) copy-start(f32[192,2240]{1,0:T(8,128)} %get-tuple-element.154) | copy-start | bytes 5160964
  938.7 7.2 copy-start
  1091.7 5.1 copy-start.4
  1102.4 4.2 copy-start.1
  1102.4 4.2 copy-start.2

commit v8 on v7

--- a/solution.py
+++ b/solution.py
@@ -741,7 +741,7 @@
                 self.corner(m, h).start()
 
     def keep(self, m):
-        kept = self.outs[m]
+        kept = self.outs[m].at[0]
         return pltpu.make_async_copy(
             self.bufs[m].at[pl.ds(self.half, self.half)], kept, self.local.at[max(len(self.near), 2)]
         )
@@ -968,12 +968,29 @@
     1: (("second", 0), ("swap", 0), ("first", 1)),
     2: (("third", 0), ("second", 1)),
 }
-WHOLE_END = (("first", 2), ("third", 1), ("second", 2), ("fourth", 0), ("third", 2))
-WHOLE_END += (("fourth", 1), ("fourth", 2), ("drain", 0), ("drain", 1), ("drain", 2))
-LATE_END = (("kept", 1), ("first", 2), ("second", 2), ("fourth", 0), ("kept", 2))
-LATE_END += (("sent", 1), ("sent", 2), ("drain", 0))
-
-
+ENDS = {
+    (1, 2): (
+        ("kept", 1),
+        ("first", 2),
+        ("second", 2),
+        ("fourth", 0),
+        ("kept", 2),
+        ("sent", 1),
+        ("sent", 2),
+        ("drain", 0),
+    ),
+    (2,): (
+        ("first", 2),
+        ("third", 1),
+        ("second", 2),
+        ("fourth", 0),
+        ("kept", 2),
+        ("fourth", 1),
+        ("sent", 2),
+        ("drain", 0),
+        ("drain", 1),
+    ),
+}
 TAIL_BEGIN, TAIL_MIDDLE = ("step", 0), ("step", 2)
 
 
@@ -989,12 +1006,7 @@
     grad_ref, gate_ref, up_ref, hidden_ref, turned_ref, wg_ref, wu_ref, wd_ref = refs[:8]
     held, refs = refs[8 : 8 + (tails > 0)], refs[8 + (tails > 0) :]
     sum_ref, refs = refs[0], refs[1:]
-    if late:
-        od, b_all, a_all, r_all, c_all = refs[:5]
-        outs, refs = (od, b_all.at[0], b_all.at[1]), refs[5:]
-    else:
-        og, ou, od, a_all, r_all, c_all = refs[:6]
-        outs, refs = (od, og, ou), refs[6:]
+    outs, (a_all, r_all, c_all), refs = refs[:3], refs[3:6], refs[6:]
     tail_refs, scratch = refs[: tails + 2 * (tails > 0)], refs[tails + 2 * (tails > 0) :]
     gathered, part, outb, inb = scratch[:4]
     sems = scratch[4:LINE]
@@ -1102,11 +1114,11 @@
             old = plan.get(key)
             plan[key] = act if old is None else both(act, old)
     line_pass(grad_ref, sum_ref, gathered, part, outb, inb, sems, load, finish, peers, plan)
-    for verb, m in LATE_END if late else WHOLE_END:
+    for verb, m in ENDS[late]:
         run(verb, m)
 
 
-def backward_ffn(grad, gate, up, hidden, turned, wg, wu, wd, late=False, held=None):
+def backward_ffn(grad, gate, up, hidden, turned, wg, wu, wd, late, held=None):
     rows, width = grad.shape
     devices, size, wide = lax.axis_size("gx"), lax.axis_size("gy"), wg.shape[1]
     near = 2 if devices == 8 else devices // 2 - 1
@@ -1116,9 +1128,9 @@
     def between(*dims):
         return jax.ShapeDtypeStruct(dims + (wide,), bf16)
 
-    count = 1 if late else 3
+    count = 3 - len(late)
     out = [jax.ShapeDtypeStruct((rows, width), f32)]
-    out += [mine, between(2, width // 2)] if late else [mine] * 3
+    out += [between(1, width // 2) if m in late else mine for m in range(3)]
     out += [between(3, width // 2), between(count, 2, r // 2), between(count, near, r)]
     tails = 0 if held is None else held.shape[0]
     if tails:
@@ -1126,7 +1138,7 @@
         out += [between(tails, 2, r // 2), between(tails, near, 2, r // 2)]
     extra = [held] if tails else []
     return pl.pallas_call(
-        functools.partial(backward_kernel, (1, 2) if late else (), tails),
+        functools.partial(backward_kernel, late, tails),
         out_shape=out,
         in_specs=[ANY] * (8 + len(extra)),
         out_specs=[pl.BlockSpec(memory_space=pltpu.VMEM)] + [ANY] * (len(out) - 1),
@@ -1137,7 +1149,7 @@
         + reduce_scratch(width, wide)
         + (tail_scratch(tails) if tails else []),
         compiler_params=pltpu.CompilerParams(
-            collective_id=1 if late else 5, has_side_effects=True, vmem_limit_bytes=VMEM_LIMIT
+            collective_id=1 if held is None else 5, has_side_effects=True, vmem_limit_bytes=VMEM_LIMIT
         ),
         cost_estimate=pl.CostEstimate(
             flops=12 * size * rows * width * wide, bytes_accessed=40 << 20, transcendentals=0
@@ -1494,11 +1506,14 @@
 
 
 def attention_pull_kernel(*refs):
+    held, (late_grad, r_all, c_all) = refs[17], refs[24:27]
+    refs = refs[:17] + refs[18:24] + refs[27:]
     (grad, grad_ffn, norm_b, scale_b, gain_b, norm_a, scale_a, gain_a) = refs[:8]
     acts, q, k, v, lse, cosine, sine, qkv_ref, out_ref = refs[8:17]
     grad_out, grad_low, acts_turned, branch_turned, gqkv, small = refs[17:23]
     qkv, wout, heads, branch, dq, dk_sum, dv_sum, kv_out, kv_in, total = refs[23:33]
-    w_sem, kv_send, kv_recv = refs[33:]
+    w_sem, kv_send, kv_recv, abuf, fbuf, ftail = refs[33:39]
+    tail = Tail(held, r_all, c_all, [late_grad], abuf, fbuf, ftail, refs[39:])
     gx, me, size = lax.axis_index("gx"), lax.axis_index("gy"), lax.axis_size("gy")
     count, rows = q.shape[0], k.shape[0]
     loads = [
@@ -1507,7 +1522,8 @@
     ]
     for load in loads:
         load.start()
-    greet([], [lax.rem(me + d, size) for d in range(1, size)])
+    greet(tail.near, [lax.rem(me + d, size) for d in range(1, size)])
+    tail.begin(0)
     small[...] = jnp.zeros_like(small)
     row, pulled = norm_pull(grad_ffn[...], norm_b[...], scale_b[...], gain_b[...])
     small[1:2] = row
@@ -1519,6 +1535,7 @@
     cq = wout.shape[2]
     heads[...] = jnp.concatenate([nn(low, wout[z]) for z in range(size)], axis=1).astype(bf16)
 
+    tail.middle(0)
     query = me * count + lax.broadcasted_iota(jnp.int32, (rows, count), 1)
     key = lax.broadcasted_iota(jnp.int32, (rows, count), 0)
     allowed = key <= query
@@ -1612,17 +1629,21 @@
     final = branch[...] + pulled
     grad_out[...] = final
     grad_low[...] = final.astype(bf16)
+    tail.close(0)
     for g in range(KV_HEADS):
         for d in range(1, size):
             kv_copy(g, d).wait_send()
 
 
-def attention_pull(vectors, acts, q, k, v, lse, tables, qkv, wout):
+def attention_pull(vectors, acts, q, k, v, lse, tables, qkv, wout, held):
     count, width = acts.shape
     size, rows = lax.axis_size("gy"), k.shape[0]
     local = pl.BlockSpec(memory_space=pltpu.VMEM)
     vmem, dma = pltpu.VMEM, pltpu.SemaphoreType.DMA
     turned = jax.ShapeDtypeStruct((2, width // 2, count), bf16)
+    devices, wide = lax.axis_size("gx"), held.shape[2]
+    near = 2 if devices == 8 else devices // 2 - 1
+    r = width // devices
     return pl.pallas_call(
         attention_pull_kernel,
         out_shape=[
@@ -1632,9 +1653,12 @@
             turned,
             jax.ShapeDtypeStruct((size, count, qkv.shape[2]), bf16),
             jax.ShapeDtypeStruct((8, width), f32),
+            jax.ShapeDtypeStruct((r, wide), f32),
+            jax.ShapeDtypeStruct((1, 2, r // 2, wide), bf16),
+            jax.ShapeDtypeStruct((1, near, 2, r // 2, wide), bf16),
         ],
-        in_specs=[local] * 15 + [ANY] * 2,
-        out_specs=[local] * 6,
+        in_specs=[local] * 15 + [ANY] * 3,
+        out_specs=[local] * 6 + [ANY] * 3,
         scratch_shapes=[
             vmem(qkv.shape, bf16),
             vmem(wout.shape, bf16),
@@ -1649,12 +1673,16 @@
             dma((2,)),
             dma((KV_HEADS, size)),
             dma((KV_HEADS, size)),
-        ],
+            vmem((width // 4, wide), bf16),
+            vmem((r, FF_CHUNK), f32),
+            vmem((r, wide % FF_CHUNK), f32),
+        ]
+        + tail_scratch(1),
         compiler_params=pltpu.CompilerParams(
             collective_id=6, has_side_effects=True, vmem_limit_bytes=VMEM_LIMIT
         ),
         name="attention_pull",
-    )(*vectors, acts, q, k, v, lse, *tables, qkv, wout)
+    )(*vectors, acts, q, k, v, lse, *tables, qkv, wout, held)
 
 
 def greet_line(gx_peers=()):
@@ -1934,18 +1962,22 @@
         wg, wu, wd = ffn_full[l]
         operands = (grad_low, gate, up, hidden, acts_two, wg, wu, wd)
         if l == LAYERS - 1:
-            done = backward_ffn(*operands, late=True)
-            grad_down, held = done[1:3]
+            done = backward_ffn(*operands, (1, 2))
+            held = done[2]
+            ffn_grads[l] = [None, None, done[1]]
         else:
-            done = backward_ffn(*operands, held=held)
-            ffn_grads[l] = done[1:4]
-            ffn_grads[l + 1] = [*done[7:9], grad_down]
+            done = backward_ffn(*operands, (2,), held_next)
+            ffn_grads[l] = [done[2], None, done[1]]
+            ffn_grads[l + 1][1] = done[7]
+            held = done[3]
+        held_next = done[3]
         grad_acts_two = done[0]
         vectors = [grad, grad_acts_two, normed_two, scale_two, gains_two[l][None]]
         vectors += [normed_one, scale_one, gains_one[l][None]]
         done = attention_pull(
-            vectors, acts_one, q_rot, k_rot, v_heads, log_total, (cos_table, sin_table), w_qkv, w_out
-        )
+            vectors, acts_one, q_rot, k_rot, v_heads, log_total, (cos_table, sin_table), w_qkv, w_out, held
+        )
+        ffn_grads[l][0 if l == LAYERS - 1 else 1] = done[6]
         grad, grad_low = done[:2]
         attn_grads[l] = [*done[2:5], mixed]
         rows = done[5]

time: 1120 us -> 1120 us (level)
    pallas_call x2, Pallas kernels: 336 us -> 300 us  [backward_ffn(): pl.pallas_call(functools.partial(backward_kernel, late, tails), out_shape...]
    pallas_call x2, Pallas kernels: 100 us -> 134 us  [attention_pull(): pl.pallas_call(attention_pull_kernel, out_shape=[jax.ShapeDtypeStruct((co...]
where the time goes in v8:
time: 1120 us; the launch traced here: 1110 us
  Pallas kernels  1050 us (94%)
  local copies, waits for them, and re-layouts  31.7 us (3%)
  other arithmetic  23 us (2%)
    pallas_call x2, Pallas kernels, backward_ffn(): pl.pallas_call(functools.partial(backward_kernel, late, tails), out_shape...  300 us
    pallas_call x2, Pallas kernels, forward_ffn(): pl.pallas_call(functools.partial(forward_kernel, extra), out_shape=[jax.S...  228 us
    pallas_call x1, Pallas kernels, closing(): pl.pallas_call(functools.partial(closing_kernel, layers), out_shape=[jax....  141 us
    pallas_call x1, Pallas kernels, opening(): pl.pallas_call(opening_kernel, out_shape=out, in_specs=[ANY] * 9, out_spe...  135 us
    pallas_call x2, Pallas kernels, attention_pull(): pl.pallas_call(attention_pull_kernel, out_shape=[jax.ShapeDtypeStruct((co...  134 us
    pallas_call x2, Pallas kernels, attention_push(): pl.pallas_call(functools.partial(attention_push_kernel, layer), out_shape...  112 us

profile of v8, /device:TPU:9, one launch (start us, length us, event | category | flops | bytes accessed | tf_op | source)
XLA Modules:
  0.0 1105.8 jit_solution(12807239441873835807)
XLA Ops:
  4.2 1.0 slice_bitcast_fusion.1
  8.2 134.6 %opening.1 = (bf16[4,384,256]{2,1,0:T(8,128)(2,1)}, bf16[4,384,256]{2,1,0:T(8,128)(2,1)}, f32[4,8,1280]{2,1,0:T(8,128)}, bf16[4,192,512]{2,1,0:T(8,128)(2,1)}, b...) custom-call(bf16[384,1024]{1,0:T(8,128)(2,1)} %refs_0_.1, ...), custom_call_target="tpu_custom_call" | custom-call | tf_op jit(solution)/shard_map/opening/pallas_call | solution.py:332
  142.8 0.9 slice_bitcast_fusion.4
  147.0 1.2 bitcast_convert_fusion.1
  148.7 1.2 bitcast_convert_fusion
  150.0 1.6 copy.53
  151.6 47.3 %attention_push.2 = (f32[256,1536]{1,0:T(8,128)}, f32[256,1536]{1,0:T(8,128)}, f32[256,1]{1,0:T(8,128)}, bf16[256,1536]{1,0:T(8,128)(2,1)}, bf16[256,1536]{1,0:T...) custom-call(f32[256,1536]{1,0:T(8,128)} %bitcast.65, ...), custom_call_target="tpu_custom_call" | custom-call | tf_op jit(solution)/shard_map/attention_push/pallas_call | solution.py:1832
  198.9 121.4 %ffn_forward.2 = (f32[256,1536]{1,0:T(8,128)}, bf16[2,768,1024]{2,1,0:T(8,128)(2,1)}, bf16[4,256,2240]{2,1,0:T(8,128)(2,1)}, bf16[4,256,2240]{2,1,0:T(8,128)(2,1...) custom-call(bf16[256,1536]{1,0:T(8,128)(2,1)} %get-tuple-element.95., ...), custom_call_target="tpu_custom_call" | custom-call | flops 21139292160 | bytes 41943040 | tf_op jit(solution)/shard_map/ffn_forward/pallas_call | solution.py:627
  320.3 3.2 add.36.refs_0_
  323.5 64.9 %attention_push.3 = (f32[256,1536]{1,0:T(8,128)}, f32[256,1536]{1,0:T(8,128)}, f32[256,1]{1,0:T(8,128)}, bf16[256,1536]{1,0:T(8,128)(2,1)}, bf16[256,1536]{1,0:T...) custom-call(f32[256,1536]{1,0:T(8,128)} %add.36.refs_0_, ...), custom_call_target="tpu_custom_call" | custom-call | tf_op jit(solution)/shard_map/attention_push/pallas_call | solution.py:1832
  388.5 106.6 %ffn_forward.3 = (f32[256,1536]{1,0:T(8,128)}, bf16[2,768,1024]{2,1,0:T(8,128)(2,1)}, bf16[4,256,2240]{2,1,0:T(8,128)(2,1)}, bf16[4,256,2240]{2,1,0:T(8,128)(2,1)}, bf16[4,256,2240]{2,1,0:T(8,128)(2,1)}) custom-call(bf16[256,1536]{1,0:T(8,128)(2,1)} %get-tuple-element.105.refs_0_, bf16[1536,2240]{1,0:T(8,128)(2,1)} %bitcast.99, ...), custom_call_target="tpu_custom_call" | custom-call | flops 21139292160 | bytes 41943040 | tf_op jit(solution)/shard_map/ffn_forward/pallas_call | solution.py:627
  495.0 4.1 fusion.3
  499.1 140.1 %ffn_backward.2 = (f32[256,1536]{1,0:T(8,128)}, f32[192,2240]{1,0:T(8,128)}, bf16[1,768,2240]{2,1,0:T(8,128)(2,1)}, bf16[1,768,2240]{2,1,0:T(8,128)(2,1)}, bf16[...) custom-call(bf16[256,1536]{1,0:T(8,128)(2,1)} %get-tuple-element.206.refs_0_, ...), custom_call_target="tpu_custom_call" | custom-call | flops 42278584320 | bytes 41943040 | tf_op jit(solution)/shard_map/ffn_backward/pallas_call | solution.py:1140
  639.2 70.7 %attention_pull.2 = (f32[256,1536]{1,0:T(8,128)}, bf16[256,1536]{1,0:T(8,128)(2,1)}, bf16[2,768,256]{2,1,0:T(8,128)(2,1)}, bf16[2,768,256]{2,1,0:T(8,128)(2,1)},...) custom-call(f32[256,1536]{1,0:T(8,128)} %get-tuple-element.207.refs_, ...), custom_call_target="tpu_custom_call" | custom-call | tf_op jit(solution)/shard_map/attention_pull/pallas_call | solution.py:1647
  710.0 159.4 %ffn_backward.3 = (f32[256,1536]{1,0:T(8,128)}, f32[192,2240]{1,0:T(8,128)}, f32[192,2240]{1,0:T(8,128)}, bf16[1,768,2240]{2,1,0:T(8,128)(2,1)}, bf16[3,768,2240...) custom-call(bf16[256,1536]{1,0:T(8,128)(2,1)} %get-tuple-element.126, ...), custom_call_target="tpu_custom_call" | custom-call | flops 42278584320 | bytes 41943040 | tf_op jit(solution)/shard_map/ffn_backward/pallas_call | solution.py:1140
  869.5 63.5 %attention_pull.3 = (f32[256,1536]{1,0:T(8,128)}, bf16[256,1536]{1,0:T(8,128)(2,1)}, bf16[2,768,256]{2,1,0:T(8,128)(2,1)}, bf16[2,768,256]{2,1,0:T(8,128)(2,1)},...) custom-call(f32[256,1536]{1,0:T(8,128)} %get-tuple-element.125.refs_, ...), custom_call_target="tpu_custom_call" | custom-call | tf_op jit(solution)/shard_map/attention_pull/pallas_call | solution.py:1647
  933.8 1.0 slice_reduce_fusion.3
  935.7 1.0 slice_reduce_fusion
  937.9 2.3 copy.45
  940.2 1.2 copy.44
  941.3 141.4 %closing.1 = (f32[2,192,896]{2,1,0:T(8,128)}, f32[8,1280]{1,0:T(8,128)}, bf16[4,384,256]{2,1,0:T(8,128)(2,1)}, bf16[4,384,256]{2,1,0:T(8,128)(2,1)}) custom-call(bf16[2,768,256]{2,1,0:T(8,128)(2,1)} %get-tuple-element.143.refs_0_, bf16[2,768,256]{2,1,0:T(8,128)(2,1)} %get-tuple-element.144.refs_1_, bf16[4,256,512]{2,1,0:T(8,128)(2,1)} %get-tuple-element.145.refs_2_, ...), custom_call_target="tpu_custom_call" | custom-call | tf_op jit(solution)/shard_map/closing/pallas_call | solution.py:1436
  1082.7 1.4 fusion.10
  1084.1 1.3 fusion.9
  1085.4 1.2 fusion.6
  1086.6 2.3 fusion.5
  1091.1 1.6 copy.48
  1092.8 1.3 convert_bitcast_fusion
  1094.5 1.6 copy.49
  1096.1 4.2 pad_maximum_fusion.1
  1100.3 2.0 pad_maximum_fusion
  1102.5 1.1 copy-done.3
  1103.6 2.0 pad_maximum_fusion.2
  (56 shorter events, 15.9 us)
Async XLA Ops:
  0.6 5.4 copy-start.6
  933.0 7.2 copy-start
  1085.4 5.1 copy-start.5
  1096.1 4.2 copy-start.2
  1096.1 4.2 copy-start.4
  1100.3 2.2 copy-start.1
  1100.3 3.3 copy-start.3

commit v9 on v8

--- a/solution.py
+++ b/solution.py
@@ -652,6 +652,29 @@
     )(acts, wg, wu, wd, *shards)
 
 
+def put_rows(totals, out, row, fbuf, ftail, sems, lanes):
+    stores, edge, wide = [], 0, 0
+    for j, make in enumerate(totals):
+        total = make()
+        part, width = total.shape
+        full = width == FF_CHUNK
+        wide += full
+        if full and j >= 2:
+            stores[j - 2].wait()
+        stage = fbuf.at[pl.ds((j % 2) * part, part)] if full else ftail.at[pl.ds(0, part)]
+        stage[...] = total
+        store = pltpu.make_async_copy(
+            stage,
+            out.at[pl.ds(row, part), edge : edge + width],
+            sems.at[lanes[j % 2 if full else 2]],
+        )
+        store.start()
+        stores.append(store)
+        edge += width
+    for store in stores[max(wide - 2, 0) :]:
+        store.wait()
+
+
 class Reduce:
     def __init__(self, lhs, rhs, bufs, abuf, fbuf, ftail, a_all, r_all, c_all, outs, late, sems):
         self.late = late
@@ -783,16 +806,22 @@
             fetches.append(fetch)
         for fetch in fetches:
             fetch.wait()
-        first = pl.multiple_of(self.half + self.chip * self.r, 16)
-        for _, at in self.columns():
-            total = self.bufs[m][pl.ds(first, self.r), at].astype(f32)
-            for k in range(len(self.near)):
-                total = total + self.bufs[m][k * self.r : (k + 1) * self.r, at].astype(f32)
-            stage = self.fbuf if total.shape[1] == FF_CHUNK else self.ftail
-            stage[...] = total
-            store = pltpu.make_async_copy(stage, self.outs[m].at[:, at], self.local.at[0])
-            store.start()
-            store.wait()
+        part = self.r // 2
+        for h in range(2):
+            first = pl.multiple_of(self.half + self.chip * self.r + h * part, 16)
+            totals = []
+            for _, at in self.columns():
+
+                def make(at=at, first=first, h=h):
+                    total = self.bufs[m][pl.ds(first, part), at].astype(f32)
+                    for k in range(len(self.near)):
+                        start = k * self.r + h * part
+                        total = total + self.bufs[m][start : start + part, at].astype(f32)
+                    return total
+
+                totals.append(make)
+            lanes = (0, 1, max(len(self.near), 2) + 1)
+            put_rows(totals, self.outs[m], h * part, self.fbuf, self.ftail, self.local, lanes)
 
     def drain(self, m):
         if self.four:
@@ -817,12 +846,13 @@
         dma((count, 2)),
         dma((count, near)),
         dma((count, near)),
-        dma((max(near, 2) + 1,)),
+        dma((max(near, 2) + 2,)),
     ]
 
 
 class Tail:
-    def __init__(self, b_all, r_all, c_all, outs, abuf, fbuf, ftail, sems):
+    def __init__(self, b_all, r_all, c_all, outs, abuf, fbuf, ftail, sems, direct=False):
+        self.direct = direct
         self.b_all, self.r_all, self.c_all, self.outs = b_all, r_all, c_all, outs
         self.abuf, self.fbuf, self.ftail = abuf, fbuf, ftail
         self.r_send, self.r_recv, self.c_send, self.c_recv, self.local = sems
@@ -922,20 +952,23 @@
                 fetch.start()
             for fetch in fetches:
                 fetch.wait()
+            totals = []
             for start, width in spans(self.abuf.shape[1]):
                 at = slice(start, start + width)
-                total = self.slot(i, 0)[:, at].astype(f32)
-                for k in range(1, count + 1):
-                    total = total + self.slot(i, k)[:, at].astype(f32)
-                stage = self.fbuf if width == FF_CHUNK else self.ftail
-                stage[: self.part] = total
-                store = pltpu.make_async_copy(
-                    stage.at[pl.ds(0, self.part)],
-                    self.outs[i].at[pl.ds(h * self.part, self.part), at],
-                    self.local.at[0],
-                )
-                store.start()
-                store.wait()
+
+                def make(at=at):
+                    total = self.slot(i, 0)[:, at].astype(f32)
+                    for k in range(1, count + 1):
+                        total = total + self.slot(i, k)[:, at].astype(f32)
+                    return total
+
+                if self.direct:
+                    self.outs[i][h * self.part : (h + 1) * self.part, at] = make()
+                else:
+                    totals.append(make)
+            put_rows(
+                totals, self.outs[i], h * self.part, self.fbuf, self.ftail, self.local, (0, 1, 2)
+            )
 
 
 def tail_scratch(count):
@@ -1512,8 +1545,8 @@
     acts, q, k, v, lse, cosine, sine, qkv_ref, out_ref = refs[8:17]
     grad_out, grad_low, acts_turned, branch_turned, gqkv, small = refs[17:23]
     qkv, wout, heads, branch, dq, dk_sum, dv_sum, kv_out, kv_in, total = refs[23:33]
-    w_sem, kv_send, kv_recv, abuf, fbuf, ftail = refs[33:39]
-    tail = Tail(held, r_all, c_all, [late_grad], abuf, fbuf, ftail, refs[39:])
+    w_sem, kv_send, kv_recv, abuf = refs[33:37]
+    tail = Tail(held, r_all, c_all, [late_grad], abuf, None, None, refs[37:], True)
     gx, me, size = lax.axis_index("gx"), lax.axis_index("gy"), lax.axis_size("gy")
     count, rows = q.shape[0], k.shape[0]
     loads = [
@@ -1658,7 +1691,7 @@
             jax.ShapeDtypeStruct((1, near, 2, r // 2, wide), bf16),
         ],
         in_specs=[local] * 15 + [ANY] * 3,
-        out_specs=[local] * 6 + [ANY] * 3,
+        out_specs=[local] * 7 + [ANY] * 2,
         scratch_shapes=[
             vmem(qkv.shape, bf16),
             vmem(wout.shape, bf16),
@@ -1674,8 +1707,6 @@
             dma((KV_HEADS, size)),
             dma((KV_HEADS, size)),
             vmem((width // 4, wide), bf16),
-            vmem((r, FF_CHUNK), f32),
-            vmem((r, wide % FF_CHUNK), f32),
         ]
         + tail_scratch(1),
         compiler_params=pltpu.CompilerParams(

time: 1120 us -> 1100 us (0.982)
  Pallas kernels: 1050 us -> 1030 us
    pallas_call x2, Pallas kernels: 134 us -> 121 us  [attention_pull(): pl.pallas_call(attention_pull_kernel, out_shape=[jax.ShapeDtypeStruct((co...]
where the time goes in v9:
time: 1100 us; the launch traced here: 1090 us
  Pallas kernels  1030 us (94%)
  local copies, waits for them, and re-layouts  31.7 us (3%)
  other arithmetic  23 us (2%)
    pallas_call x2, Pallas kernels, backward_ffn(): pl.pallas_call(functools.partial(backward_kernel, late, tails), out_shape...  293 us
    pallas_call x2, Pallas kernels, forward_ffn(): pl.pallas_call(functools.partial(forward_kernel, extra), out_shape=[jax.S...  228 us
    pallas_call x1, Pallas kernels, closing(): pl.pallas_call(functools.partial(closing_kernel, layers), out_shape=[jax....  142 us
    pallas_call x1, Pallas kernels, opening(): pl.pallas_call(opening_kernel, out_shape=out, in_specs=[ANY] * 9, out_spe...  135 us
    pallas_call x2, Pallas kernels, attention_pull(): pl.pallas_call(attention_pull_kernel, out_shape=[jax.ShapeDtypeStruct((co...  121 us
    pallas_call x2, Pallas kernels, attention_push(): pl.pallas_call(functools.partial(attention_push_kernel, layer), out_shape...  112 us

profile of v9, /device:TPU:9, one launch (start us, length us, event | category | flops | bytes accessed | tf_op | source)
XLA Modules:
  0.0 1086.5 jit_solution(3110210868114529633)
XLA Ops:
  4.2 1.0 slice_bitcast_fusion.1
  8.2 134.6 %opening.1 = (bf16[4,384,256]{2,1,0:T(8,128)(2,1)}, bf16[4,384,256]{2,1,0:T(8,128)(2,1)}, f32[4,8,1280]{2,1,0:T(8,128)}, bf16[4,192,512]{2,1,0:T(8,128)(2,1)}, b...) custom-call(bf16[384,1024]{1,0:T(8,128)(2,1)} %refs_0_.1, ...), custom_call_target="tpu_custom_call" | custom-call | tf_op jit(solution)/shard_map/opening/pallas_call | solution.py:332
  142.8 0.9 slice_bitcast_fusion.4
  147.0 1.2 bitcast_convert_fusion.1
  148.7 1.2 bitcast_convert_fusion
  150.0 1.6 copy.53
  151.6 47.3 %attention_push.2 = (f32[256,1536]{1,0:T(8,128)}, f32[256,1536]{1,0:T(8,128)}, f32[256,1]{1,0:T(8,128)}, bf16[256,1536]{1,0:T(8,128)(2,1)}, bf16[256,1536]{1,0:T...) custom-call(f32[256,1536]{1,0:T(8,128)} %bitcast.65, ...), custom_call_target="tpu_custom_call" | custom-call | tf_op jit(solution)/shard_map/attention_push/pallas_call | solution.py:1863
  198.9 121.4 %ffn_forward.2 = (f32[256,1536]{1,0:T(8,128)}, bf16[2,768,1024]{2,1,0:T(8,128)(2,1)}, bf16[4,256,2240]{2,1,0:T(8,128)(2,1)}, bf16[4,256,2240]{2,1,0:T(8,128)(2,1...) custom-call(bf16[256,1536]{1,0:T(8,128)(2,1)} %get-tuple-element.95., ...), custom_call_target="tpu_custom_call" | custom-call | flops 21139292160 | bytes 41943040 | tf_op jit(solution)/shard_map/ffn_forward/pallas_call | solution.py:627
  320.3 3.2 add.36.refs_0_
  323.5 64.9 %attention_push.3 = (f32[256,1536]{1,0:T(8,128)}, f32[256,1536]{1,0:T(8,128)}, f32[256,1]{1,0:T(8,128)}, bf16[256,1536]{1,0:T(8,128)(2,1)}, bf16[256,1536]{1,0:T...) custom-call(f32[256,1536]{1,0:T(8,128)} %add.36.refs_0_, ...), custom_call_target="tpu_custom_call" | custom-call | tf_op jit(solution)/shard_map/attention_push/pallas_call | solution.py:1863
  388.5 106.6 %ffn_forward.3 = (f32[256,1536]{1,0:T(8,128)}, bf16[2,768,1024]{2,1,0:T(8,128)(2,1)}, bf16[4,256,2240]{2,1,0:T(8,128)(2,1)}, bf16[4,256,2240]{2,1,0:T(8,128)(2,1)}, bf16[4,256,2240]{2,1,0:T(8,128)(2,1)}) custom-call(bf16[256,1536]{1,0:T(8,128)(2,1)} %get-tuple-element.105.refs_0_, bf16[1536,2240]{1,0:T(8,128)(2,1)} %bitcast.99, ...), custom_call_target="tpu_custom_call" | custom-call | flops 21139292160 | bytes 41943040 | tf_op jit(solution)/shard_map/ffn_forward/pallas_call | solution.py:627
  495.0 4.1 fusion.3
  499.1 139.2 %ffn_backward.2 = (f32[256,1536]{1,0:T(8,128)}, f32[192,2240]{1,0:T(8,128)}, bf16[1,768,2240]{2,1,0:T(8,128)(2,1)}, bf16[1,768,2240]{2,1,0:T(8,128)(2,1)}, bf16[...) custom-call(bf16[256,1536]{1,0:T(8,128)(2,1)} %get-tuple-element.206.refs_0_, ...), custom_call_target="tpu_custom_call" | custom-call | flops 42278584320 | bytes 41943040 | tf_op jit(solution)/shard_map/ffn_backward/pallas_call | solution.py:1173
  638.4 64.3 %attention_pull.2 = (f32[256,1536]{1,0:T(8,128)}, bf16[256,1536]{1,0:T(8,128)(2,1)}, bf16[2,768,256]{2,1,0:T(8,128)(2,1)}, bf16[2,768,256]{2,1,0:T(8,128)(2,1)},...) custom-call(f32[256,1536]{1,0:T(8,128)} %get-tuple-element.207.refs_, ...), custom_call_target="tpu_custom_call" | custom-call | tf_op jit(solution)/shard_map/attention_pull/pallas_call | solution.py:1680
  702.7 153.7 %ffn_backward.3 = (f32[256,1536]{1,0:T(8,128)}, f32[192,2240]{1,0:T(8,128)}, f32[192,2240]{1,0:T(8,128)}, bf16[1,768,2240]{2,1,0:T(8,128)(2,1)}, bf16[3,768,2240...) custom-call(bf16[256,1536]{1,0:T(8,128)(2,1)} %get-tuple-element.126, ...), custom_call_target="tpu_custom_call" | custom-call | flops 42278584320 | bytes 41943040 | tf_op jit(solution)/shard_map/ffn_backward/pallas_call | solution.py:1173
  856.4 57.1 %attention_pull.3 = (f32[256,1536]{1,0:T(8,128)}, bf16[256,1536]{1,0:T(8,128)(2,1)}, bf16[2,768,256]{2,1,0:T(8,128)(2,1)}, bf16[2,768,256]{2,1,0:T(8,128)(2,1)},...) custom-call(f32[256,1536]{1,0:T(8,128)} %get-tuple-element.125.refs_, ...), custom_call_target="tpu_custom_call" | custom-call | tf_op jit(solution)/shard_map/attention_pull/pallas_call | solution.py:1680
  914.3 1.0 slice_reduce_fusion.3
  916.3 1.0 slice_reduce_fusion
  918.4 2.3 copy.45
  920.7 1.2 copy.44
  921.8 141.5 %closing.1 = (f32[2,192,896]{2,1,0:T(8,128)}, f32[8,1280]{1,0:T(8,128)}, bf16[4,384,256]{2,1,0:T(8,128)(2,1)}, bf16[4,384,256]{2,1,0:T(8,128)(2,1)}) custom-call(bf16[2,768,256]{2,1,0:T(8,128)(2,1)} %get-tuple-element.143.refs_0_, bf16[2,768,256]{2,1,0:T(8,128)(2,1)} %get-tuple-element.144.refs_1_, bf16[4,256,512]{2,1,0:T(8,128)(2,1)} %get-tuple-element.145.refs_2_, ...), custom_call_target="tpu_custom_call" | custom-call | tf_op jit(solution)/shard_map/closing/pallas_call | solution.py:1469
  1063.4 1.4 fusion.10
  1064.8 1.3 fusion.9
  1066.1 1.2 fusion.6
  1067.3 2.3 fusion.5
  1071.8 1.6 copy.48
  1073.4 1.3 convert_bitcast_fusion
  1075.2 1.6 copy.49
  1076.8 4.2 pad_maximum_fusion.1
  1081.0 2.0 pad_maximum_fusion
  1083.1 1.1 copy-done.3
  1084.2 2.0 pad_maximum_fusion.2
  (56 shorter events, 15.9 us)
Async XLA Ops:
  0.6 5.4 copy-start.6
  913.5 7.2 copy-start
  1066.1 5.1 copy-start.5
  1076.8 4.2 copy-start.2
  1076.8 4.2 copy-start.4
  1081.0 2.2 copy-start.1
  1081.0 3.3 copy-start.3

commit v10 on v9

--- a/solution.py
+++ b/solution.py
@@ -1435,8 +1435,6 @@
     total.begin()
     for m in range(layers):
         fold.first(m)
-    for swap in swaps:
-        swap.begin()
     fold.second(0)
     total.middle()
     for m in range(1, layers):
@@ -1444,6 +1442,9 @@
     total.later()
     for m in range(layers):
         fold.third(m)
+        if m == 0:
+            for swap in swaps:
+                swap.begin()
     for m in range(layers):
         fold.fourth(m)
     total.close(small_out)

time: 1100 us -> 1100 us (level)
  no operation moved by 1% of the time
where the time goes in v10:
time: 1100 us; the launch traced here: 1090 us
  Pallas kernels  1030 us (94%)
  local copies, waits for them, and re-layouts  31.7 us (3%)
  other arithmetic  23 us (2%)
    pallas_call x2, Pallas kernels, backward_ffn(): pl.pallas_call(functools.partial(backward_kernel, late, tails), out_shape...  293 us
    pallas_call x2, Pallas kernels, forward_ffn(): pl.pallas_call(functools.partial(forward_kernel, extra), out_shape=[jax.S...  228 us
    pallas_call x1, Pallas kernels, closing(): pl.pallas_call(functools.partial(closing_kernel, layers), out_shape=[jax....  142 us
    pallas_call x1, Pallas kernels, opening(): pl.pallas_call(opening_kernel, out_shape=out, in_specs=[ANY] * 9, out_spe...  135 us
    pallas_call x2, Pallas kernels, attention_pull(): pl.pallas_call(attention_pull_kernel, out_shape=[jax.ShapeDtypeStruct((co...  121 us
    pallas_call x2, Pallas kernels, attention_push(): pl.pallas_call(functools.partial(attention_push_kernel, layer), out_shape...  112 us

profile of v10, /device:TPU:9, one launch (start us, length us, event | category | flops | bytes accessed | tf_op | source)
XLA Modules:
  0.0 1086.5 jit_solution(17876839474806897426)
XLA Ops:
  4.2 1.0 slice_bitcast_fusion.1
  8.2 134.6 %opening.1 = (bf16[4,384,256]{2,1,0:T(8,128)(2,1)}, bf16[4,384,256]{2,1,0:T(8,128)(2,1)}, f32[4,8,1280]{2,1,0:T(8,128)}, bf16[4,192,512]{2,1,0:T(8,128)(2,1)}, b...) custom-call(bf16[384,1024]{1,0:T(8,128)(2,1)} %refs_0_.1, ...), custom_call_target="tpu_custom_call" | custom-call | tf_op jit(solution)/shard_map/opening/pallas_call | solution.py:332
  142.8 0.9 slice_bitcast_fusion.4
  147.0 1.2 bitcast_convert_fusion.1
  148.7 1.2 bitcast_convert_fusion
  150.0 1.6 copy.53
  151.6 47.3 %attention_push.2 = (f32[256,1536]{1,0:T(8,128)}, f32[256,1536]{1,0:T(8,128)}, f32[256,1]{1,0:T(8,128)}, bf16[256,1536]{1,0:T(8,128)(2,1)}, bf16[256,1536]{1,0:T...) custom-call(f32[256,1536]{1,0:T(8,128)} %bitcast.65, ...), custom_call_target="tpu_custom_call" | custom-call | tf_op jit(solution)/shard_map/attention_push/pallas_call | solution.py:1864
  198.9 121.4 %ffn_forward.2 = (f32[256,1536]{1,0:T(8,128)}, bf16[2,768,1024]{2,1,0:T(8,128)(2,1)}, bf16[4,256,2240]{2,1,0:T(8,128)(2,1)}, bf16[4,256,2240]{2,1,0:T(8,128)(2,1...) custom-call(bf16[256,1536]{1,0:T(8,128)(2,1)} %get-tuple-element.95., ...), custom_call_target="tpu_custom_call" | custom-call | flops 21139292160 | bytes 41943040 | tf_op jit(solution)/shard_map/ffn_forward/pallas_call | solution.py:627
  320.3 3.2 add.36.refs_0_
  323.5 64.9 %attention_push.3 = (f32[256,1536]{1,0:T(8,128)}, f32[256,1536]{1,0:T(8,128)}, f32[256,1]{1,0:T(8,128)}, bf16[256,1536]{1,0:T(8,128)(2,1)}, bf16[256,1536]{1,0:T...) custom-call(f32[256,1536]{1,0:T(8,128)} %add.36.refs_0_, ...), custom_call_target="tpu_custom_call" | custom-call | tf_op jit(solution)/shard_map/attention_push/pallas_call | solution.py:1864
  388.5 106.6 %ffn_forward.3 = (f32[256,1536]{1,0:T(8,128)}, bf16[2,768,1024]{2,1,0:T(8,128)(2,1)}, bf16[4,256,2240]{2,1,0:T(8,128)(2,1)}, bf16[4,256,2240]{2,1,0:T(8,128)(2,1)}, bf16[4,256,2240]{2,1,0:T(8,128)(2,1)}) custom-call(bf16[256,1536]{1,0:T(8,128)(2,1)} %get-tuple-element.105.refs_0_, bf16[1536,2240]{1,0:T(8,128)(2,1)} %bitcast.99, ...), custom_call_target="tpu_custom_call" | custom-call | flops 21139292160 | bytes 41943040 | tf_op jit(solution)/shard_map/ffn_forward/pallas_call | solution.py:627
  495.0 4.1 fusion.3
  499.1 139.2 %ffn_backward.2 = (f32[256,1536]{1,0:T(8,128)}, f32[192,2240]{1,0:T(8,128)}, bf16[1,768,2240]{2,1,0:T(8,128)(2,1)}, bf16[1,768,2240]{2,1,0:T(8,128)(2,1)}, bf16[...) custom-call(bf16[256,1536]{1,0:T(8,128)(2,1)} %get-tuple-element.206.refs_0_, ...), custom_call_target="tpu_custom_call" | custom-call | flops 42278584320 | bytes 41943040 | tf_op jit(solution)/shard_map/ffn_backward/pallas_call | solution.py:1173
  638.4 64.3 %attention_pull.2 = (f32[256,1536]{1,0:T(8,128)}, bf16[256,1536]{1,0:T(8,128)(2,1)}, bf16[2,768,256]{2,1,0:T(8,128)(2,1)}, bf16[2,768,256]{2,1,0:T(8,128)(2,1)},...) custom-call(f32[256,1536]{1,0:T(8,128)} %get-tuple-element.207.refs_, ...), custom_call_target="tpu_custom_call" | custom-call | tf_op jit(solution)/shard_map/attention_pull/pallas_call | solution.py:1681
  702.7 153.7 %ffn_backward.3 = (f32[256,1536]{1,0:T(8,128)}, f32[192,2240]{1,0:T(8,128)}, f32[192,2240]{1,0:T(8,128)}, bf16[1,768,2240]{2,1,0:T(8,128)(2,1)}, bf16[3,768,2240...) custom-call(bf16[256,1536]{1,0:T(8,128)(2,1)} %get-tuple-element.126, ...), custom_call_target="tpu_custom_call" | custom-call | flops 42278584320 | bytes 41943040 | tf_op jit(solution)/shard_map/ffn_backward/pallas_call | solution.py:1173
  856.4 57.1 %attention_pull.3 = (f32[256,1536]{1,0:T(8,128)}, bf16[256,1536]{1,0:T(8,128)(2,1)}, bf16[2,768,256]{2,1,0:T(8,128)(2,1)}, bf16[2,768,256]{2,1,0:T(8,128)(2,1)},...) custom-call(f32[256,1536]{1,0:T(8,128)} %get-tuple-element.125.refs_, ...), custom_call_target="tpu_custom_call" | custom-call | tf_op jit(solution)/shard_map/attention_pull/pallas_call | solution.py:1681
  914.3 1.0 slice_reduce_fusion.3
  916.3 1.0 slice_reduce_fusion
  918.4 2.3 copy.45
  920.7 1.2 copy.44
  921.8 141.5 %closing.1 = (f32[2,192,896]{2,1,0:T(8,128)}, f32[8,1280]{1,0:T(8,128)}, bf16[4,384,256]{2,1,0:T(8,128)(2,1)}, bf16[4,384,256]{2,1,0:T(8,128)(2,1)}) custom-call(bf16[2,768,256]{2,1,0:T(8,128)(2,1)} %get-tuple-element.143.refs_0_, bf16[2,768,256]{2,1,0:T(8,128)(2,1)} %get-tuple-element.144.refs_1_, bf16[4,256,512]{2,1,0:T(8,128)(2,1)} %get-tuple-element.145.refs_2_, ...), custom_call_target="tpu_custom_call" | custom-call | tf_op jit(solution)/shard_map/closing/pallas_call | solution.py:1470
  1063.4 1.4 fusion.10
  1064.8 1.3 fusion.9
  1066.1 1.2 fusion.6
  1067.3 2.3 fusion.5
  1071.8 1.6 copy.48
  1073.4 1.3 convert_bitcast_fusion
  1075.2 1.6 copy.49
  1076.8 4.2 pad_maximum_fusion.1
  1081.0 2.0 pad_maximum_fusion
  1083.1 1.1 copy-done.3
  1084.2 2.0 pad_maximum_fusion.2
  (56 shorter events, 15.9 us)
Async XLA Ops:
  0.6 5.4 copy-start.6
  913.5 7.2 copy-start
  1066.1 5.1 copy-start.5
  1076.8 4.2 copy-start.2
  1076.8 4.2 copy-start.4
  1081.0 2.2 copy-start.1
  1081.0 3.3 copy-start.3
